TPU v7x, 32 devices: a whole 2x2x4 slice. The times are simulated.
32 devices in a mesh: gx: 8 (over z, y), gy: 4 (over x, core).
Axes of the slice: x: 2, y: 2, z: 4, core: 2. Of those that a mesh axis runs over, the one named last changes fastest.
Arguments:
- populations: float32 [19, 16, 32, 1024], P(None, None, 'gx', 'gy'), may hold values from -6 to 6
- fraction: float32 [16, 3, 4096], P('gx', None, 'gy'), may hold values from 0 to 1
- spans: int32 [16, 32, 1], P('gx'), may hold values from 0 to 3; in each aligned block of 64 rows (0 to 63, 64 to 127, ..., all dimensions but the last counted through in order) at most 32 rows name the same one
- stiffness: int32 [16], P('gx'), may hold values from 1 to 8
Outputs:
- populations_out: float32 [19, 16, 32, 1024], P(None, None, 'gx', 'gy')
- marker_vel: float32 [16, 3, 4096], P('gx', None, 'gy')
Inputs may be any that keep to these rules, and one draw needn't show every extreme that they name: `spans`: among the 64 blocks of the filaments of one gx index, no tile is named by more than 32 blocks, and one is named by exactly 32.
All inputs are finite; a program needn't handle non-finite values.
Results may differ from a plain program's by a relative error of at most 0.0003.
Values sent between devices are 32-bit elements; how exact they have to be, the bound alone decides.
No kernel may reach another device: no remote copies, remote signals or barrier semaphores. Data moves between devices by JAX's collectives and lax.ppermute only.
A program may use at most 64 MiB of HBM per device.

v0:
```python
import math

import jax
import jax.numpy as jnp
from jax import lax
from jax.sharding import PartitionSpec as P

STEPS = 2


velocity_set = (
    (0, 0, 0),
    (1, 0, 0),
    (-1, 0, 0),
    (0, 1, 0),
    (0, -1, 0),
    (0, 0, 1),
    (0, 0, -1),
    (1, 1, 0),
    (-1, -1, 0),
    (1, -1, 0),
    (-1, 1, 0),
    (1, 0, 1),
    (-1, 0, -1),
    (1, 0, -1),
    (-1, 0, 1),
    (0, 1, 1),
    (0, -1, -1),
    (0, 1, -1),
    (0, -1, 1),
)
lattice_weight = (1.0 / 3.0,) + (1.0 / 18.0,) * 6 + (1.0 / 36.0,) * 12
relax_time = 0.8
deviation_unit = 0.002
feedback_gain = 2.0
stiff_unit = 0.002


def extended_2(cells, sides, width):
    for axis, dim in sides:
        count = lax.axis_size(axis)
        head = lax.slice_in_dim(cells, 0, width, axis=dim)
        tail = lax.slice_in_dim(cells, cells.shape[dim] - width, cells.shape[dim], axis=dim)
        cells = jnp.concatenate(
            [
                lax.ppermute(tail, axis, [(i, (i + 1) % count) for i in range(count)]),
                cells,
                lax.ppermute(head, axis, [((i + 1) % count, i) for i in range(count)]),
            ],
            axis=dim,
        )
    return cells


def opposite(entry):
    return entry + 1 if entry % 2 == 1 else entry - 1


def kernel_weight(distance):
    return jnp.where(jnp.abs(distance) < 2.0, 0.25 * (1.0 + jnp.cos(0.5 * math.pi * distance)), 0.0)


def periodic_gap(gap, period):
    half = 0.5 * period
    return jnp.where(gap > half, gap - period, jnp.where(gap < -half, gap + period, gap))


def marker_places(fraction, spans, row_anchor, tile_x, tile_y, depth):
    block_size = fraction.shape[2] // spans.shape[1]
    span_cells = jnp.repeat(spans[:, :, 0] * tile_y, block_size, axis=1).astype(jnp.float32)
    xpos = row_anchor[:, None] + 1.0 + fraction[:, 0] * (tile_x - 3.01)
    ypos = span_cells + fraction[:, 1] * tile_y
    zpos = 1.0 + fraction[:, 2] * (depth - 3.01)
    return jnp.stack([xpos, ypos, zpos], axis=1)


def elastic(places, period):
    ahead = places[:, :, 1:] - places[:, :, :-1]
    ahead = jnp.stack([ahead[:, 0], periodic_gap(ahead[:, 1], period), ahead[:, 2]], axis=1)
    edge = jnp.zeros(ahead.shape[:2] + (1,), jnp.float32)
    return jnp.concatenate([ahead, edge], 2) - jnp.concatenate([edge, ahead], 2)


def project(vector, parts, like):
    total = jnp.zeros_like(like)
    for axis_dim in range(3):
        if vector[axis_dim] != 0:
            total = total + float(vector[axis_dim]) * parts[axis_dim]
    return total


def moments(deviation):
    fpop = [lattice_weight[entry] + deviation_unit * deviation[entry] for entry in range(19)]
    dens = fpop[0]
    for entry in range(1, 19):
        dens = dens + fpop[entry]
    momentum = []
    for axis_dim in range(3):
        total = jnp.zeros_like(dens)
        for entry in range(19):
            if velocity_set[entry][axis_dim] != 0:
                total = total + float(velocity_set[entry][axis_dim]) * fpop[entry]
        momentum.append(total)
    return (fpop, dens, momentum)


def relax(fpop, dens, momentum, force):
    velocity = [(momentum[axis_dim] + 0.5 * force[axis_dim]) / dens for axis_dim in range(3)]
    speed_sq = velocity[0] * velocity[0] + velocity[1] * velocity[1] + velocity[2] * velocity[2]
    factor = 1.0 - 0.5 / relax_time
    drift_base = -(velocity[0] * force[0] + velocity[1] * force[1] + velocity[2] * force[2])
    post = []
    for entry in range(19):
        vector = velocity_set[entry]
        along = project(vector, velocity, dens)
        push = project(vector, force, dens)
        drift = push + drift_base
        equil = (
            lattice_weight[entry]
            * dens
            * (1.0 + 3.0 * along + 4.5 * along * along - 1.5 * speed_sq)
        )
        source = factor * lattice_weight[entry] * (3.0 * drift + 9.0 * along * push)
        post.append(fpop[entry] - (fpop[entry] - equil) / relax_time + source)
    return post


def bounce(moved, post):
    result = []
    for entry in range(19):
        lift = velocity_set[entry][2]
        plane = moved[entry]
        if lift == 1:
            plane = jnp.concatenate([post[opposite(entry)][:1], plane[:-1]], 0)
        elif lift == -1:
            plane = jnp.concatenate([plane[1:], post[opposite(entry)][-1:]], 0)
        result.append((plane - lattice_weight[entry]) / deviation_unit)
    return jnp.stack(result)


def stream_tile(post, tile_x, tile_y):
    extended = extended_2(jnp.stack(post), (("gx", 2), ("gy", 3)), 1)
    moved = []
    for entry in range(19):
        shift_x, shift_y = (velocity_set[entry][0], velocity_set[entry][1])
        moved.append(
            extended[
                entry, :, 1 - shift_x : 1 - shift_x + tile_x, 1 - shift_y : 1 - shift_y + tile_y
            ]
        )
    return bounce(moved, post)


def per_device(populations, fraction, spans, stiffness):
    depth, tile_x, tile_y = (populations.shape[1], populations.shape[2], populations.shape[3])
    column_count = lax.axis_size("gy")
    span_y = tile_y * column_count
    my_row = lax.axis_index("gx")
    my_column = lax.axis_index("gy")
    share = fraction.shape[2]
    row_fraction = lax.all_gather(fraction, "gy", axis=2, tiled=True)
    filaments, markers = (row_fraction.shape[0], row_fraction.shape[2])
    row_anchor = jnp.broadcast_to((my_row * tile_x).astype(jnp.float32), (filaments,))
    places = marker_places(row_fraction, spans, row_anchor, tile_x, tile_y, depth)
    bend = (
        elastic(places, span_y)
        * (stiffness.astype(jnp.float32) * (stiff_unit / tile_y))[:, None, None]
    )
    block_count = spans.shape[1]
    block_size = markers // block_count
    block_total = filaments * block_count
    slot_cap = max(2, 2 * block_total // column_count)
    flat_spans = spans[:, :, 0].reshape(-1)
    order = jnp.arange(block_total, dtype=jnp.int32)
    chosen_list = []
    valid_list = []
    for offset in (-1, 0, 1):
        target = jnp.mod(my_column + offset, column_count)
        ranking = jnp.where(flat_spans == target, 2 * block_total - order, -order)
        _, picked = lax.top_k(ranking, slot_cap)
        chosen_list.append(picked)
        valid_list.append(flat_spans[picked] == target)
    chosen = jnp.concatenate(chosen_list)
    valid = jnp.concatenate(valid_list)
    slot_total = chosen.shape[0]
    blocks = (
        places.reshape(filaments, 3, block_count, block_size)
        .transpose(0, 2, 1, 3)
        .reshape(block_total, 3, block_size)
    )
    slot_places = blocks[chosen]
    flat_x = slot_places[:, 0].reshape(-1)
    flat_y = slot_places[:, 1].reshape(-1)
    flat_z = slot_places[:, 2].reshape(-1)
    live = jnp.repeat(valid, block_size).astype(jnp.float32)
    x_cells = (my_row * tile_x + jnp.arange(tile_x, dtype=jnp.int32)).astype(jnp.float32)
    y_index = my_column * tile_y + jnp.arange(tile_y, dtype=jnp.int32)
    y_cells = y_index.astype(jnp.float32)
    y_lower = (y_index - span_y).astype(jnp.float32)
    y_upper = (y_index + span_y).astype(jnp.float32)
    z_cells = jnp.arange(depth, dtype=jnp.int32).astype(jnp.float32)
    weight_x = kernel_weight(flat_x[None, :] - x_cells[:, None])
    weight_z = kernel_weight(flat_z[None, :] - z_cells[:, None])
    gap_mid = flat_y[:, None] - y_cells[None, :]
    gap_y = jnp.where(
        gap_mid > 0.5 * span_y,
        flat_y[:, None] - y_upper[None, :],
        jnp.where(gap_mid < -0.5 * span_y, flat_y[:, None] - y_lower[None, :], gap_mid),
    )
    weight_y = kernel_weight(gap_y) * live[:, None]
    plane_weight = weight_z[:, None, :] * weight_x[None, :, :]
    selector = (chosen[:, None] == order[None, :]).astype(jnp.float32)
    highest = lax.Precision.HIGHEST
    deviation = populations
    own_speed = jnp.zeros((filaments, 3, share), jnp.float32)
    for step in range(STEPS):
        fpop, dens, momentum = moments(deviation)
        flow = jnp.stack([part / dens for part in momentum])
        across = jnp.dot(flow.reshape(3 * depth * tile_x, tile_y), weight_y.T, precision=highest)
        slot_speed = jnp.sum(across.reshape(3, depth, tile_x, -1) * plane_weight[None], axis=(1, 2))
        slot_rows = (
            slot_speed.reshape(3, slot_total, block_size)
            .transpose(1, 0, 2)
            .reshape(slot_total, 3 * block_size)
        )
        row_speed = jnp.dot(selector.T, slot_rows, precision=highest)
        partial_speed = (
            row_speed.reshape(filaments, block_count, 3, block_size)
            .transpose(0, 2, 1, 3)
            .reshape(filaments, 3, markers)
        )
        row_speed = lax.psum(partial_speed, "gy")
        own_speed = lax.dynamic_slice_in_dim(row_speed, my_column * share, share, 2)
        force_row = bend - feedback_gain * row_speed
        force_blocks = (
            force_row.reshape(filaments, 3, block_count, block_size)
            .transpose(0, 2, 1, 3)
            .reshape(block_total, 3, block_size)
        )
        slot_force = force_blocks[chosen].transpose(1, 0, 2).reshape(3, -1)
        weighted = (slot_force[:, None, None, :] * plane_weight[None]).reshape(
            3 * depth * tile_x, -1
        )
        field_force = jnp.dot(weighted, weight_y, precision=highest).reshape(
            3, depth, tile_x, tile_y
        )
        post = relax(fpop, dens, momentum, [field_force[axis_dim] for axis_dim in range(3)])
        deviation = stream_tile(post, tile_x, tile_y)
    return (deviation, own_speed / deviation_unit)


def solution(mesh):
    placed = (P(None, None, "gx", "gy"), P("gx", None, "gy"), P("gx", None, None), P("gx"))
    return jax.shard_map(
        per_device,
        mesh=mesh,
        in_specs=placed,
        out_specs=(P(None, None, "gx", "gy"), P("gx", None, "gy")),
        check_vma=False,
    )
```

profile of v0, /device:TPU:0, one launch (start us, length us, event | category | flops | bytes accessed | tf_op | source)
XLA Modules:
  0.0 511.5 jit_solution(9764331265515568716)
XLA Ops:
  10.4 2.0 top_k.37
  12.5 2.0 top_k.27
  14.5 2.0 top_k.30
  20.2 6.3 %all_gather.3 = f32[2,3,4096]{2,0,1:T(2,128)S(1)} all-gather(f32[2,3,1024]{2,0,1:T(2,128)S(1)} %copy-done.116), channel_id=1, replica_groups=mesh['gx'=8,'gy'=4] {'gy'}, dimensions={2}, use_global_device_ids=true | all-gather | bytes 122880 | tf_op jit(solution)/shard_map/all_gather | solution.py:161
  32.3 2.7 fusion.15
  35.8 58.9 %fusion.5 = f32[3,12288]{1,0:T(4,128)S(1)} fusion(f32[16,4,12288]{2,0,1:T(8,128)S(1)} %broadcast_multiply_fusion.2, f32[12288]{0:T(1024)S(1)} %copy-done.111, f32[256]{0:T(256)S(1)} %copy-done.125, f32[256]{0:T(256)S(1)} %copy-done.128, f32[256]{0:T(256)S(1)} %copy-done.132, f32[12288]{0:T(1024)S(1)} %bitcast.695, ...), kind=kOutput, calls=%fused_computation.19 | convolution fusion | flops 7296577536 | bytes 3591168 | tf_op jit(solution)/shard_map/dot_general | solution.py:219
  99.6 30.9 %all-reduce.5.cloned.1.call-done = f32[2,3,4096]{2,0,1:T(2,128)} async-done(((f32[2,3,4096]{2,0,1:T(2,128)}), f32[2,3,4096]{2,0,1:T(2,128)}) %all-reduce.5.cloned.1.call-update) | async-done | bytes 98320 | tf_op jit(solution)/shard_map/psum | solution.py:232
  130.4 1.8 multiply_subtract_fusion.1
  133.8 1.6 copy.214
  135.5 2.3 gather_fusion.4
  137.8 5.7 %broadcast_multiply_fusion.1 = f32[3,16,4,12288]{3,1,2,0:T(8,128)} fusion(f32[3,12288]{1,0:T(4,128)} %bitcast.657, f32[16,4,12288]{2,0,1:T(8,128)S(1)} %broadcast_multiply_fusion.2), kind=kLoop, calls=%fused_computation.18 | loop fusion | flops 2359296 | bytes 12730368 | tf_op jit(solution)/shard_map/mul | solution.py:241
  143.5 13.3 %copy.215 = f32[3,16,4,12288]{3,2,1,0:T(4,128)} copy(f32[3,16,4,12288]{3,1,2,0:T(8,128)} %broadcast_multiply_fusion.1) | data formatting | bytes 18874368 | tf_op jit(solution)/shard_map/mul | solution.py:241
  156.8 11.0 %mul.5346 = f32[192,12288]{1,0:T(8,128)} reshape(f32[3,16,4,12288]{3,2,1,0:T(4,128)} %copy.215) | data formatting | bytes 18874368 | tf_op jit(solution)/shard_map/mul | solution.py:241
  167.9 66.5 %fusion.4 = f32[192,256]{1,0:T(8,128)S(1)} fusion(f32[192,12288]{1,0:T(8,128)} %mul.5346, f32[12288]{0:T(1024)S(1)} %copy-done.112, f32[256]{0:T(256)S(1)} %copy-done.126, f32[256]{0:T(256)S(1)} %copy-done.129, f32[256]{0:T(256)S(1)} %copy-done.133, f32[12288]{0:T(1024)S(1)} %bitcast.696), kind=kOutput, calls=%fused_computation.16 | convolution fusion | flops 7291797504 | bytes 9735168 | tf_op jit(solution)/shard_map/dot_general | solution.py:244
  241.6 3.3 collective-permute-start.1
  251.2 2.7 collective-permute-done
  253.9 2.2 collective-permute-done.1
  257.5 1.9 copy.243
  261.3 2.4 collective-permute-done.2
  268.9 59.2 %fusion.8 = f32[3,12288]{1,0:T(4,128)S(1)} fusion(f32[16,4,12288]{2,0,1:T(8,128)S(1)} %copy-done.2, f32[12288]{0:T(1024)S(1)} %copy-done.113, f32[256]{0:T(256)S(1)} %copy-done.127, f32[256]{0:T(256)S(1)} %copy-done.130, f32[256]{0:T(256)S(1)} %copy-done.134, f32[12288]{0:T(1024)S(1)} %bitcast.697, f32[1,16,4,256]{3,1,2,0:T(8,128)S(1)} %get-tuple-element.60, ...), kind=kOutput, calls=%fused_computation.20 | convolution fusion | flops 7296577536 | bytes 3591168 | tf_op jit(solution)/shard_map/dot_general | solution.py:219
  329.2 31.3 %all-reduce.7.cloned.1.call-done = f32[2,3,4096]{2,0,1:T(2,128)} async-done(((f32[2,3,4096]{2,0,1:T(2,128)}), f32[2,3,4096]{2,0,1:T(2,128)}) %all-reduce.7.cloned.1.call-update) | async-done | bytes 98320 | tf_op jit(solution)/shard_map/psum | solution.py:232
  362.5 6.5 %broadcast_multiply_fusion = f32[3,16,4,12288]{3,1,2,0:T(8,128)} fusion(f32[3,12288]{1,0:T(4,128)S(1)} %bitcast.656, f32[16,4,12288]{2,0,1:T(8,128)} %copy-done.1), kind=kLoop, calls=%fused_computation.17 | loop fusion | flops 2359296 | bytes 12730368 | tf_op jit(solution)/shard_map/mul | solution.py:241
  369.0 13.4 %copy.279 = f32[3,16,4,12288]{3,2,1,0:T(4,128)} copy(f32[3,16,4,12288]{3,1,2,0:T(8,128)} %broadcast_multiply_fusion) | data formatting | bytes 18874368 | tf_op jit(solution)/shard_map/mul | solution.py:241
  382.4 10.7 %mul.5646 = f32[192,12288]{1,0:T(8,128)} reshape(f32[3,16,4,12288]{3,2,1,0:T(4,128)} %copy.279) | data formatting | bytes 18874368 | tf_op jit(solution)/shard_map/mul | solution.py:241
  393.2 66.5 %fusion.3 = f32[192,256]{1,0:T(8,128)S(1)} fusion(f32[192,12288]{1,0:T(8,128)} %mul.5646, f32[12288]{0:T(1024)S(1)} %copy-done.113, f32[256]{0:T(256)S(1)} %copy-done.127, f32[256]{0:T(256)S(1)} %copy-done.130, f32[256]{0:T(256)S(1)} %copy-done.134, f32[12288]{0:T(1024)S(1)} %bitcast.698), kind=kOutput, calls=%fused_computation.15 | convolution fusion | flops 7291797504 | bytes 9735168 | tf_op jit(solution)/shard_map/dot_general | solution.py:244
  464.4 4.3 collective-permute-start.5
  471.0 3.3 collective-permute-done.5
  474.3 4.9 collective-permute-done.4
  480.6 1.9 copy.309
  483.3 1.7 collective-permute-start.7
  487.7 1.9 copy.308
  501.3 3.2 copy.340
  (452 shorter events, 66.9 us)
Async XLA Ops:
  7.2 123.3 %all-reduce.5.cloned.1.call-start = ((), (), s32[]{:S(2)}) async-start(), calls=%async_computation | async-start | bytes 196608 | tf_op jit(solution)/shard_map/psum | solution.py:232
  7.3 87.4 %copy-start.120 = (s32[2,32]{1,0:T(2,128)}, s32[2,32]{1,0:T(2,128)S(1)}, u32[]{:S(2)}) copy-start(s32[2,32]{1,0:T(2,128)S(1)} %multiply_add_fusion.27) | copy-start | bytes 772
  17.1 118.3 %copy-start.117 = (s32[1024]{0:T(1024)}, s32[1024]{0:T(1024)S(1)}, u32[]{:S(2)}) copy-start(s32[1024]{0:T(1024)S(1)} %pad_clamp_fusion.3) | copy-start | bytes 12292
  35.3 102.5 %copy-start.1 = (f32[16,4,12288]{2,0,1:T(8,128)}, f32[16,4,12288]{2,0,1:T(8,128)S(1)}, u32[]{:S(2)}) copy-start(f32[16,4,12288]{2,0,1:T(8,128)S(1)} %broadcast_multiply_fusion.2) | copy-start | bytes 9437188
  97.2 263.2 %all-reduce.7.cloned.1.call-start = ((), (), s32[]{:S(2)}) async-start(), calls=%async_computation.1 | async-start | bytes 196608 | tf_op jit(solution)/shard_map/psum | solution.py:232
  167.8 66.8 %copy-start.22 = (f32[1,16,4,256]{3,2,1,0:T(4,128)S(1)}, f32[1,16,4,256]{3,2,1,0:T(4,128)}, u32[]{:S(2)}) copy-start(f32[1,16,4,256]{3,2,1,0:T(4,128)} %copy-done.21) | copy-start | bytes 196612
  167.8 66.8 %copy-start.24 = (f32[1,16,4,256]{3,2,1,0:T(4,128)S(1)}, f32[1,16,4,256]{3,2,1,0:T(4,128)}, u32[]{:S(2)}) copy-start(f32[1,16,4,256]{3,2,1,0:T(4,128)} %copy-done.23) | copy-start | bytes 196612
  167.8 66.8 %copy-start.26 = (f32[1,16,4,256]{3,2,1,0:T(4,128)S(1)}, f32[1,16,4,256]{3,2,1,0:T(4,128)}, u32[]{:S(2)}) copy-start(f32[1,16,4,256]{3,2,1,0:T(4,128)} %copy-done.25) | copy-start | bytes 196612
  240.1 13.8 %collective-permute-start = (f32[19,16,1,256]{3,1,2,0:T(8,128)S(1)}, f32[19,16,1,256]{3,1,2,0:T(8,128)S(1)}, u32[]{:S(2)}, u32[]{:S(2)}) collective-permute-start(f32[19,16,1,256]{3,1,2,0:T(8,128)S(1)} %get-tuple-element.112), channel_id=1, source_target_pairs={{0,4},{4,8},{8,12},{12,16},{16,20},{20,24},{24,28},{28,0},{1,5},{5... | collective-permute-start | bytes 933896 | tf_op jit(solution)/shard_map/ppermute | solution.py:46
  241.6 14.5 %collective-permute-start.1 = (f32[19,16,1,256]{3,1,2,0:T(8,128)S(1)}, f32[19,16,1,256]{3,1,2,0:T(8,128)S(1)}, u32[]{:S(2)}, u32[]{:S(2)}) collective-permute-start(f32[19,16,1,256]{3,1,2,0:T(8,128)S(1)} %get-tuple-element.113), channel_id=1, source_target_pairs={{4,0},{8,4},{12,8},{16,12},{20,16},{24,20},{28,24},{0,28},{5,1},{9... | collective-permute-start | bytes 933896 | tf_op jit(solution)/shard_map/ppermute | solution.py:48
  260.1 4.6 collective-permute-start.3
  260.1 3.6 collective-permute-start.2
  268.9 91.5 %copy-start.77 = (f32[2,3,4095]{2,0,1:T(2,128)S(1)}, f32[2,3,4095]{2,0,1:T(2,128)}, u32[]{:S(2)}) copy-start(f32[2,3,4095]{2,0,1:T(2,128)} %pad_maximum_fusion.4) | copy-start | bytes 294844
  268.9 91.5 %copy-start.123 = (f32[2]{0:T(128)S(1)}, f32[2]{0:T(128)}, u32[]{:S(2)}) copy-start(f32[2]{0:T(128)} %copy-done.122) | copy-start | bytes 28
  393.1 67.0 %copy-start.79 = (f32[16,4,256]{2,0,1:T(8,128)S(1)}, f32[16,4,256]{2,0,1:T(8,128)}, u32[]{:S(2)}) copy-start(f32[16,4,256]{2,0,1:T(8,128)} %copy-done.78) | copy-start | bytes 196612
  393.1 67.0 %copy-start.81 = (f32[16,4,256]{2,0,1:T(8,128)S(1)}, f32[16,4,256]{2,0,1:T(8,128)}, u32[]{:S(2)}) copy-start(f32[16,4,256]{2,0,1:T(8,128)} %copy-done.80) | copy-start | bytes 196612
  393.1 67.0 %copy-start.84 = (f32[15,4,256]{2,0,1:T(8,128)S(1)}, f32[15,4,256]{2,0,1:T(8,128)}, u32[]{:S(2)}) copy-start(f32[15,4,256]{2,0,1:T(8,128)} %get-tuple-element.213) | copy-start | bytes 184324
  393.1 67.0 %copy-start.85 = (f32[15,4,256]{2,0,1:T(8,128)S(1)}, f32[15,4,256]{2,0,1:T(8,128)}, u32[]{:S(2)}) copy-start(f32[15,4,256]{2,0,1:T(8,128)} %get-tuple-element.215) | copy-start | bytes 184324
  393.1 67.0 %copy-start.89 = (f32[1,4,256]{2,0,1:T(1,128)S(1)}, f32[1,4,256]{2,0,1:T(1,128)}, u32[]{:S(2)}) copy-start(f32[1,4,256]{2,0,1:T(1,128)} %get-tuple-element.143) | copy-start | bytes 12292
  393.1 67.0 %copy-start.91 = (f32[1,4,256]{2,0,1:T(1,128)S(1)}, f32[1,4,256]{2,0,1:T(1,128)}, u32[]{:S(2)}) copy-start(f32[1,4,256]{2,0,1:T(1,128)} %get-tuple-element.149) | copy-start | bytes 12292
  393.2 67.0 %copy-start.93 = (f32[1,4,256]{2,0,1:T(1,128)S(1)}, f32[1,4,256]{2,0,1:T(1,128)}, u32[]{:S(2)}) copy-start(f32[1,4,256]{2,0,1:T(1,128)} %get-tuple-element.144) | copy-start | bytes 12292
  393.2 67.0 %copy-start.95 = (f32[1,4,256]{2,0,1:T(1,128)S(1)}, f32[1,4,256]{2,0,1:T(1,128)}, u32[]{:S(2)}) copy-start(f32[1,4,256]{2,0,1:T(1,128)} %get-tuple-element.150) | copy-start | bytes 12292
  393.2 67.0 %copy-start.97 = (f32[1,4,256]{2,0,1:T(1,128)S(1)}, f32[1,4,256]{2,0,1:T(1,128)}, u32[]{:S(2)}) copy-start(f32[1,4,256]{2,0,1:T(1,128)} %get-tuple-element.148) | copy-start | bytes 12292
  393.2 67.0 %copy-start.99 = (f32[1,4,256]{2,0,1:T(1,128)S(1)}, f32[1,4,256]{2,0,1:T(1,128)}, u32[]{:S(2)}) copy-start(f32[1,4,256]{2,0,1:T(1,128)} %get-tuple-element.147) | copy-start | bytes 12292
  393.2 67.0 %copy-start.101 = (f32[1,4,256]{2,0,1:T(1,128)S(1)}, f32[1,4,256]{2,0,1:T(1,128)}, u32[]{:S(2)}) copy-start(f32[1,4,256]{2,0,1:T(1,128)} %get-tuple-element.146) | copy-start | bytes 12292
  393.2 67.0 %copy-start.103 = (f32[1,4,256]{2,0,1:T(1,128)S(1)}, f32[1,4,256]{2,0,1:T(1,128)}, u32[]{:S(2)}) copy-start(f32[1,4,256]{2,0,1:T(1,128)} %get-tuple-element.145) | copy-start | bytes 12292
  393.2 67.0 %copy-start.114 = (f32[1,4,256]{2,0,1:T(1,128)S(1)}, f32[1,4,256]{2,0,1:T(1,128)}, u32[]{:S(2)}) copy-start(f32[1,4,256]{2,0,1:T(1,128)} %get-tuple-element.211) | copy-start | bytes 12292
  393.2 67.0 %copy-start.115 = (f32[1,4,256]{2,0,1:T(1,128)S(1)}, f32[1,4,256]{2,0,1:T(1,128)}, u32[]{:S(2)}) copy-start(f32[1,4,256]{2,0,1:T(1,128)} %get-tuple-element.217) | copy-start | bytes 12292
  464.4 9.9 %collective-permute-start.5 = (f32[19,16,1,256]{3,1,2,0:T(8,128)S(1)}, f32[19,16,1,256]{3,1,2,0:T(8,128)S(1)}, u32[]{:S(2)}, u32[]{:S(2)}) collective-permute-start(f32[19,16,1,256]{3,1,2,0:T(8,128)S(1)} %get-tuple-element.109), channel_id=1, source_target_pairs={{4,0},{8,4},{12,8},{16,12},{20,16},{24,20},{28,24},{0,28},{5,1},{9... | collective-permute-start | bytes 933896 | tf_op jit(solution)/shard_map/ppermute | solution.py:48
  468.7 10.5 %collective-permute-start.4 = (f32[19,16,1,256]{3,1,2,0:T(8,128)S(1)}, f32[19,16,1,256]{3,1,2,0:T(8,128)S(1)}, u32[]{:S(2)}, u32[]{:S(2)}) collective-permute-start(f32[19,16,1,256]{3,1,2,0:T(8,128)S(1)} %get-tuple-element.110), channel_id=1, source_target_pairs={{0,4},{4,8},{8,12},{12,16},{16,20},{20,24},{24,28},{28,0},{1,5},{5... | collective-permute-start | bytes 933896 | tf_op jit(solution)/shard_map/ppermute | solution.py:46
  483.2 4.5 collective-permute-start.6
  483.3 3.5 collective-permute-start.7
  (113 other events, 1376.5 us)
Sparse Core Ops, SparseCore 0:
  97.4 33.0 all-reduce.4
  329.3 31.0 all-reduce.6
where the time goes:
time: 520 us; the launch traced here: 512 us
  matrix products  252 us (48%)
  local copies, waits for them, and re-layouts  86 us (17%)
  waiting for transfers between devices  78.2 us (15%)
  other arithmetic  61.2 us (12%)
  between operations  16.4 us (3%)
  starting transfers between devices  12 us (2%)
  blocking collectives  6.29 us (1%)
    dot_general x2, matrix products, per_device(): jnp.dot(weighted, weight_y, precision=highest)  133 us
    dot_general x2, matrix products, per_device(): jnp.dot(flow.reshape(3 * depth * tile_x, tile_y), weight_y.T, precision=h...  118 us
    psum x2, waiting for transfers between devices, per_device(): row_speed = lax.psum(partial_speed, 'gy')  62.1 us
    mul x4, local copies, waits for them, and re-layouts, per_device(): slot_force[:, None, None, :] * plane_weight[None]  48.4 us
    unnamed x55, other arithmetic  17.8 us
    mul x2, other arithmetic, per_device(): slot_force[:, None, None, :] * plane_weight[None]  12.2 us
  transfers between devices with their start and end apart: 10, of which 8 were waited for; matrix products, arithmetic and copies ran while one was open for 3% of the time, Pallas kernels for 0%

commit v1 on v0

v1 whole, which is shorter than its diff:
```python
import functools
import math

import jax
import jax.numpy as jnp
from jax import lax
from jax.experimental import pallas as pl
from jax.experimental.pallas import tpu as pltpu
from jax.sharding import PartitionSpec as P

STEPS = 2

velocity_set = (
    (0, 0, 0),
    (1, 0, 0),
    (-1, 0, 0),
    (0, 1, 0),
    (0, -1, 0),
    (0, 0, 1),
    (0, 0, -1),
    (1, 1, 0),
    (-1, -1, 0),
    (1, -1, 0),
    (-1, 1, 0),
    (1, 0, 1),
    (-1, 0, -1),
    (1, 0, -1),
    (-1, 0, 1),
    (0, 1, 1),
    (0, -1, -1),
    (0, 1, -1),
    (0, -1, 1),
)
lattice_weight = (1.0 / 3.0,) + (1.0 / 18.0,) * 6 + (1.0 / 36.0,) * 12
unit = 0.002
feedback_gain = 2.0
EAST = tuple(i for i in range(19) if velocity_set[i][0] == 1)
WEST = tuple(i for i in range(19) if velocity_set[i][0] == -1)

DEPTH = 16
ROWS = DEPTH * 8
BLOCK = 128
GROUP = 4
FIELDS = 9
VMEM_LIMIT = 40 * 1024 * 1024


def opposite(entry):
    return entry + 1 if entry % 2 == 1 else entry - 1


def iotas(shape=(8, 128)):
    return lax.broadcasted_iota(jnp.int32, shape, 0), lax.broadcasted_iota(jnp.int32, shape, 1)


def turn(value, shift, axis):
    shift = shift % value.shape[axis]
    return pltpu.roll(value, shift, axis) if shift else value


def pack_edges(slices):
    _, lane = iotas()
    total = jnp.zeros((8, 128), jnp.float32)
    for z in range(DEPTH):
        total = jnp.where((lane >= 5 * z) & (lane < 5 * z + 5), turn(slices(z), 5 * z + 2, 1), total)
    return total


def signed_sum(terms):
    total = None
    for sign, value in terms:
        if total is None:
            total = value if sign > 0 else -value
        else:
            total = total + value if sign > 0 else total - value
    return total


def dot_c(vector, parts):
    return signed_sum([(vector[a], parts[a]) for a in range(3) if vector[a] != 0])


def moments(dev):
    total = dev[0]
    for entry in range(1, 19):
        total = total + dev[entry]
    momentum = [
        signed_sum([(velocity_set[e][a], dev[e]) for e in range(19) if velocity_set[e][a] != 0]) for a in range(3)
    ]
    return total, momentum, 1.0 + unit * total


def collide(dev, force):
    total, momentum, dens = moments(dev)
    inverse = 1.0 / dens
    vel = [(momentum[a] + 0.5 * force[a]) * inverse for a in range(3)]
    odd_base = [3.75 * momentum[a] + 3.0 * force[a] for a in range(3)]
    even_base = [5.625 * momentum[a] + 6.1875 * force[a] for a in range(3)]
    along = vel[0] * even_base[0] + vel[1] * even_base[1] + vel[2] * even_base[2]
    base = 1.25 * total - (unit / 3.0) * along
    post = [lattice_weight[0] * base - 0.25 * dev[0]]
    scaled = [unit * vel[a] for a in range(3)]
    for entry in range(1, 19, 2):
        vector, weight = velocity_set[entry], lattice_weight[entry]
        odd = weight * dot_c(vector, odd_base)
        even = weight * (base + dot_c(vector, scaled) * dot_c(vector, even_base))
        post.append((even + odd) - 0.25 * dev[entry])
        post.append((even - odd) - 0.25 * dev[entry + 1])
    return post


def edge_kernel(pop_ref, edge_ref):
    for entry in range(19):
        edge_ref[entry] = pack_edges(lambda z: pop_ref[entry, 8 * z : 8 * z + 8, :])


def shifted(tiles, shift):
    lane = lax.broadcasted_iota(jnp.int32, tiles[0].shape, 1)
    if shift == 0:
        return tiles[1:-1]
    rolled = [turn(tile, -shift, 1) for tile in tiles]
    if shift > 0:
        return [jnp.where(lane >= 128 - shift, rolled[i + 1], rolled[i]) for i in range(1, len(tiles) - 1)]
    return [jnp.where(lane < -shift, rolled[i - 1], rolled[i]) for i in range(1, len(tiles) - 1)]


def basis_fields(four):
    return (
        0.25 * ((four[0] + four[2]) + (four[1] + four[3])),
        0.25 * (four[2] - four[0]),
        0.25 * (four[1] - four[3]),
    )


def basis_cells(three):
    one, sine, cosine = three
    return one - sine, one + cosine, one + sine, one - cosine


def prepare_matrix(flow_ref, halo_ref, matrix_ref):
    for c in range(3):
        per_x = []
        for x in range(4):
            per_x.append(
                [
                    halo_ref[c, pl.ds(4 + x, DEPTH, stride=8), :],
                    flow_ref[c, pl.ds(x, DEPTH, stride=8), :],
                    flow_ref[c, pl.ds(4 + x, DEPTH, stride=8), :],
                    halo_ref[c, pl.ds(x, DEPTH, stride=8), :],
                ]
            )
        by_basis = [basis_fields([per_x[x][t] for x in range(4)]) for t in range(4)]
        for xf in range(3):
            tiles = [by_basis[t][xf] for t in range(4)]
            four = [shifted(tiles, s) for s in (-1, 0, 1, 2)]
            for half in range(2):
                fields = basis_fields([four[s][half] for s in range(4)])
                for yf in range(3):
                    row = ((c * 3 + yf) * 3 + xf) * DEPTH
                    high = fields[yf].astype(jnp.bfloat16)
                    low = (fields[yf] - high.astype(jnp.float32)).astype(jnp.bfloat16)
                    matrix_ref[row : row + DEPTH, half * 128 : half * 128 + 128] = high
                    matrix_ref[row : row + DEPTH, 256 + half * 128 : 256 + half * 128 + 128] = low


def couple(slots, table_ref, matrix_ref, total_ref, speed_ref):
    rows = 3 * FIELDS * DEPTH
    width = GROUP * BLOCK
    total_ref[...] = jnp.zeros_like(total_ref)
    column = lax.broadcasted_iota(jnp.int32, (256, BLOCK), 0).astype(jnp.float32)
    z_cell = lax.broadcasted_iota(jnp.int32, (DEPTH, BLOCK), 0).astype(jnp.float32)

    def body(step, carry):
        first = step * GROUP
        hot, weight_z, coef = [], [], []
        for g in range(GROUP):
            slot = first + g
            q = lambda k: table_ref[slot, k : k + 1, :]
            hot.append(jnp.where(column == q(0), 1.0, 0.0).astype(jnp.bfloat16))
            gap = z_cell - q(5)
            sine, cosine = q(6), q(7)
            weight_z.append(
                jnp.where(
                    gap == -1.0,
                    0.25 - 0.25 * sine,
                    jnp.where(
                        gap == 0.0,
                        0.25 + 0.25 * cosine,
                        jnp.where(gap == 1.0, 0.25 + 0.25 * sine, jnp.where(gap == 2.0, 0.25 - 0.25 * cosine, 0.0)),
                    ),
                )
            )
            by, bx = (None, q(1), q(2)), (None, q(3), q(4))
            coef.append(
                [
                    [by[i] if bx[k] is None else bx[k] if by[i] is None else by[i] * bx[k] for k in range(3)]
                    for i in range(3)
                ]
            )
        hot = jnp.concatenate(hot, axis=1)
        across = jnp.dot(
            matrix_ref[...], jnp.concatenate([hot, hot], axis=0), preferred_element_type=jnp.float32
        )
        spread_high, spread_low = [], []
        for g in range(GROUP):
            slot = first + g
            columns = slice(g * BLOCK, (g + 1) * BLOCK)
            pieces = []
            for c in range(3):
                sums = None
                for yf in range(3):
                    for xf in range(3):
                        row = ((c * 3 + yf) * 3 + xf) * DEPTH
                        term = across[row : row + DEPTH, columns]
                        factor = coef[g][yf][xf]
                        term = term if factor is None else term * factor
                        sums = term if sums is None else sums + term
                speed = jnp.sum(sums * weight_z[g], axis=0, keepdims=True)
                speed_ref[slot, c : c + 1, :] = speed
                push = (table_ref[slot, 8 + c : 9 + c, :] - feedback_gain * speed) * table_ref[slot, 11:12, :]
                for yf in range(3):
                    for xf in range(3):
                        factor = coef[g][yf][xf]
                        pieces.append(weight_z[g] * (push if factor is None else push * factor))
            piece = jnp.concatenate(pieces, axis=0)
            high = piece.astype(jnp.bfloat16)
            spread_high.append(high)
            spread_low.append((piece - high.astype(jnp.float32)).astype(jnp.bfloat16))
        left = jnp.concatenate(spread_high + spread_low, axis=1)
        total_ref[...] += lax.dot_general(
            left,
            jnp.concatenate([hot, hot], axis=1),
            (((1,), (1,)), ((), ())),
            preferred_element_type=jnp.float32,
        )
        return carry

    lax.fori_loop(0, slots // GROUP, body, 0)


def finish_force(total_ref, halo_ref, force_ref, force_edge_ref):
    lane = lax.broadcasted_iota(jnp.int32, (DEPTH, 128), 1)
    zero = jnp.zeros((DEPTH, 128), jnp.float32)
    for c in range(3):
        by_basis = []
        for xf in range(3):
            field = []
            for yf in range(3):
                row = ((c * 3 + yf) * 3 + xf) * DEPTH
                field.append([total_ref[row : row + DEPTH, 0:128], total_ref[row : row + DEPTH, 128:256]])
            cells = [basis_cells([field[yf][half] for yf in range(3)]) for half in range(2)]
            sums = None
            for k, shift in enumerate((1, 0, -1, -2)):
                tiles = shifted([zero, zero, cells[0][k], cells[1][k], zero, zero], shift)
                sums = tiles if sums is None else [a + b for a, b in zip(sums, tiles)]
            by_basis.append(sums)
        by_x = [basis_cells([by_basis[xf][t] * 0.0625 for xf in range(3)]) for t in range(4)]
        for x in range(4):
            left, low, high, right = (by_x[t][x] for t in range(4))
            force_ref[c, pl.ds(x, DEPTH, stride=8), :] = low
            force_ref[c, pl.ds(4 + x, DEPTH, stride=8), :] = high
            halo_ref[c, pl.ds(4 + x, DEPTH, stride=8), :] = jnp.where(lane >= 64, left, low)
            halo_ref[c, pl.ds(x, DEPTH, stride=8), :] = jnp.where(lane >= 64, high, right)
        force_edge_ref[c] = pack_edges(lambda z: halo_ref[c, 8 * z : 8 * z + 8, :])


def flow_slices(load, flow_ref):
    for z in range(DEPTH):
        total, momentum, dens = moments(load(z))
        inverse = 1.0 / dens
        for c in range(3):
            flow_ref[c, 8 * z : 8 * z + 8, :] = momentum[c] * inverse


def flow_edges(edges, halo_ref):
    total, momentum, dens = moments(edges)
    inverse = 1.0 / dens
    for c in range(3):
        flow = momentum[c] * inverse
        for z in range(DEPTH):
            halo_ref[c, 8 * z : 8 * z + 8, :] = turn(flow, -(5 * z + 2), 1)


def gather_markers(span_y, slots, spans_ref, where_ref, stiff_ref, fraction_ref, span_ref, places_ref, picked_ref, table_ref):
    filaments = fraction_ref.shape[0] // 3
    blocks = fraction_ref.shape[1]
    block, lane = iotas((blocks, BLOCK))
    anchor = (where_ref[0] * 4).astype(jnp.float32)
    mine = where_ref[1]
    tile_start = (mine * 256).astype(jnp.float32)
    for f in range(filaments):
        places = [
            anchor + 1.0 + fraction_ref[3 * f] * (4 - 3.01),
            span_ref[f] + fraction_ref[3 * f + 1] * 256.0,
            1.0 + fraction_ref[3 * f + 2] * (DEPTH - 3.01),
        ]
        factor = stiff_ref[f].astype(jnp.float32) * (1.0 / 256.0)
        for c in range(3):
            ahead = turn(places[c], -1, 1)
            ahead = jnp.where(lane == BLOCK - 1, turn(ahead, -1, 0), ahead) - places[c]
            if c == 1:
                half = 0.5 * span_y
                ahead = jnp.where(ahead > half, ahead - span_y, jnp.where(ahead < -half, ahead + span_y, ahead))
            ahead = jnp.where((lane == BLOCK - 1) & (block == blocks - 1), 0.0, ahead)
            behind = turn(ahead, 1, 1)
            behind = jnp.where(lane == 0, turn(behind, 1, 0), behind)
            start = f * blocks * 8
            places_ref[pl.ds(start + 3 + c, blocks, stride=8), :] = (ahead - behind) * factor
        places_ref[pl.ds(start, blocks, stride=8), :] = places[0] - anchor
        places_ref[pl.ds(start + 1, blocks, stride=8), :] = places[1] - tile_start
        places_ref[pl.ds(start + 2, blocks, stride=8), :] = places[2]
    picked_ref[...] = jnp.zeros_like(picked_ref)

    def pick(index, count):
        source = pl.multiple_of(index * 8, 8)
        target = pl.multiple_of(count * 8, 8)
        picked_ref[pl.ds(target, 8), :] = places_ref[pl.ds(source, 8), :]
        return count + (spans_ref[index] == mine).astype(jnp.int32)

    count = lax.fori_loop(0, filaments * blocks, pick, jnp.int32(0))
    got = lambda k: picked_ref[pl.ds(k, slots, stride=8), :]
    slot, _ = iotas((slots, BLOCK))

    def put(k, value):
        table_ref[:, k, :] = value

    def basis(t):
        return jnp.cos((0.5 * math.pi) * (1.0 - t)), jnp.cos((0.5 * math.pi) * t)

    y = got(1)
    base = jnp.minimum(jnp.floor(y), 255.0)
    put(0, base)
    sine, cosine = basis(y - base)
    put(1, sine)
    put(2, cosine)
    sine, cosine = basis(got(0) - 1.0)
    put(3, sine)
    put(4, cosine)
    z = got(2)
    base = jnp.floor(z)
    put(5, base)
    sine, cosine = basis(z - base)
    put(6, sine)
    put(7, cosine)
    for c in range(3):
        put(8 + c, got(3 + c))
    put(11, jnp.where(slot < count, 1.0, 0.0))


def first_kernel(
    span_y, slots, spans_ref, where_ref, stiff_ref,
    pop_ref, edge_ref, left_ref, right_ref, fraction_ref, span_ref,
    force_ref, force_edge_ref, edges_ref, table_ref,
    flow_ref, halo_ref, matrix_ref, total_ref, speed_ref, places_ref, picked_ref,
):
    gather_markers(span_y, slots, spans_ref, where_ref, stiff_ref, fraction_ref, span_ref, places_ref, picked_ref, table_ref)
    row, lane = iotas()
    j = lane % 5
    from_left = (row >= 4) & (j < 2)
    from_right = (row < 4) & (j >= 2)
    edges = []
    for entry in range(19):
        own = turn(edge_ref[entry], 4, 0)
        value = jnp.where(from_left, left_ref[entry], jnp.where(from_right, right_ref[entry], own))
        edges_ref[entry] = value
        edges.append(value)
    flow_slices(lambda z: [pop_ref[e, 8 * z : 8 * z + 8, :] for e in range(19)], flow_ref)
    flow_edges(edges, halo_ref)
    prepare_matrix(flow_ref, halo_ref, matrix_ref)
    couple(slots, table_ref, matrix_ref, total_ref, speed_ref)
    finish_force(total_ref, halo_ref, force_ref, force_edge_ref)


def collide_kernel(pop_ref, edges_ref, force_ref, force_edge_ref, left_ref, right_ref, post_ref, post_edge_ref, east_ref, west_ref):
    row, lane = iotas()
    force_edge = [
        force_edge_ref[c] + jnp.where(row >= 4, turn(left_ref[c], 4, 0), turn(right_ref[c], 4, 0)) for c in range(3)
    ]
    swapped = [turn(value, 4, 0) for value in force_edge]
    patch = ((row < 4) & (lane < 3)) | ((row >= 4) & (lane >= 126))
    for z in range(DEPTH):
        part = slice(8 * z, 8 * z + 8)
        force = [jnp.where(patch, turn(swapped[c], -(5 * z + 2), 1), force_ref[c, part, :]) for c in range(3)]
        post = collide([pop_ref[e, part, :] for e in range(19)], force)
        for e in range(19):
            post_ref[e, part, :] = post[e]
    post = collide([edges_ref[e] for e in range(19)], force_edge)
    for e in range(19):
        post_edge_ref[e] = post[e]
    for k in range(5):
        east_ref[k, 0:32, :] = post_ref[EAST[k], pl.ds(3, 32, stride=4), :]
        east_ref[k, 32:40, :] = post[EAST[k]]
        west_ref[k, 0:32, :] = post_ref[WEST[k], pl.ds(0, 32, stride=4), :]
        west_ref[k, 32:40, :] = post[WEST[k]]


def stream(post_ref, post_edge_ref, east_ref, west_ref, moved_ref, store, store_edge):
    row, lane = iotas()
    patches = {1: (row < 4) & (lane == 0), -1: (row >= 4) & (lane == 127)}
    low_wall, high_wall = lane < 5, lane >= 75
    for e in range(19):
        cx, cy, cz = velocity_set[e]
        edge = post_edge_ref[e]
        if cx == 1:
            k = EAST.index(e)
            edge = jnp.where(row % 4 == 0, turn(east_ref[k, 32:40, :], 5, 0), turn(edge, 1, 0))
        elif cx == -1:
            k = WEST.index(e)
            edge = jnp.where(row % 4 == 3, turn(west_ref[k, 32:40, :], 3, 0), turn(edge, -1, 0))
        edge = turn(edge, cy + 5 * cz, 1)
        if cz == 1:
            edge = jnp.where(low_wall, post_edge_ref[opposite(e)], edge)
        elif cz == -1:
            edge = jnp.where(high_wall, post_edge_ref[opposite(e)], edge)
        store_edge(e, edge)
        if cx != 0:
            for z in range(DEPTH):
                moved_ref[k, 8 * z : 8 * z + 8, :] = turn(post_ref[e, 8 * z : 8 * z + 8, :], cx, 0)
            if cx == 1:
                moved_ref[k, pl.ds(0, 32, stride=4), :] = east_ref[k, 0:32, :]
            else:
                moved_ref[k, pl.ds(3, 32, stride=4), :] = west_ref[k, 0:32, :]
        swapped = turn(edge, 4, 0)
        for z in range(DEPTH):
            source = z - cz
            if 0 <= source < DEPTH:
                part = slice(8 * source, 8 * source + 8)
                value = post_ref[e, part, :] if cx == 0 else moved_ref[k, part, :]
                if cy != 0:
                    value = turn(value, cy, 1)
                    value = jnp.where(lane == (0 if cy == 1 else 127), turn(value, 4, 0), value)
                    value = jnp.where(patches[cy], turn(swapped, -(5 * z + 2), 1), value)
            else:
                value = post_ref[opposite(e), 8 * z : 8 * z + 8, :]
            store(e, z, value)


def second_kernel(
    slots, blocks, shares, spans_ref, where_ref,
    post_ref, post_edge_ref, east_ref, west_ref, table_ref,
    dev_ref, edges_ref, force_ref, force_edge_ref, speeds_ref,
    moved_ref, flow_ref, halo_ref, matrix_ref, total_ref, speed_ref, spot_ref,
):
    def store(e, z, value):
        dev_ref[e, 8 * z : 8 * z + 8, :] = value

    def store_edge(e, value):
        edges_ref[e] = value

    stream(post_ref, post_edge_ref, east_ref, west_ref, moved_ref, store, store_edge)
    flow_slices(lambda z: [dev_ref[e, 8 * z : 8 * z + 8, :] for e in range(19)], flow_ref)
    flow_edges([edges_ref[e] for e in range(19)], halo_ref)
    prepare_matrix(flow_ref, halo_ref, matrix_ref)
    speed_ref[...] = jnp.zeros_like(speed_ref)
    couple(slots, table_ref, matrix_ref, total_ref, speed_ref)
    finish_force(total_ref, halo_ref, force_ref, force_edge_ref)
    mine = where_ref[1]

    def place(index, count):
        here = spans_ref[index] == mine
        value = speed_ref[jnp.minimum(count, slots - 1)]
        spot_ref[pl.ds(pl.multiple_of(index * 8, 8), 8), :] = jnp.where(here, value, 0.0)
        return count + here.astype(jnp.int32)

    lax.fori_loop(0, spans_ref.shape[0], place, jnp.int32(0))
    filaments = spans_ref.shape[0] // blocks
    share = blocks // shares
    for s in range(shares):
        for f in range(filaments):
            for c in range(3):
                speeds_ref[s, 3 * f + c] = spot_ref[pl.ds((f * blocks + s * share) * 8 + c, share, stride=8), :]


def last_kernel(post_ref, post_edge_ref, east_ref, west_ref, dev_ref, moved_ref):
    def store(e, z, value):
        dev_ref[e, 8 * z : 8 * z + 8, :] = value

    stream(post_ref, post_edge_ref, east_ref, west_ref, moved_ref, store, lambda e, value: None)


def call(body, outs, scratch, n_smem, args):
    spec = [pl.BlockSpec(memory_space=pltpu.SMEM)] * n_smem
    spec += [pl.BlockSpec(memory_space=pltpu.VMEM)] * (len(args) - n_smem)
    return pl.pallas_call(
        body,
        out_shape=[jax.ShapeDtypeStruct(shape, jnp.float32) for shape in outs],
        in_specs=spec,
        out_specs=[pl.BlockSpec(memory_space=pltpu.VMEM)] * len(outs),
        scratch_shapes=scratch,
        compiler_params=pltpu.CompilerParams(vmem_limit_bytes=VMEM_LIMIT),
    )(*args)


def ring(value, axis, step):
    count = lax.axis_size(axis)
    return lax.ppermute(value, axis, [(i, (i + step) % count) for i in range(count)])


def per_device(populations, fraction, spans, stiffness):
    depth, tile_x, tile_y = populations.shape[1:]
    columns = lax.axis_size("gy")
    span_y = float(tile_y * columns)
    my_row, my_column = lax.axis_index("gx"), lax.axis_index("gy")
    filaments, _, share = fraction.shape
    blocks = spans.shape[1]
    share_blocks = share // BLOCK
    slots = max(GROUP, 2 * filaments * blocks // columns)
    f32 = jnp.float32

    field = (19, ROWS, 128)
    edge = (19, 8, 128)
    halves = tile_y // 128
    pop = populations.reshape(19, depth, tile_x, halves, 128).transpose(0, 1, 3, 2, 4).reshape(field)
    rows = lax.all_gather(fraction.reshape(filaments * 3, share_blocks, BLOCK), "gy", axis=0)
    rows = rows.transpose(1, 0, 2, 3).reshape(filaments * 3, blocks, BLOCK)
    flat_spans = spans[:, :, 0].reshape(-1)
    span_rows = jnp.broadcast_to((spans * tile_y).astype(f32), (filaments, blocks, BLOCK))
    where = jnp.stack([my_row, my_column]).astype(jnp.int32)

    (own_edge,) = call(edge_kernel, [edge], [], 0, (pop,))
    left, right = ring(own_edge, "gy", 1), ring(own_edge, "gy", -1)

    force_shape, force_edge_shape = (3, ROWS, 128), (3, 8, 128)
    table_shape = (slots, 16, BLOCK)
    coupling = [
        pltpu.VMEM(force_shape, f32),
        pltpu.VMEM(force_shape, f32),
        pltpu.VMEM((3 * FIELDS * DEPTH, 512), jnp.bfloat16),
        pltpu.VMEM((3 * FIELDS * DEPTH, 256), f32),
        pltpu.VMEM((slots, 8, BLOCK), f32),
    ]
    force, force_edge, edges, table = call(
        functools.partial(first_kernel, span_y, slots),
        [force_shape, force_edge_shape, edge, table_shape],
        coupling + [pltpu.VMEM((filaments * blocks * 8, BLOCK), f32), pltpu.VMEM(((slots + 1) * 8, BLOCK), f32)],
        3,
        (flat_spans, where, stiffness, pop, own_edge, left, right, rows, span_rows),
    )

    plane = (5, 40, 128)
    moved = pltpu.VMEM((5, ROWS, 128), f32)

    def collision(dev, edges, force, force_edge):
        left, right = ring(force_edge, "gy", 1), ring(force_edge, "gy", -1)
        post, post_edge, east, west = call(
            collide_kernel, [field, edge, plane, plane], [], 0, (dev, edges, force, force_edge, left, right)
        )
        return post, post_edge, ring(east, "gx", 1), ring(west, "gx", -1)

    post = collision(pop, edges, force, force_edge)
    speeds_shape = (columns, filaments * 3, share_blocks, BLOCK)
    dev, edges, force, force_edge, speeds = call(
        functools.partial(second_kernel, slots, blocks, columns),
        [field, edge, force_shape, force_edge_shape, speeds_shape],
        [moved] + coupling + [pltpu.VMEM((filaments * blocks * 8, BLOCK), f32)],
        2,
        (flat_spans, where) + tuple(post) + (table,),
    )
    post = collision(dev, edges, force, force_edge)
    speed = jnp.sum(lax.all_to_all(speeds, "gy", 0, 0, tiled=True), axis=0)
    (dev,) = call(last_kernel, [field], [moved], 0, tuple(post))
    dev = dev.reshape(19, depth, halves, tile_x, 128).transpose(0, 1, 3, 2, 4).reshape(populations.shape)
    return dev, speed.reshape(fraction.shape)


def solution(mesh):
    placed = (P(None, None, "gx", "gy"), P("gx", None, "gy"), P("gx", None, None), P("gx"))
    return jax.shard_map(
        per_device,
        mesh=mesh,
        in_specs=placed,
        out_specs=(P(None, None, "gx", "gy"), P("gx", None, "gy")),
        check_vma=False,
    )
```

time: 520 us -> 62.1 us (0.12); the launches traced: 512 us -> 62 us
  matrix products: 252 us -> 0 us
  local copies, waits for them, and re-layouts: 86 us -> 2.66 us
  waiting for transfers between devices: 78.2 us -> 9.04 us
  other arithmetic: 61.2 us -> 0.75 us
  Pallas kernels: 0 us -> 23 us
  between operations: 16.4 us -> 0.73 us
  blocking collectives: 6.29 us -> 12.1 us
    dot_general x6 -> x0, matrix products: 252 us -> none  [the longest x2 133 us: per_device(): jnp.dot(weighted, weight_y, precision=highest)]
    psum x2 -> x0, waiting for transfers between devices: 62.1 us -> none  [per_device(): row_speed = lax.psum(partial_speed, 'gy')]
    mul x4 -> x0, local copies, waits for them, and re-layouts: 48.4 us -> none  [per_device(): slot_force[:, None, None, :] * plane_weight[None]]
    pallas_call x0 -> x6, Pallas kernels: none -> 23 us  [call(): pl.pallas_call(body, out_shape=[jax.ShapeDtypeStruct(shape, jnp.float32)...]
    unnamed x55 -> x0, other arithmetic: 17.8 us -> none
    mul x4 -> x0, other arithmetic: 12.4 us -> none  [the longest x2 12.2 us: per_device(): slot_force[:, None, None, :] * plane_weight[None]]
    slice x16 -> x0, local copies, waits for them, and re-layouts: 10.9 us -> none  [the longest x4 3.91 us: extended_2(): lax.slice_in_dim(cells, cells.shape[dim] - width, cells.shape[dim], axis=...]
    add x13 -> x0, other arithmetic: 7.94 us -> none  [the longest x6 5.81 us: relax(): post.append(fpop[entry] - (fpop[entry] - equil) / relax_time + source)]
  transfers between devices with their start and end apart: 10 -> 10, of which waited for: 8 -> 6; matrix products, arithmetic and copies ran while one was open for 3% -> 3% of each run, Pallas kernels for 0% -> 0%
where the time goes in v1:
time: 62.1 us; the launch traced here: 62 us
  Pallas kernels  23 us (37%)
  starting transfers between devices  13.7 us (22%)
  blocking collectives  12.1 us (19%)
  waiting for transfers between devices  9.04 us (15%)
  local copies, waits for them, and re-layouts  2.66 us (4%)
  other arithmetic  0.75 us (1%)
  between operations  0.73 us (1%)
    pallas_call x6, Pallas kernels, call(): pl.pallas_call(body, out_shape=[jax.ShapeDtypeStruct(shape, jnp.float32)...  23 us
    ppermute x10, starting transfers between devices, ring(): lax.ppermute(value, axis, [(i, (i + step) % count) for i in range(count)])  13.7 us
    ppermute x10, waiting for transfers between devices, ring(): lax.ppermute(value, axis, [(i, (i + step) % count) for i in range(count)])  9.04 us
    all_to_all x1, blocking collectives, per_device(): speed = jnp.sum(lax.all_to_all(speeds, 'gy', 0, 0, tiled=True), axis=0)  6.66 us
    all_gather x1, blocking collectives, per_device(): lax.all_gather(fraction.reshape(filaments * 3, share_blocks, BLOCK), 'gy'...  5.42 us
    unnamed x13, local copies, waits for them, and re-layouts  2.47 us
  transfers between devices with their start and end apart: 10, of which 6 were waited for; matrix products, arithmetic and copies ran while one was open for 3% of the time, Pallas kernels for 0%

profile of v1, /device:TPU:0, one launch (start us, length us, event | category | flops | bytes accessed | tf_op | source)
XLA Modules:
  0.0 62.0 jit_solution(4855376985608889133)
XLA Ops:
  0.7 1.3 %copy-done = f32[19,16,4,256]{3,2,1,0:T(4,128)S(1)} copy-done((f32[19,16,4,256]{3,2,1,0:T(4,128)S(1)}, f32[19,16,4,256]{3,2,1,0:T(4,128)}, u32[]{:S(2)}) %copy-start) | copy-done | bytes 1245208
  2.0 0.4 shard_map.59.edge_ref
  2.3 2.4 %collective-permute-start.1 = (f32[19,8,128]{2,1,0:T(8,128)S(1)}, f32[19,8,128]{2,1,0:T(8,128)S(1)}, u32[]{:S(2)}, u32[]{:S(2)}) collective-permute-start(f32[19,8,128]{2,1,0:T(8,128)S(1)} %shard_map.59.edge_ref), channel_id=1, source_target_pairs={{0,3},{1,0},{2,1},{3,2},{4,7},{5,4},{6,5},{7,6},{8,11},{9,8},{10,9... | collective-permute-start | bytes 233480 | tf_op jit(solution)/shard_map/ppermute | solution.py:496
  4.8 0.0 collective-permute-start
  4.8 0.5 broadcast.3
  5.3 0.7 %multiply_convert_fusion = (f32[2,32,1]{1,2,0:T(1,128)S(1)}, s32[2,32]{1,0:T(2,128)S(1)}) fusion(s32[2,32,1]{1,2,0:T(1,128)S(1)} %copy-done.4, s32[]{:T(128)} %broadcast.3), kind=kLoop, calls=%fused_computation.1 | loop fusion | flops 128 | bytes 772 | tf_op jit(solution)/shard_map/convert_element_type | solution.py:517
  6.0 0.1 reshape_squeeze.3.spans_ref
  6.1 5.4 %all_gather.3 = f32[4,6,8,128]{3,2,1,0:T(8,128)S(1)} all-gather(f32[1,6,8,128]{3,2,1,0:T(8,128)S(1)} %all_gather_reshape.3), channel_id=1, replica_groups=mesh['gx'=8,'gy'=4] {'gy'}, dimensions={0}, use_global_device_ids=true | all-gather | bytes 122880 | tf_op jit(solution)/shard_map/all_gather | solution.py:514
  11.5 0.1 pad_add_fusion.where_ref
  11.6 0.1 broadcast_in_dim.8.span_ref
  11.7 9.8 %shard_map.60 = (f32[3,128,128]{2,1,0:T(8,128)S(1)}, f32[3,8,128]{2,1,0:T(8,128)S(1)}, f32[19,8,128]{2,1,0:T(8,128)S(1)}, f32[32,16,128]{2,1,0:T(8,128)S(1)}) custom-call(s32[64]{0:T(128)S(1)} %reshape_squeeze.3.spans_ref, s32[2]{0:T(128)S(1)} %pad_add_fusion.where_ref, s32[2]{0:T(128)S(1)} %copy-done.2, f32[19,128,128]{2,1,0:T(8,128)S(1)} %bitcast.20, ...), custom_call_target="tpu_custom_call" | custom-call | tf_op jit(solution)/shard_map/pallas_call | solution.py:484
  21.5 1.1 %collective-permute-start.3 = (f32[3,8,128]{2,1,0:T(8,128)S(1)}, f32[3,8,128]{2,1,0:T(8,128)S(1)}, u32[]{:S(2)}, u32[]{:S(2)}) collective-permute-start(f32[3,8,128]{2,1,0:T(8,128)S(1)} %get-tuple-element.21.force_edge_ref), channel_id=1, source_target_pairs={{0,3},{1,0},{2,1},{3,2},{4,7},{5,4},{6,5},{7,6},{8,11},{9,8},{10,9... | collective-permute-start | bytes 36872 | tf_op jit(solution)/shard_map/ppermute | solution.py:496
  22.6 0.0 collective-permute-start.2
  22.6 1.4 %collective-permute-done.3.right_ref = f32[3,8,128]{2,1,0:T(8,128)S(1)} collective-permute-done((f32[3,8,128]{2,1,0:T(8,128)S(1)}, f32[3,8,128]{2,1,0:T(8,128)S(1)}, u32[]{:S(2)}, u32[]{:S(2)}) %collective-permute-start.3) | collective-permute-done | bytes 12320 | tf_op jit(solution)/shard_map/ppermute | solution.py:496
  24.0 1.7 %collective-permute-done.2.left_ref = f32[3,8,128]{2,1,0:T(8,128)S(1)} collective-permute-done((f32[3,8,128]{2,1,0:T(8,128)S(1)}, f32[3,8,128]{2,1,0:T(8,128)S(1)}, u32[]{:S(2)}, u32[]{:S(2)}) %collective-permute-start.2) | collective-permute-done | bytes 12320 | tf_op jit(solution)/shard_map/ppermute | solution.py:496
  25.8 0.6 shard_map.61
  26.3 1.6 %collective-permute-start.4 = (f32[5,40,128]{2,1,0:T(8,128)S(1)}, f32[5,40,128]{2,1,0:T(8,128)S(1)}, u32[]{:S(2)}, u32[]{:S(2)}) collective-permute-start(f32[5,40,128]{2,1,0:T(8,128)S(1)} %get-tuple-element.24), channel_id=1, source_target_pairs={{0,4},{4,8},{8,12},{12,16},{16,20},{20,24},{24,28},{28,0},{1,5},{5... | collective-permute-start | bytes 307208 | tf_op jit(solution)/shard_map/ppermute | solution.py:496
  27.9 3.2 %collective-permute-start.5 = (f32[5,40,128]{2,1,0:T(8,128)S(1)}, f32[5,40,128]{2,1,0:T(8,128)S(1)}, u32[]{:S(2)}, u32[]{:S(2)}) collective-permute-start(f32[5,40,128]{2,1,0:T(8,128)S(1)} %get-tuple-element.25), channel_id=1, source_target_pairs={{0,28},{4,0},{8,4},{12,8},{16,12},{20,16},{24,20},{28,24},{1,29},{... | collective-permute-start | bytes 307208 | tf_op jit(solution)/shard_map/ppermute | solution.py:496
  31.1 2.7 %collective-permute-done.4.east_ref = f32[5,40,128]{2,1,0:T(8,128)S(1)} collective-permute-done((f32[5,40,128]{2,1,0:T(8,128)S(1)}, f32[5,40,128]{2,1,0:T(8,128)S(1)}, u32[]{:S(2)}, u32[]{:S(2)}) %collective-permute-start.4) | collective-permute-done | bytes 102432 | tf_op jit(solution)/shard_map/ppermute | solution.py:496
  33.8 0.5 collective-permute-done.5.west_ref
  34.3 9.9 %shard_map.62 = (f32[19,128,128]{2,1,0:T(8,128)S(1)}, f32[19,8,128]{2,1,0:T(8,128)S(1)}, f32[3,128,128]{2,1,0:T(8,128)S(1)}, f32[3,8,128]{2,1,0:T(8,128)S(1)}, f32[4,6,8,128]{3,2,1,0:T(8,128)S(1)}) custom-call(s32[64]{0:T(128)S(1)} %reshape_squeeze.3.spans_ref, s32[2]{0:T(128)S(1)} %pad_add_fusion.where_ref, f32[19,128,128]{2,1,0:T(8,128)S(1)} %get-tuple-element.22.post_ref, ...), custom_call_target="tpu_custom_call" | custom-call | tf_op jit(solution)/shard_map/pallas_call | solution.py:484
  44.2 0.1 collective-permute-start.7
  44.3 0.5 collective-permute-start.6
  44.8 0.9 %collective-permute-done.7.right_ref = f32[3,8,128]{2,1,0:T(8,128)S(1)} collective-permute-done((f32[3,8,128]{2,1,0:T(8,128)S(1)}, f32[3,8,128]{2,1,0:T(8,128)S(1)}, u32[]{:S(2)}, u32[]{:S(2)}) %collective-permute-start.7) | collective-permute-done | bytes 12320 | tf_op jit(solution)/shard_map/ppermute | solution.py:496
  45.7 1.8 %collective-permute-done.6.left_ref = f32[3,8,128]{2,1,0:T(8,128)S(1)} collective-permute-done((f32[3,8,128]{2,1,0:T(8,128)S(1)}, f32[3,8,128]{2,1,0:T(8,128)S(1)}, u32[]{:S(2)}, u32[]{:S(2)}) %collective-permute-start.6) | collective-permute-done | bytes 12320 | tf_op jit(solution)/shard_map/ppermute | solution.py:496
  47.5 0.6 shard_map.63
  48.0 0.7 %collective-permute-start.8 = (f32[5,40,128]{2,1,0:T(8,128)S(1)}, f32[5,40,128]{2,1,0:T(8,128)S(1)}, u32[]{:S(2)}, u32[]{:S(2)}) collective-permute-start(f32[5,40,128]{2,1,0:T(8,128)S(1)} %get-tuple-element.33), channel_id=1, source_target_pairs={{0,4},{4,8},{8,12},{12,16},{16,20},{20,24},{24,28},{28,0},{1,5},{5... | collective-permute-start | bytes 307208 | tf_op jit(solution)/shard_map/ppermute | solution.py:496
  48.7 4.1 %collective-permute-start.9 = (f32[5,40,128]{2,1,0:T(8,128)S(1)}, f32[5,40,128]{2,1,0:T(8,128)S(1)}, u32[]{:S(2)}, u32[]{:S(2)}) collective-permute-start(f32[5,40,128]{2,1,0:T(8,128)S(1)} %get-tuple-element.34), channel_id=1, source_target_pairs={{0,28},{4,0},{8,4},{12,8},{16,12},{20,16},{24,20},{28,24},{1,29},{... | collective-permute-start | bytes 307208 | tf_op jit(solution)/shard_map/ppermute | solution.py:496
  52.8 6.7 %all_to_all.5 = f32[4,6,8,128]{3,2,1,0:T(8,128)S(1)} all-to-all(f32[4,6,8,128]{3,2,1,0:T(8,128)S(1)} %get-tuple-element.35), channel_id=1, replica_groups=mesh['gx'=8,'gy'=4] {'gy'}, dimensions={0} | all-to-all | bytes 196608 | tf_op jit(solution)/shard_map/all_to_all | solution.py:560
  59.5 0.6 %copy.17 = f32[2,3,1024]{2,0,1:T(2,128)} copy(f32[2,3,1024]{2,1,0:T(4,128)S(1)} %reshape.27) | data formatting | bytes 49152
  60.1 0.0 collective-permute-done.8.east_ref
  60.2 1.8 %shard_map.64 = f32[19,128,128]{2,1,0:T(8,128)} custom-call(f32[19,128,128]{2,1,0:T(8,128)S(1)} %get-tuple-element.31.post_ref, f32[19,8,128]{2,1,0:T(8,128)S(1)} %get-tuple-element.32.post_edge_ref, f32[5,40,128]{2,1,0:T(8,128)S(1)} %collective-permute-done.8.east_ref, f32[5,40,128]{2,1,0:T(8,128)S(1)} %collective-permute-done.9.west_ref), custom_call_target="tpu_custom_call" | custom-call | tf_op jit(solution)/shard_map/pallas_call | solution.py:484
  (17 shorter events, 0.1 us)
Async XLA Ops:
  0.6 4.7 %copy-start.4 = (s32[2,32,1]{1,2,0:T(1,128)S(1)}, s32[2,32,1]{1,2,0:T(1,128)}, u32[]{:S(2)}) copy-start(s32[2,32,1]{1,2,0:T(1,128)} %param.6) | copy-start | bytes 772
  0.6 11.0 %copy-start.2 = (s32[2]{0:T(128)S(1)}, s32[2]{0:T(128)}, u32[]{:S(2)}) copy-start(s32[2]{0:T(128)} %stiff_ref.1) | copy-start | bytes 28
  0.7 1.3 %copy-start = (f32[19,16,4,256]{3,2,1,0:T(4,128)S(1)}, f32[19,16,4,256]{3,2,1,0:T(4,128)}, u32[]{:S(2)}) copy-start(f32[19,16,4,256]{3,2,1,0:T(4,128)} %param.4) | copy-start | bytes 3735556
  2.0 4.1 %copy-start.3 = (f32[2,3,1024]{2,0,1:T(2,128)S(1)}, f32[2,3,1024]{2,0,1:T(2,128)}, u32[]{:S(2)}) copy-start(f32[2,3,1024]{2,0,1:T(2,128)} %param.5) | copy-start | bytes 73732
  2.0 9.7 %copy-start.1 = (f32[19,16,4,256]{3,2,1,0:T(4,128)S(1)}, f32[19,16,4,256]{3,2,1,0:T(4,128)}, u32[]{:S(2)}) copy-start(f32[19,16,4,256]{3,2,1,0:T(4,128)} %param.4) | copy-start | bytes 3735556
  2.3 9.2 %collective-permute-start.1 = (f32[19,8,128]{2,1,0:T(8,128)S(1)}, f32[19,8,128]{2,1,0:T(8,128)S(1)}, u32[]{:S(2)}, u32[]{:S(2)}) collective-permute-start(f32[19,8,128]{2,1,0:T(8,128)S(1)} %shard_map.59.edge_ref), channel_id=1, source_target_pairs={{0,3},{1,0},{2,1},{3,2},{4,7},{5,4},{6,5},{7,6},{8,11},{9,8},{10,9... | collective-permute-start | bytes 233480 | tf_op jit(solution)/shard_map/ppermute | solution.py:496
  4.8 6.8 %collective-permute-start = (f32[19,8,128]{2,1,0:T(8,128)S(1)}, f32[19,8,128]{2,1,0:T(8,128)S(1)}, u32[]{:S(2)}, u32[]{:S(2)}) collective-permute-start(f32[19,8,128]{2,1,0:T(8,128)S(1)} %shard_map.59.edge_ref), channel_id=1, source_target_pairs={{0,1},{1,2},{2,3},{3,0},{4,5},{5,6},{6,7},{7,4},{8,9},{9,10},{10,1... | collective-permute-start | bytes 233480 | tf_op jit(solution)/shard_map/ppermute | solution.py:496
  21.5 2.5 %collective-permute-start.3 = (f32[3,8,128]{2,1,0:T(8,128)S(1)}, f32[3,8,128]{2,1,0:T(8,128)S(1)}, u32[]{:S(2)}, u32[]{:S(2)}) collective-permute-start(f32[3,8,128]{2,1,0:T(8,128)S(1)} %get-tuple-element.21.force_edge_ref), channel_id=1, source_target_pairs={{0,3},{1,0},{2,1},{3,2},{4,7},{5,4},{6,5},{7,6},{8,11},{9,8},{10,9... | collective-permute-start | bytes 36872 | tf_op jit(solution)/shard_map/ppermute | solution.py:496
  22.6 3.1 %collective-permute-start.2 = (f32[3,8,128]{2,1,0:T(8,128)S(1)}, f32[3,8,128]{2,1,0:T(8,128)S(1)}, u32[]{:S(2)}, u32[]{:S(2)}) collective-permute-start(f32[3,8,128]{2,1,0:T(8,128)S(1)} %get-tuple-element.21.force_edge_ref), channel_id=1, source_target_pairs={{0,1},{1,2},{2,3},{3,0},{4,5},{5,6},{6,7},{7,4},{8,9},{9,10},{10,1... | collective-permute-start | bytes 36872 | tf_op jit(solution)/shard_map/ppermute | solution.py:496
  26.3 7.5 %collective-permute-start.4 = (f32[5,40,128]{2,1,0:T(8,128)S(1)}, f32[5,40,128]{2,1,0:T(8,128)S(1)}, u32[]{:S(2)}, u32[]{:S(2)}) collective-permute-start(f32[5,40,128]{2,1,0:T(8,128)S(1)} %get-tuple-element.24), channel_id=1, source_target_pairs={{0,4},{4,8},{8,12},{12,16},{16,20},{20,24},{24,28},{28,0},{1,5},{5... | collective-permute-start | bytes 307208 | tf_op jit(solution)/shard_map/ppermute | solution.py:496
  27.9 6.4 %collective-permute-start.5 = (f32[5,40,128]{2,1,0:T(8,128)S(1)}, f32[5,40,128]{2,1,0:T(8,128)S(1)}, u32[]{:S(2)}, u32[]{:S(2)}) collective-permute-start(f32[5,40,128]{2,1,0:T(8,128)S(1)} %get-tuple-element.25), channel_id=1, source_target_pairs={{0,28},{4,0},{8,4},{12,8},{16,12},{20,16},{24,20},{28,24},{1,29},{... | collective-permute-start | bytes 307208 | tf_op jit(solution)/shard_map/ppermute | solution.py:496
  44.2 1.5 %collective-permute-start.7 = (f32[3,8,128]{2,1,0:T(8,128)S(1)}, f32[3,8,128]{2,1,0:T(8,128)S(1)}, u32[]{:S(2)}, u32[]{:S(2)}) collective-permute-start(f32[3,8,128]{2,1,0:T(8,128)S(1)} %get-tuple-element.30.force_edge_ref), channel_id=1, source_target_pairs={{0,3},{1,0},{2,1},{3,2},{4,7},{5,4},{6,5},{7,6},{8,11},{9,8},{10,9... | collective-permute-start | bytes 36872 | tf_op jit(solution)/shard_map/ppermute | solution.py:496
  44.3 3.2 %collective-permute-start.6 = (f32[3,8,128]{2,1,0:T(8,128)S(1)}, f32[3,8,128]{2,1,0:T(8,128)S(1)}, u32[]{:S(2)}, u32[]{:S(2)}) collective-permute-start(f32[3,8,128]{2,1,0:T(8,128)S(1)} %get-tuple-element.30.force_edge_ref), channel_id=1, source_target_pairs={{0,1},{1,2},{2,3},{3,0},{4,5},{5,6},{6,7},{7,4},{8,9},{9,10},{10,1... | collective-permute-start | bytes 36872 | tf_op jit(solution)/shard_map/ppermute | solution.py:496
  48.0 12.1 %collective-permute-start.8 = (f32[5,40,128]{2,1,0:T(8,128)S(1)}, f32[5,40,128]{2,1,0:T(8,128)S(1)}, u32[]{:S(2)}, u32[]{:S(2)}) collective-permute-start(f32[5,40,128]{2,1,0:T(8,128)S(1)} %get-tuple-element.33), channel_id=1, source_target_pairs={{0,4},{4,8},{8,12},{12,16},{16,20},{20,24},{24,28},{28,0},{1,5},{5... | collective-permute-start | bytes 307208 | tf_op jit(solution)/shard_map/ppermute | solution.py:496
  48.7 11.4 %collective-permute-start.9 = (f32[5,40,128]{2,1,0:T(8,128)S(1)}, f32[5,40,128]{2,1,0:T(8,128)S(1)}, u32[]{:S(2)}, u32[]{:S(2)}) collective-permute-start(f32[5,40,128]{2,1,0:T(8,128)S(1)} %get-tuple-element.34), channel_id=1, source_target_pairs={{0,28},{4,0},{8,4},{12,8},{16,12},{20,16},{24,20},{28,24},{1,29},{... | collective-permute-start | bytes 307208 | tf_op jit(solution)/shard_map/ppermute | solution.py:496

commit v2 on v1

--- a/solution.py
+++ b/solution.py
@@ -36,6 +36,8 @@
 feedback_gain = 2.0
 EAST = tuple(i for i in range(19) if velocity_set[i][0] == 1)
 WEST = tuple(i for i in range(19) if velocity_set[i][0] == -1)
+STILL = tuple(i for i in range(19) if velocity_set[i][0] == 0)
+MOVING = EAST + WEST
 
 DEPTH = 16
 ROWS = DEPTH * 8
@@ -112,6 +114,10 @@
 def edge_kernel(pop_ref, edge_ref):
     for entry in range(19):
         edge_ref[entry] = pack_edges(lambda z: pop_ref[entry, 8 * z : 8 * z + 8, :])
+
+
+def flow_kernel(pop_ref, flow_ref):
+    flow_slices(lambda z: [pop_ref[e, 8 * z : 8 * z + 8, :] for e in range(19)], flow_ref)
 
 
 def shifted(tiles, shift):
@@ -170,7 +176,7 @@
     column = lax.broadcasted_iota(jnp.int32, (256, BLOCK), 0).astype(jnp.float32)
     z_cell = lax.broadcasted_iota(jnp.int32, (DEPTH, BLOCK), 0).astype(jnp.float32)
 
-    def body(step, carry):
+    def body(step):
         first = step * GROUP
         hot, weight_z, coef = [], [], []
         for g in range(GROUP):
@@ -233,9 +239,9 @@
             (((1,), (1,)), ((), ())),
             preferred_element_type=jnp.float32,
         )
-        return carry
-
-    lax.fori_loop(0, slots // GROUP, body, 0)
+
+    for step in range(slots // GROUP):
+        body(step)
 
 
 def finish_force(total_ref, halo_ref, force_ref, force_edge_ref):
@@ -261,7 +267,7 @@
             force_ref[c, pl.ds(4 + x, DEPTH, stride=8), :] = high
             halo_ref[c, pl.ds(4 + x, DEPTH, stride=8), :] = jnp.where(lane >= 64, left, low)
             halo_ref[c, pl.ds(x, DEPTH, stride=8), :] = jnp.where(lane >= 64, high, right)
-        force_edge_ref[c] = pack_edges(lambda z: halo_ref[c, 8 * z : 8 * z + 8, :])
+        force_edge_ref[8 * c : 8 * c + 8, :] = pack_edges(lambda z: halo_ref[c, 8 * z : 8 * z + 8, :])
 
 
 def flow_slices(load, flow_ref):
@@ -281,20 +287,28 @@
             halo_ref[c, 8 * z : 8 * z + 8, :] = turn(flow, -(5 * z + 2), 1)
 
 
-def gather_markers(span_y, slots, spans_ref, where_ref, stiff_ref, fraction_ref, span_ref, places_ref, picked_ref, table_ref):
-    filaments = fraction_ref.shape[0] // 3
-    blocks = fraction_ref.shape[1]
+def gather_markers(span_y, slots, filaments, spans_ref, where_ref, stiff_ref, part_refs, places_ref, picked_ref, table_ref):
+    columns = len(part_refs)
+    share = part_refs[0].shape[0] // (3 * filaments)
+    blocks = share * columns
     block, lane = iotas((blocks, BLOCK))
     anchor = (where_ref[0] * 4).astype(jnp.float32)
     mine = where_ref[1]
     tile_start = (mine * 256).astype(jnp.float32)
+    for s in range(columns):
+        source = lax.rem(mine + (columns - s), columns)
+        for f in range(filaments):
+            for k in range(share):
+                index = f * blocks + source * share + k
+                span = (spans_ref[index] * 256).astype(jnp.float32)
+                row = lambda c: part_refs[s][(c * share + k) * filaments + f][None, :]
+                start = pl.multiple_of(index * 8, 8)
+                three = [anchor + 1.0 + row(0) * (4 - 3.01), span + row(1) * 256.0, 1.0 + row(2) * (DEPTH - 3.01)]
+                places_ref[pl.ds(start, 8), :] = jnp.concatenate(three + [jnp.zeros((5, BLOCK), jnp.float32)], axis=0)
     for f in range(filaments):
-        places = [
-            anchor + 1.0 + fraction_ref[3 * f] * (4 - 3.01),
-            span_ref[f] + fraction_ref[3 * f + 1] * 256.0,
-            1.0 + fraction_ref[3 * f + 2] * (DEPTH - 3.01),
-        ]
         factor = stiff_ref[f].astype(jnp.float32) * (1.0 / 256.0)
+        start = f * blocks * 8
+        places = [places_ref[pl.ds(start + c, blocks, stride=8), :] for c in range(3)]
         for c in range(3):
             ahead = turn(places[c], -1, 1)
             ahead = jnp.where(lane == BLOCK - 1, turn(ahead, -1, 0), ahead) - places[c]
@@ -304,11 +318,9 @@
             ahead = jnp.where((lane == BLOCK - 1) & (block == blocks - 1), 0.0, ahead)
             behind = turn(ahead, 1, 1)
             behind = jnp.where(lane == 0, turn(behind, 1, 0), behind)
-            start = f * blocks * 8
             places_ref[pl.ds(start + 3 + c, blocks, stride=8), :] = (ahead - behind) * factor
         places_ref[pl.ds(start, blocks, stride=8), :] = places[0] - anchor
         places_ref[pl.ds(start + 1, blocks, stride=8), :] = places[1] - tile_start
-        places_ref[pl.ds(start + 2, blocks, stride=8), :] = places[2]
     picked_ref[...] = jnp.zeros_like(picked_ref)
 
     def pick(index, count):
@@ -317,7 +329,7 @@
         picked_ref[pl.ds(target, 8), :] = places_ref[pl.ds(source, 8), :]
         return count + (spans_ref[index] == mine).astype(jnp.int32)
 
-    count = lax.fori_loop(0, filaments * blocks, pick, jnp.int32(0))
+    count = lax.fori_loop(0, filaments * blocks, pick, jnp.int32(0), unroll=8)
     got = lambda k: picked_ref[pl.ds(k, slots, stride=8), :]
     slot, _ = iotas((slots, BLOCK))
 
@@ -347,13 +359,13 @@
     put(11, jnp.where(slot < count, 1.0, 0.0))
 
 
-def first_kernel(
-    span_y, slots, spans_ref, where_ref, stiff_ref,
-    pop_ref, edge_ref, left_ref, right_ref, fraction_ref, span_ref,
-    force_ref, force_edge_ref, edges_ref, table_ref,
-    flow_ref, halo_ref, matrix_ref, total_ref, speed_ref, places_ref, picked_ref,
-):
-    gather_markers(span_y, slots, spans_ref, where_ref, stiff_ref, fraction_ref, span_ref, places_ref, picked_ref, table_ref)
+def first_kernel(span_y, slots, filaments, columns, spans_ref, where_ref, stiff_ref, flow_ref, edge_ref, left_ref, right_ref, *refs):
+    part_refs, refs = refs[:columns], refs[columns:]
+    force_ref, force_edge_ref, edges_ref, table_ref = refs[:4]
+    halo_ref, matrix_ref, total_ref, speed_ref, places_ref, picked_ref = refs[4:]
+    gather_markers(
+        span_y, slots, filaments, spans_ref, where_ref, stiff_ref, part_refs, places_ref, picked_ref, table_ref
+    )
     row, lane = iotas()
     j = lane % 5
     from_left = (row >= 4) & (j < 2)
@@ -364,24 +376,33 @@
         value = jnp.where(from_left, left_ref[entry], jnp.where(from_right, right_ref[entry], own))
         edges_ref[entry] = value
         edges.append(value)
-    flow_slices(lambda z: [pop_ref[e, 8 * z : 8 * z + 8, :] for e in range(19)], flow_ref)
     flow_edges(edges, halo_ref)
     prepare_matrix(flow_ref, halo_ref, matrix_ref)
     couple(slots, table_ref, matrix_ref, total_ref, speed_ref)
     finish_force(total_ref, halo_ref, force_ref, force_edge_ref)
 
 
-def collide_kernel(pop_ref, edges_ref, force_ref, force_edge_ref, left_ref, right_ref, post_ref, post_edge_ref, east_ref, west_ref):
+def collide_kernel(split, *refs):
+    dev_refs, refs = refs[: split + 1], refs[split + 1 :]
+    edges_ref, force_ref, force_edge_ref, left_ref, right_ref, post_ref, post_edge_ref, east_ref, west_ref = refs
+
+    def dev(e, part):
+        if not split:
+            return dev_refs[0][e, part, :]
+        return dev_refs[0][STILL.index(e), part, :] if e in STILL else dev_refs[1][MOVING.index(e), part, :]
+
     row, lane = iotas()
     force_edge = [
-        force_edge_ref[c] + jnp.where(row >= 4, turn(left_ref[c], 4, 0), turn(right_ref[c], 4, 0)) for c in range(3)
+        force_edge_ref[8 * c : 8 * c + 8, :]
+        + jnp.where(row >= 4, turn(left_ref[8 * c : 8 * c + 8, :], 4, 0), turn(right_ref[8 * c : 8 * c + 8, :], 4, 0))
+        for c in range(3)
     ]
     swapped = [turn(value, 4, 0) for value in force_edge]
     patch = ((row < 4) & (lane < 3)) | ((row >= 4) & (lane >= 126))
     for z in range(DEPTH):
         part = slice(8 * z, 8 * z + 8)
         force = [jnp.where(patch, turn(swapped[c], -(5 * z + 2), 1), force_ref[c, part, :]) for c in range(3)]
-        post = collide([pop_ref[e, part, :] for e in range(19)], force)
+        post = collide([dev(e, part) for e in range(19)], force)
         for e in range(19):
             post_ref[e, part, :] = post[e]
     post = collide([edges_ref[e] for e in range(19)], force_edge)
@@ -394,11 +415,11 @@
         west_ref[k, 32:40, :] = post[WEST[k]]
 
 
-def stream(post_ref, post_edge_ref, east_ref, west_ref, moved_ref, store, store_edge):
+def stream(entries, post_ref, post_edge_ref, east_ref, west_ref, moved_ref, store, store_edge):
     row, lane = iotas()
     patches = {1: (row < 4) & (lane == 0), -1: (row >= 4) & (lane == 127)}
     low_wall, high_wall = lane < 5, lane >= 75
-    for e in range(19):
+    for e in entries:
         cx, cy, cz = velocity_set[e]
         edge = post_edge_ref[e]
         if cx == 1:
@@ -435,59 +456,108 @@
             store(e, z, value)
 
 
+def still_kernel(post_ref, post_edge_ref, dev_ref, edges_ref):
+    def store(e, z, value):
+        dev_ref[STILL.index(e), 8 * z : 8 * z + 8, :] = value
+
+    def store_edge(e, value):
+        edges_ref[STILL.index(e)] = value
+
+    stream(STILL, post_ref, post_edge_ref, None, None, None, store, store_edge)
+
+
 def second_kernel(
-    slots, blocks, shares, spans_ref, where_ref,
-    post_ref, post_edge_ref, east_ref, west_ref, table_ref,
-    dev_ref, edges_ref, force_ref, force_edge_ref, speeds_ref,
-    moved_ref, flow_ref, halo_ref, matrix_ref, total_ref, speed_ref, spot_ref,
+    slots, blocks, columns, spans_ref, where_ref,
+    post_ref, post_edge_ref, still_ref, still_edge_ref, east_ref, west_ref, table_ref, *refs
 ):
+    dev_ref, edges_ref, force_ref, to_right_ref, to_left_ref = refs[:5]
+    share_refs, refs = refs[5 : 3 + columns], refs[3 + columns :]
+    moved_ref, flow_ref, halo_ref, matrix_ref, total_ref, speed_ref, spot_ref = refs
+
     def store(e, z, value):
-        dev_ref[e, 8 * z : 8 * z + 8, :] = value
+        dev_ref[MOVING.index(e), 8 * z : 8 * z + 8, :] = value
 
     def store_edge(e, value):
         edges_ref[e] = value
 
-    stream(post_ref, post_edge_ref, east_ref, west_ref, moved_ref, store, store_edge)
-    flow_slices(lambda z: [dev_ref[e, 8 * z : 8 * z + 8, :] for e in range(19)], flow_ref)
+    def dev(e, z):
+        part = slice(8 * z, 8 * z + 8)
+        return still_ref[STILL.index(e), part, :] if e in STILL else dev_ref[MOVING.index(e), part, :]
+
+    stream(MOVING, post_ref, post_edge_ref, east_ref, west_ref, moved_ref, store, store_edge)
+    for k, e in enumerate(STILL):
+        edges_ref[e] = still_edge_ref[k]
+    flow_slices(lambda z: [dev(e, z) for e in range(19)], flow_ref)
     flow_edges([edges_ref[e] for e in range(19)], halo_ref)
     prepare_matrix(flow_ref, halo_ref, matrix_ref)
     speed_ref[...] = jnp.zeros_like(speed_ref)
     couple(slots, table_ref, matrix_ref, total_ref, speed_ref)
-    finish_force(total_ref, halo_ref, force_ref, force_edge_ref)
+    finish_force(total_ref, halo_ref, force_ref, to_right_ref)
+    to_left_ref[0:24, :] = to_right_ref[0:24, :]
     mine = where_ref[1]
 
     def place(index, count):
         here = spans_ref[index] == mine
-        value = speed_ref[jnp.minimum(count, slots - 1)]
-        spot_ref[pl.ds(pl.multiple_of(index * 8, 8), 8), :] = jnp.where(here, value, 0.0)
+        spot_ref[index] = jnp.where(here, speed_ref[jnp.minimum(count, slots - 1)], 0.0)
         return count + here.astype(jnp.int32)
 
-    lax.fori_loop(0, spans_ref.shape[0], place, jnp.int32(0))
-    filaments = spans_ref.shape[0] // blocks
-    share = blocks // shares
-    for s in range(shares):
+    total = spans_ref.shape[0]
+    lax.fori_loop(0, total, place, jnp.int32(0), unroll=8)
+    filaments = total // blocks
+    share = blocks // columns
+    others = iter(share_refs)
+    for s in range(columns):
+        target, start = (to_right_ref, 24) if s == 1 else (to_left_ref, 24) if s == columns - 1 else (next(others), 0)
+        owner = lax.rem(mine + s, columns)
         for f in range(filaments):
-            for c in range(3):
-                speeds_ref[s, 3 * f + c] = spot_ref[pl.ds((f * blocks + s * share) * 8 + c, share, stride=8), :]
-
-
-def last_kernel(post_ref, post_edge_ref, east_ref, west_ref, dev_ref, moved_ref):
+            for k in range(share):
+                for c in range(3):
+                    row = start + (c * share + k) * filaments + f
+                    target[row : row + 1, :] = spot_ref[f * blocks + owner * share + k, c : c + 1, :]
+
+
+def last_still_kernel(post_ref, post_edge_ref, dev_ref, kept_ref, sems):
     def store(e, z, value):
-        dev_ref[e, 8 * z : 8 * z + 8, :] = value
-
-    stream(post_ref, post_edge_ref, east_ref, west_ref, moved_ref, store, lambda e, value: None)
-
-
-def call(body, outs, scratch, n_smem, args):
+        kept_ref[STILL.index(e), 8 * z : 8 * z + 8, :] = value
+
+    copies = []
+    for k, e in enumerate(STILL):
+        stream((e,), post_ref, post_edge_ref, None, None, None, store, lambda e, value: None)
+        copies.append(pltpu.make_async_copy(kept_ref.at[k], dev_ref.at[e], sems.at[k]))
+        copies[-1].start()
+    for copy in copies:
+        copy.wait()
+
+
+def last_kernel(post_ref, post_edge_ref, east_ref, west_ref, old_ref, dev_ref, moved_ref, kept_ref, sems):
+    def store(e, z, value):
+        kept_ref[MOVING.index(e), 8 * z : 8 * z + 8, :] = value
+
+    copies = []
+    for k, e in enumerate(MOVING):
+        stream((e,), post_ref, post_edge_ref, east_ref, west_ref, moved_ref, store, lambda e, value: None)
+        copies.append(pltpu.make_async_copy(kept_ref.at[k], dev_ref.at[e], sems.at[k]))
+        copies[-1].start()
+    for copy in copies:
+        copy.wait()
+
+
+def call(body, outs, scratch, n_smem, args, flops=0, **extra):
     spec = [pl.BlockSpec(memory_space=pltpu.SMEM)] * n_smem
     spec += [pl.BlockSpec(memory_space=pltpu.VMEM)] * (len(args) - n_smem)
+    moved = 4 * sum(math.prod(shape) for shape in outs)
+    options = dict(
+        in_specs=spec,
+        out_specs=[pl.BlockSpec(memory_space=pltpu.VMEM)] * len(outs),
+        cost_estimate=pl.CostEstimate(flops=flops, bytes_accessed=2 * moved, transcendentals=0),
+    )
+    options.update(extra)
     return pl.pallas_call(
         body,
         out_shape=[jax.ShapeDtypeStruct(shape, jnp.float32) for shape in outs],
-        in_specs=spec,
-        out_specs=[pl.BlockSpec(memory_space=pltpu.VMEM)] * len(outs),
         scratch_shapes=scratch,
         compiler_params=pltpu.CompilerParams(vmem_limit_bytes=VMEM_LIMIT),
+        **options,
     )(*args)
 
 
@@ -500,67 +570,86 @@
     depth, tile_x, tile_y = populations.shape[1:]
     columns = lax.axis_size("gy")
     span_y = float(tile_y * columns)
-    my_row, my_column = lax.axis_index("gx"), lax.axis_index("gy")
     filaments, _, share = fraction.shape
     blocks = spans.shape[1]
     share_blocks = share // BLOCK
     slots = max(GROUP, 2 * filaments * blocks // columns)
     f32 = jnp.float32
 
+    own_part = fraction.reshape(filaments, 3, share_blocks, BLOCK).transpose(1, 2, 0, 3)
+    own_part = own_part.reshape(3 * share_blocks * filaments, BLOCK)
+    parts = [own_part] + [ring(own_part, "gy", s) for s in range(1, columns)]
+
     field = (19, ROWS, 128)
     edge = (19, 8, 128)
     halves = tile_y // 128
     pop = populations.reshape(19, depth, tile_x, halves, 128).transpose(0, 1, 3, 2, 4).reshape(field)
-    rows = lax.all_gather(fraction.reshape(filaments * 3, share_blocks, BLOCK), "gy", axis=0)
-    rows = rows.transpose(1, 0, 2, 3).reshape(filaments * 3, blocks, BLOCK)
-    flat_spans = spans[:, :, 0].reshape(-1)
-    span_rows = jnp.broadcast_to((spans * tile_y).astype(f32), (filaments, blocks, BLOCK))
-    where = jnp.stack([my_row, my_column]).astype(jnp.int32)
+    flat_spans = spans.reshape(-1)
+    where = jnp.stack([lax.axis_index("gx"), lax.axis_index("gy")]).astype(jnp.int32)
 
     (own_edge,) = call(edge_kernel, [edge], [], 0, (pop,))
     left, right = ring(own_edge, "gy", 1), ring(own_edge, "gy", -1)
-
-    force_shape, force_edge_shape = (3, ROWS, 128), (3, 8, 128)
+    force_shape = (3, ROWS, 128)
+    (flow,) = call(flow_kernel, [force_shape], [], 0, (pop,))
+
     table_shape = (slots, 16, BLOCK)
     coupling = [
-        pltpu.VMEM(force_shape, f32),
         pltpu.VMEM(force_shape, f32),
         pltpu.VMEM((3 * FIELDS * DEPTH, 512), jnp.bfloat16),
         pltpu.VMEM((3 * FIELDS * DEPTH, 256), f32),
         pltpu.VMEM((slots, 8, BLOCK), f32),
     ]
     force, force_edge, edges, table = call(
-        functools.partial(first_kernel, span_y, slots),
-        [force_shape, force_edge_shape, edge, table_shape],
+        functools.partial(first_kernel, span_y, slots, filaments, columns),
+        [force_shape, (24, 128), edge, table_shape],
         coupling + [pltpu.VMEM((filaments * blocks * 8, BLOCK), f32), pltpu.VMEM(((slots + 1) * 8, BLOCK), f32)],
         3,
-        (flat_spans, where, stiffness, pop, own_edge, left, right, rows, span_rows),
+        (flat_spans, where, stiffness, flow, own_edge, left, right, *parts),
     )
 
     plane = (5, 40, 128)
     moved = pltpu.VMEM((5, ROWS, 128), f32)
 
-    def collision(dev, edges, force, force_edge):
-        left, right = ring(force_edge, "gy", 1), ring(force_edge, "gy", -1)
+    def collision(dev, edges, force, force_edge, left, right):
         post, post_edge, east, west = call(
-            collide_kernel, [field, edge, plane, plane], [], 0, (dev, edges, force, force_edge, left, right)
+            functools.partial(collide_kernel, len(dev) - 1),
+            [field, edge, plane, plane], [], 0, (*dev, edges, force, force_edge, left, right),
         )
         return post, post_edge, ring(east, "gx", 1), ring(west, "gx", -1)
 
-    post = collision(pop, edges, force, force_edge)
-    speeds_shape = (columns, filaments * 3, share_blocks, BLOCK)
-    dev, edges, force, force_edge, speeds = call(
+    left, right = ring(force_edge, "gy", 1), ring(force_edge, "gy", -1)
+    post, post_edge, east, west = collision((pop,), edges, force, force_edge, left, right)
+    still, still_edge = call(still_kernel, [(9, ROWS, 128), (9, 8, 128)], [], 0, (post, post_edge))
+    share_rows = 3 * share_blocks * filaments
+    dev, edges, force, to_right, to_left, *chunks = call(
         functools.partial(second_kernel, slots, blocks, columns),
-        [field, edge, force_shape, force_edge_shape, speeds_shape],
-        [moved] + coupling + [pltpu.VMEM((filaments * blocks * 8, BLOCK), f32)],
+        [(10, ROWS, 128), edge, force_shape] + [(24 + share_rows, BLOCK)] * 2 + [(share_rows, BLOCK)] * (columns - 2),
+        [moved, pltpu.VMEM(force_shape, f32)] + coupling + [pltpu.VMEM((filaments * blocks, 8, BLOCK), f32)],
         2,
-        (flat_spans, where) + tuple(post) + (table,),
-    )
-    post = collision(dev, edges, force, force_edge)
-    speed = jnp.sum(lax.all_to_all(speeds, "gy", 0, 0, tiled=True), axis=0)
-    (dev,) = call(last_kernel, [field], [moved], 0, tuple(post))
+        (flat_spans, where, post, post_edge, still, still_edge, east, west, table),
+    )
+    left, right = ring(to_right, "gy", 1), ring(to_left, "gy", -1)
+    post, post_edge, east, west = collision((still, dev), edges, force, to_right, left, right)
+    speed = chunks[0] + left[24:] + right[24:]
+    for s in range(2, columns - 1):
+        speed = speed + ring(chunks[s - 1], "gy", s)
+    speed = speed.reshape(3, share_blocks, filaments, BLOCK).transpose(2, 0, 1, 3).reshape(fraction.shape)
+
+    anywhere = pl.BlockSpec(memory_space=pl.ANY)
+    inside = pl.BlockSpec(memory_space=pltpu.VMEM)
+    (dev,) = call(
+        last_still_kernel, [field],
+        [pltpu.VMEM((9, ROWS, 128), f32), pltpu.SemaphoreType.DMA((9,))],
+        0, (post, post_edge), out_specs=[anywhere],
+    )
+    (dev,) = call(
+        last_kernel, [field],
+        [moved, pltpu.VMEM((10, ROWS, 128), f32), pltpu.SemaphoreType.DMA((10,))],
+        0, (post, post_edge, east, west, dev),
+        in_specs=[inside] * 4 + [anywhere], out_specs=[anywhere], input_output_aliases={4: 0},
+    )
     dev = dev.reshape(19, depth, halves, tile_x, 128).transpose(0, 1, 3, 2, 4).reshape(populations.shape)
-    return dev, speed.reshape(fraction.shape)
+    return dev, speed
 
 
 def solution(mesh):

time: 62.1 us -> 49.6 us (0.80)
  blocking collectives: 12.1 us -> 0 us
  Pallas kernels: 23 us -> 16.3 us
  waiting for transfers between devices: 9.04 us -> 12.7 us
  starting transfers between devices: 13.7 us -> 16.3 us
  local copies, waits for them, and re-layouts: 2.66 us -> 1.91 us
    pallas_call x6 -> x9, Pallas kernels: 23 us -> 16.3 us  [call(): pl.pallas_call(body, out_shape=[jax.ShapeDtypeStruct(shape, jnp.float32)...]
    all_to_all x1 -> x0, blocking collectives: 6.66 us -> none  [per_device(): speed = jnp.sum(lax.all_to_all(speeds, 'gy', 0, 0, tiled=True), axis=0)]
    all_gather x1 -> x0, blocking collectives: 5.42 us -> none  [per_device(): lax.all_gather(fraction.reshape(filaments * 3, share_blocks, BLOCK), 'gy'...]
    ppermute x10 -> x14, waiting for transfers between devices: 9.04 us -> 12.7 us  [ring(): lax.ppermute(value, axis, [(i, (i + step) % count) for i in range(count)])]
    ppermute x10 -> x14, starting transfers between devices: 13.7 us -> 16.3 us  [ring(): lax.ppermute(value, axis, [(i, (i + step) % count) for i in range(count)])]
    convert_element_type x1 -> x0, other arithmetic: 0.66 us -> none  [per_device(): (spans * tile_y).astype(f32)]
    unnamed x0 -> x1, other arithmetic: none -> 0.66 us
    unnamed x13 -> x11, local copies, waits for them, and re-layouts: 2.47 us -> 1.82 us
  transfers between devices with their start and end apart: 10 -> 14, of which waited for: 6 -> 10; matrix products, arithmetic and copies ran while one was open for 3% -> 4% of each run, Pallas kernels for 0% -> 5%
where the time goes in v2:
time: 49.6 us; the launch traced here: 49.4 us
  starting transfers between devices  16.3 us (33%)
  Pallas kernels  16.3 us (33%)
  waiting for transfers between devices  12.7 us (26%)
  local copies, waits for them, and re-layouts  1.91 us (4%)
  other arithmetic  1.36 us (3%)
  between operations  0.88 us (2%)
    ppermute x14, starting transfers between devices, ring(): lax.ppermute(value, axis, [(i, (i + step) % count) for i in range(count)])  16.3 us
    pallas_call x9, Pallas kernels, call(): pl.pallas_call(body, out_shape=[jax.ShapeDtypeStruct(shape, jnp.float32)...  16.3 us
    ppermute x14, waiting for transfers between devices, ring(): lax.ppermute(value, axis, [(i, (i + step) % count) for i in range(count)])  12.7 us
    unnamed x11, local copies, waits for them, and re-layouts  1.82 us
  transfers between devices with their start and end apart: 14, of which 10 were waited for; matrix products, arithmetic and copies ran while one was open for 4% of the time, Pallas kernels for 5%

profile of v2, /device:TPU:0, one launch (start us, length us, event | category | flops | bytes accessed | tf_op | source)
XLA Modules:
  0.0 49.4 jit_solution(15580052195451053606)
XLA Ops:
  0.6 2.4 %collective-permute-start.4 = (f32[48,128]{1,0:T(8,128)}, f32[48,128]{1,0:T(8,128)S(1)}, u32[]{:S(2)}, u32[]{:S(2)}) collective-permute-start(f32[48,128]{1,0:T(8,128)} %bitcast.26), channel_id=1, source_target_pairs={{0,3},{1,0},{2,1},{3,2},{4,7},{5,4},{6,5},{7,6},{8,11},{9,8},{10,9... | collective-permute-start | bytes 73736 | tf_op jit(solution)/shard_map/ppermute | solution.py:566
  3.1 0.6 %collective-permute-start.3 = (f32[48,128]{1,0:T(8,128)}, f32[48,128]{1,0:T(8,128)S(1)}, u32[]{:S(2)}, u32[]{:S(2)}) collective-permute-start(f32[48,128]{1,0:T(8,128)} %bitcast.27), channel_id=1, source_target_pairs={{0,2},{1,3},{2,0},{3,1},{4,6},{5,7},{6,4},{7,5},{8,10},{9,11},{10,... | collective-permute-start | bytes 73736 | tf_op jit(solution)/shard_map/ppermute | solution.py:566
  3.9 1.3 %copy-done = f32[19,16,4,256]{3,2,1,0:T(4,128)S(1)} copy-done((f32[19,16,4,256]{3,2,1,0:T(4,128)S(1)}, f32[19,16,4,256]{3,2,1,0:T(4,128)}, u32[]{:S(2)}) %copy-start) | copy-done | bytes 1245208
  5.2 0.4 shard_map.60.edge_ref
  5.6 1.6 %collective-permute-start.1 = (f32[19,8,128]{2,1,0:T(8,128)S(1)}, f32[19,8,128]{2,1,0:T(8,128)S(1)}, u32[]{:S(2)}, u32[]{:S(2)}) collective-permute-start(f32[19,8,128]{2,1,0:T(8,128)S(1)} %shard_map.60.edge_ref), channel_id=1, source_target_pairs={{0,3},{1,0},{2,1},{3,2},{4,7},{5,4},{6,5},{7,6},{8,11},{9,8},{10,9... | collective-permute-start | bytes 233480 | tf_op jit(solution)/shard_map/ppermute | solution.py:566
  7.4 0.5 %broadcast.3 = s32[]{:T(128)} broadcast(s32[]{:T(128)} %constant.20), dimensions={} | broadcast | bytes 8 | tf_op args[2]
  7.9 0.7 %reduce.3 = s32[2,32]{1,0:T(2,128)S(1)} reduce(s32[2,32,1]{1,2,0:T(1,128)S(1)} %copy-done.4, s32[]{:T(128)} %broadcast.3), dimensions={2}, to_apply=%param.6.reduce_sub_computation.3 | reduce | bytes 516 | tf_op args[2]
  8.7 0.5 %collective-permute-done.1.right_ref = f32[19,8,128]{2,1,0:T(8,128)S(1)} collective-permute-done((f32[19,8,128]{2,1,0:T(8,128)S(1)}, f32[19,8,128]{2,1,0:T(8,128)S(1)}, u32[]{:S(2)}, u32[]{:S(2)}) %collective-permute-start.1) | collective-permute-done | bytes 77856 | tf_op jit(solution)/shard_map/ppermute | solution.py:566
  9.2 2.6 %collective-permute-done.left_ref = f32[19,8,128]{2,1,0:T(8,128)S(1)} collective-permute-done((f32[19,8,128]{2,1,0:T(8,128)S(1)}, f32[19,8,128]{2,1,0:T(8,128)S(1)}, u32[]{:S(2)}, u32[]{:S(2)}) %collective-permute-start) | collective-permute-done | bytes 77856 | tf_op jit(solution)/shard_map/ppermute | solution.py:566
  11.8 5.9 %shard_map.61 = (f32[3,128,128]{2,1,0:T(8,128)S(1)}, f32[24,128]{1,0:T(8,128)S(1)}, f32[19,8,128]{2,1,0:T(8,128)S(1)}, f32[32,16,128]{2,1,0:T(8,128)S(1)}) custom-call(s32[64]{0:T(128)S(1)} %reshape.33.spans_ref, s32[2]{0:T(128)S(1)} %pad_add_fusion.where_ref, s32[2]{0:T(128)S(1)} %copy-done.3, f32[3,128,128]{2,1,0:T(8,128)S(1)} %shard_map.59.flow_ref, ...), custom_call_target="tpu_custom_call" | custom-call | bytes 1097728 | tf_op jit(solution)/shard_map/pallas_call | solution.py:555
  17.8 0.5 %collective-permute-start.5 = (f32[24,128]{1,0:T(8,128)S(1)}, f32[24,128]{1,0:T(8,128)S(1)}, u32[]{:S(2)}, u32[]{:S(2)}) collective-permute-start(f32[24,128]{1,0:T(8,128)S(1)} %get-tuple-element.25.refs_3_), channel_id=1, source_target_pairs={{0,1},{1,2},{2,3},{3,0},{4,5},{5,6},{6,7},{7,4},{8,9},{9,10},{10,1... | collective-permute-start | bytes 36872 | tf_op jit(solution)/shard_map/ppermute | solution.py:566
  18.3 0.9 %collective-permute-done.6.refs_5_ = f32[24,128]{1,0:T(8,128)S(1)} collective-permute-done((f32[24,128]{1,0:T(8,128)S(1)}, f32[24,128]{1,0:T(8,128)S(1)}, u32[]{:S(2)}, u32[]{:S(2)}) %collective-permute-start.6) | collective-permute-done | bytes 12320 | tf_op jit(solution)/shard_map/ppermute | solution.py:566
  19.2 1.8 %collective-permute-done.5.refs_4_ = f32[24,128]{1,0:T(8,128)S(1)} collective-permute-done((f32[24,128]{1,0:T(8,128)S(1)}, f32[24,128]{1,0:T(8,128)S(1)}, u32[]{:S(2)}, u32[]{:S(2)}) %collective-permute-start.5) | collective-permute-done | bytes 12320 | tf_op jit(solution)/shard_map/ppermute | solution.py:566
  21.0 0.6 %shard_map.62 = (f32[19,128,128]{2,1,0:T(8,128)S(1)}, f32[19,8,128]{2,1,0:T(8,128)S(1)}, f32[5,40,128]{2,1,0:T(8,128)S(1)}, f32[5,40,128]{2,1,0:T(8,128)S(1)}) custom-call(f32[19,128,128]{2,1,0:T(8,128)S(1)} %bitcast.25, f32[19,8,128]{2,1,0:T(8,128)S(1)} %get-tuple-element.23.refs_1_, f32[3,128,128]{2,1,0:T(8,128)S(1)} %get-tuple-element.24.refs_2_, ...), custom_call_target="tpu_custom_call" | custom-call | bytes 3055616 | tf_op jit(solution)/shard_map/pallas_call | solution.py:555
  21.5 1.6 %collective-permute-start.7 = (f32[5,40,128]{2,1,0:T(8,128)S(1)}, f32[5,40,128]{2,1,0:T(8,128)S(1)}, u32[]{:S(2)}, u32[]{:S(2)}) collective-permute-start(f32[5,40,128]{2,1,0:T(8,128)S(1)} %get-tuple-element.30), channel_id=1, source_target_pairs={{0,4},{4,8},{8,12},{12,16},{16,20},{20,24},{24,28},{28,0},{1,5},{5... | collective-permute-start | bytes 307208 | tf_op jit(solution)/shard_map/ppermute | solution.py:566
  23.1 3.3 %collective-permute-start.8 = (f32[5,40,128]{2,1,0:T(8,128)S(1)}, f32[5,40,128]{2,1,0:T(8,128)S(1)}, u32[]{:S(2)}, u32[]{:S(2)}) collective-permute-start(f32[5,40,128]{2,1,0:T(8,128)S(1)} %get-tuple-element.31), channel_id=1, source_target_pairs={{0,28},{4,0},{8,4},{12,8},{16,12},{20,16},{24,20},{28,24},{1,29},{... | collective-permute-start | bytes 307208 | tf_op jit(solution)/shard_map/ppermute | solution.py:566
  26.4 0.5 shard_map.63
  26.9 2.6 %collective-permute-done.7.east_ref = f32[5,40,128]{2,1,0:T(8,128)S(1)} collective-permute-done((f32[5,40,128]{2,1,0:T(8,128)S(1)}, f32[5,40,128]{2,1,0:T(8,128)S(1)}, u32[]{:S(2)}, u32[]{:S(2)}) %collective-permute-start.7) | collective-permute-done | bytes 102432 | tf_op jit(solution)/shard_map/ppermute | solution.py:566
  29.4 0.5 %collective-permute-done.8.west_ref = f32[5,40,128]{2,1,0:T(8,128)S(1)} collective-permute-done((f32[5,40,128]{2,1,0:T(8,128)S(1)}, f32[5,40,128]{2,1,0:T(8,128)S(1)}, u32[]{:S(2)}, u32[]{:S(2)}) %collective-permute-start.8) | collective-permute-done | bytes 102432 | tf_op jit(solution)/shard_map/ppermute | solution.py:566
  30.0 6.0 %shard_map.64 = (f32[10,128,128]{2,1,0:T(8,128)S(1)}, f32[19,8,128]{2,1,0:T(8,128)S(1)}, f32[3,128,128]{2,1,0:T(8,128)S(1)}, f32[72,128]{1,0:T(8,128)S(1)}, f32[...) custom-call(s32[64]{0:T(128)S(1)} %reshape.33.spans_ref, s32[2]{0:T(128)S(1)} %pad_add_fusion.where_ref, ...), custom_call_target="tpu_custom_call" | custom-call | bytes 2105344 | tf_op jit(solution)/shard_map/pallas_call | solution.py:555
  36.0 0.5 %collective-permute-start.9 = (f32[72,128]{1,0:T(8,128)S(1)}, f32[72,128]{1,0:T(8,128)S(1)}, u32[]{:S(2)}, u32[]{:S(2)}) collective-permute-start(f32[72,128]{1,0:T(8,128)S(1)} %get-tuple-element.36.refs_4_), channel_id=1, source_target_pairs={{0,1},{1,2},{2,3},{3,0},{4,5},{5,6},{6,7},{7,4},{8,9},{9,10},{10,1... | collective-permute-start | bytes 110600 | tf_op jit(solution)/shard_map/ppermute | solution.py:566
  36.5 0.7 %collective-permute-start.13 = (f32[48,128]{1,0:T(8,128)S(1)}, f32[48,128]{1,0:T(8,128)S(1)}, u32[]{:S(2)}, u32[]{:S(2)}) collective-permute-start(f32[48,128]{1,0:T(8,128)S(1)} %get-tuple-element.43), channel_id=1, source_target_pairs={{0,2},{1,3},{2,0},{3,1},{4,6},{5,7},{6,4},{7,5},{8,10},{9,11},{10,... | collective-permute-start | bytes 73736 | tf_op jit(solution)/shard_map/ppermute | solution.py:566
  37.2 0.5 %collective-permute-done.10.refs_6_ = f32[72,128]{1,0:T(8,128)S(1)} collective-permute-done((f32[72,128]{1,0:T(8,128)S(1)}, f32[72,128]{1,0:T(8,128)S(1)}, u32[]{:S(2)}, u32[]{:S(2)}) %collective-permute-start.10) | collective-permute-done | bytes 36896 | tf_op jit(solution)/shard_map/ppermute | solution.py:566
  37.8 1.7 %collective-permute-done.9.refs_5_ = f32[72,128]{1,0:T(8,128)S(1)} collective-permute-done((f32[72,128]{1,0:T(8,128)S(1)}, f32[72,128]{1,0:T(8,128)S(1)}, u32[]{:S(2)}, u32[]{:S(2)}) %collective-permute-start.9) | collective-permute-done | bytes 36896 | tf_op jit(solution)/shard_map/ppermute | solution.py:566
  39.5 0.6 %shard_map.65 = (f32[19,128,128]{2,1,0:T(8,128)S(1)}, f32[19,8,128]{2,1,0:T(8,128)S(1)}, f32[5,40,128]{2,1,0:T(8,128)S(1)}, f32[5,40,128]{2,1,0:T(8,128)S(1)}) custom-call(f32[9,128,128]{2,1,0:T(8,128)S(1)} %get-tuple-element.28.still_ref.refs_0_, f32[10,128,128]{2,1,0:T(8,128)S(1)} %get-tuple-element.33.refs_1_, ...), custom_call_target="tpu_custom_call" | custom-call | bytes 3055616 | tf_op jit(solution)/shard_map/pallas_call | solution.py:555
  40.1 0.6 %collective-permute-start.11 = (f32[5,40,128]{2,1,0:T(8,128)S(1)}, f32[5,40,128]{2,1,0:T(8,128)S(1)}, u32[]{:S(2)}, u32[]{:S(2)}) collective-permute-start(f32[5,40,128]{2,1,0:T(8,128)S(1)} %get-tuple-element.40), channel_id=1, source_target_pairs={{0,4},{4,8},{8,12},{12,16},{16,20},{20,24},{24,28},{28,0},{1,5},{5... | collective-permute-start | bytes 307208 | tf_op jit(solution)/shard_map/ppermute | solution.py:566
  40.7 4.2 %collective-permute-start.12 = (f32[5,40,128]{2,1,0:T(8,128)S(1)}, f32[5,40,128]{2,1,0:T(8,128)S(1)}, u32[]{:S(2)}, u32[]{:S(2)}) collective-permute-start(f32[5,40,128]{2,1,0:T(8,128)S(1)} %get-tuple-element.41), channel_id=1, source_target_pairs={{0,28},{4,0},{8,4},{12,8},{16,12},{20,16},{24,20},{28,24},{1,29},{... | collective-permute-start | bytes 307208 | tf_op jit(solution)/shard_map/ppermute | solution.py:566
  44.9 0.6 %fusion = f32[48,128]{1,0:T(8,128)} fusion(f32[48,128]{1,0:T(8,128)S(1)} %collective-permute-done.13, f32[72,128]{1,0:T(8,128)S(1)} %collective-permute-done.10.refs_6_, f32[48,128]{1,0:T(8,128)S(1)} %get-tuple-element.42, f32[72,128]{1,0:T(8,128)S(1)} %collective-permute-done.9.refs_5_), kind=kLoop, calls=%fused_computation.1 | loop fusion | flops 18432 | bytes 122880 | tf_op jit(solution)/shard_map/add | solution.py:635
  45.5 1.1 %shard_map.66.old_ref = f32[19,128,128]{2,1,0:T(8,128)} custom-call(f32[19,128,128]{2,1,0:T(8,128)S(1)} %get-tuple-element.38.post_ref, f32[19,8,128]{2,1,0:T(8,128)S(1)} %get-tuple-element.39.post_edge_ref), custom_call_target="tpu_custom_call" | custom-call | bytes 2490368 | tf_op jit(solution)/shard_map/pallas_call | solution.py:555
  46.6 1.0 %collective-permute-done.11.east_ref = f32[5,40,128]{2,1,0:T(8,128)S(1)} collective-permute-done((f32[5,40,128]{2,1,0:T(8,128)S(1)}, f32[5,40,128]{2,1,0:T(8,128)S(1)}, u32[]{:S(2)}, u32[]{:S(2)}) %collective-permute-start.11) | collective-permute-done | bytes 102432 | tf_op jit(solution)/shard_map/ppermute | solution.py:566
  47.6 0.6 %collective-permute-done.12.west_ref = f32[5,40,128]{2,1,0:T(8,128)S(1)} collective-permute-done((f32[5,40,128]{2,1,0:T(8,128)S(1)}, f32[5,40,128]{2,1,0:T(8,128)S(1)}, u32[]{:S(2)}, u32[]{:S(2)}) %collective-permute-start.12) | collective-permute-done | bytes 102432 | tf_op jit(solution)/shard_map/ppermute | solution.py:566
  48.1 1.1 %shard_map.67 = f32[19,128,128]{2,1,0:T(8,128)} custom-call(f32[19,128,128]{2,1,0:T(8,128)S(1)} %get-tuple-element.38.post_ref, f32[19,8,128]{2,1,0:T(8,128)S(1)} %get-tuple-element.39.post_edge_ref, f32[5,40,128]{2,1,0:T(8,128)S(1)} %collective-permute-done.11.east_ref, ...), custom_call_target="tpu_custom_call", output_to_operand_aliasing={{}: (4, {})} | custom-call | bytes 2490368 | tf_op jit(solution)/shard_map/pallas_call | solution.py:555
  (20 shorter events, 0.6 us)
Async XLA Ops:
  0.6 8.0 %collective-permute-start.4 = (f32[48,128]{1,0:T(8,128)}, f32[48,128]{1,0:T(8,128)S(1)}, u32[]{:S(2)}, u32[]{:S(2)}) collective-permute-start(f32[48,128]{1,0:T(8,128)} %bitcast.26), channel_id=1, source_target_pairs={{0,3},{1,0},{2,1},{3,2},{4,7},{5,4},{6,5},{7,6},{8,11},{9,8},{10,9... | collective-permute-start | bytes 73736 | tf_op jit(solution)/shard_map/ppermute | solution.py:566
  3.1 5.6 %collective-permute-start.3 = (f32[48,128]{1,0:T(8,128)}, f32[48,128]{1,0:T(8,128)S(1)}, u32[]{:S(2)}, u32[]{:S(2)}) collective-permute-start(f32[48,128]{1,0:T(8,128)} %bitcast.27), channel_id=1, source_target_pairs={{0,2},{1,3},{2,0},{3,1},{4,6},{5,7},{6,4},{7,5},{8,10},{9,11},{10,... | collective-permute-start | bytes 73736 | tf_op jit(solution)/shard_map/ppermute | solution.py:566
  3.7 5.0 %collective-permute-start.2 = (f32[48,128]{1,0:T(8,128)}, f32[48,128]{1,0:T(8,128)S(1)}, u32[]{:S(2)}, u32[]{:S(2)}) collective-permute-start(f32[48,128]{1,0:T(8,128)} %bitcast.28), channel_id=1, source_target_pairs={{0,1},{1,2},{2,3},{3,0},{4,5},{5,6},{6,7},{7,4},{8,9},{9,10},{10,1... | collective-permute-start | bytes 73736 | tf_op jit(solution)/shard_map/ppermute | solution.py:566
  3.9 1.3 %copy-start = (f32[19,16,4,256]{3,2,1,0:T(4,128)S(1)}, f32[19,16,4,256]{3,2,1,0:T(4,128)}, u32[]{:S(2)}) copy-start(f32[19,16,4,256]{3,2,1,0:T(4,128)} %param.4) | copy-start | bytes 3735556
  5.2 2.1 %copy-start.1 = (f32[19,16,4,256]{3,2,1,0:T(4,128)S(1)}, f32[19,16,4,256]{3,2,1,0:T(4,128)}, u32[]{:S(2)}) copy-start(f32[19,16,4,256]{3,2,1,0:T(4,128)} %param.4) | copy-start | bytes 3735556
  5.2 2.7 %copy-start.4 = (s32[2,32,1]{1,2,0:T(1,128)S(1)}, s32[2,32,1]{1,2,0:T(1,128)}, u32[]{:S(2)}) copy-start(s32[2,32,1]{1,2,0:T(1,128)} %param.6) | copy-start | bytes 772
  5.2 6.6 %copy-start.2 = (f32[2,3,1024]{2,0,1:T(2,128)S(1)}, f32[2,3,1024]{2,0,1:T(2,128)}, u32[]{:S(2)}) copy-start(f32[2,3,1024]{2,0,1:T(2,128)} %param.5) | copy-start | bytes 73732
  5.2 6.6 %copy-start.3 = (s32[2]{0:T(128)S(1)}, s32[2]{0:T(128)}, u32[]{:S(2)}) copy-start(s32[2]{0:T(128)} %stiff_ref.1) | copy-start | bytes 28
  5.6 3.7 %collective-permute-start.1 = (f32[19,8,128]{2,1,0:T(8,128)S(1)}, f32[19,8,128]{2,1,0:T(8,128)S(1)}, u32[]{:S(2)}, u32[]{:S(2)}) collective-permute-start(f32[19,8,128]{2,1,0:T(8,128)S(1)} %shard_map.60.edge_ref), channel_id=1, source_target_pairs={{0,3},{1,0},{2,1},{3,2},{4,7},{5,4},{6,5},{7,6},{8,11},{9,8},{10,9... | collective-permute-start | bytes 233480 | tf_op jit(solution)/shard_map/ppermute | solution.py:566
  7.2 4.6 %collective-permute-start = (f32[19,8,128]{2,1,0:T(8,128)S(1)}, f32[19,8,128]{2,1,0:T(8,128)S(1)}, u32[]{:S(2)}, u32[]{:S(2)}) collective-permute-start(f32[19,8,128]{2,1,0:T(8,128)S(1)} %shard_map.60.edge_ref), channel_id=1, source_target_pairs={{0,1},{1,2},{2,3},{3,0},{4,5},{5,6},{6,7},{7,4},{8,9},{9,10},{10,1... | collective-permute-start | bytes 233480 | tf_op jit(solution)/shard_map/ppermute | solution.py:566
  17.7 1.5 %collective-permute-start.6 = (f32[24,128]{1,0:T(8,128)S(1)}, f32[24,128]{1,0:T(8,128)S(1)}, u32[]{:S(2)}, u32[]{:S(2)}) collective-permute-start(f32[24,128]{1,0:T(8,128)S(1)} %get-tuple-element.25.refs_3_), channel_id=1, source_target_pairs={{0,3},{1,0},{2,1},{3,2},{4,7},{5,4},{6,5},{7,6},{8,11},{9,8},{10,9... | collective-permute-start | bytes 36872 | tf_op jit(solution)/shard_map/ppermute | solution.py:566
  17.8 3.2 %collective-permute-start.5 = (f32[24,128]{1,0:T(8,128)S(1)}, f32[24,128]{1,0:T(8,128)S(1)}, u32[]{:S(2)}, u32[]{:S(2)}) collective-permute-start(f32[24,128]{1,0:T(8,128)S(1)} %get-tuple-element.25.refs_3_), channel_id=1, source_target_pairs={{0,1},{1,2},{2,3},{3,0},{4,5},{5,6},{6,7},{7,4},{8,9},{9,10},{10,1... | collective-permute-start | bytes 36872 | tf_op jit(solution)/shard_map/ppermute | solution.py:566
  21.5 7.9 %collective-permute-start.7 = (f32[5,40,128]{2,1,0:T(8,128)S(1)}, f32[5,40,128]{2,1,0:T(8,128)S(1)}, u32[]{:S(2)}, u32[]{:S(2)}) collective-permute-start(f32[5,40,128]{2,1,0:T(8,128)S(1)} %get-tuple-element.30), channel_id=1, source_target_pairs={{0,4},{4,8},{8,12},{12,16},{16,20},{20,24},{24,28},{28,0},{1,5},{5... | collective-permute-start | bytes 307208 | tf_op jit(solution)/shard_map/ppermute | solution.py:566
  23.1 6.9 %collective-permute-start.8 = (f32[5,40,128]{2,1,0:T(8,128)S(1)}, f32[5,40,128]{2,1,0:T(8,128)S(1)}, u32[]{:S(2)}, u32[]{:S(2)}) collective-permute-start(f32[5,40,128]{2,1,0:T(8,128)S(1)} %get-tuple-element.31), channel_id=1, source_target_pairs={{0,28},{4,0},{8,4},{12,8},{16,12},{20,16},{24,20},{28,24},{1,29},{... | collective-permute-start | bytes 307208 | tf_op jit(solution)/shard_map/ppermute | solution.py:566
  36.0 1.8 %collective-permute-start.10 = (f32[72,128]{1,0:T(8,128)S(1)}, f32[72,128]{1,0:T(8,128)S(1)}, u32[]{:S(2)}, u32[]{:S(2)}) collective-permute-start(f32[72,128]{1,0:T(8,128)S(1)} %get-tuple-element.37), channel_id=1, source_target_pairs={{0,3},{1,0},{2,1},{3,2},{4,7},{5,4},{6,5},{7,6},{8,11},{9,8},{10,9... | collective-permute-start | bytes 110600 | tf_op jit(solution)/shard_map/ppermute | solution.py:566
  36.0 3.4 %collective-permute-start.9 = (f32[72,128]{1,0:T(8,128)S(1)}, f32[72,128]{1,0:T(8,128)S(1)}, u32[]{:S(2)}, u32[]{:S(2)}) collective-permute-start(f32[72,128]{1,0:T(8,128)S(1)} %get-tuple-element.36.refs_4_), channel_id=1, source_target_pairs={{0,1},{1,2},{2,3},{3,0},{4,5},{5,6},{6,7},{7,4},{8,9},{9,10},{10,1... | collective-permute-start | bytes 110600 | tf_op jit(solution)/shard_map/ppermute | solution.py:566
  36.5 8.3 %collective-permute-start.13 = (f32[48,128]{1,0:T(8,128)S(1)}, f32[48,128]{1,0:T(8,128)S(1)}, u32[]{:S(2)}, u32[]{:S(2)}) collective-permute-start(f32[48,128]{1,0:T(8,128)S(1)} %get-tuple-element.43), channel_id=1, source_target_pairs={{0,2},{1,3},{2,0},{3,1},{4,6},{5,7},{6,4},{7,5},{8,10},{9,11},{10,... | collective-permute-start | bytes 73736 | tf_op jit(solution)/shard_map/ppermute | solution.py:566
  40.1 7.5 %collective-permute-start.11 = (f32[5,40,128]{2,1,0:T(8,128)S(1)}, f32[5,40,128]{2,1,0:T(8,128)S(1)}, u32[]{:S(2)}, u32[]{:S(2)}) collective-permute-start(f32[5,40,128]{2,1,0:T(8,128)S(1)} %get-tuple-element.40), channel_id=1, source_target_pairs={{0,4},{4,8},{8,12},{12,16},{16,20},{20,24},{24,28},{28,0},{1,5},{5... | collective-permute-start | bytes 307208 | tf_op jit(solution)/shard_map/ppermute | solution.py:566
  40.7 7.5 %collective-permute-start.12 = (f32[5,40,128]{2,1,0:T(8,128)S(1)}, f32[5,40,128]{2,1,0:T(8,128)S(1)}, u32[]{:S(2)}, u32[]{:S(2)}) collective-permute-start(f32[5,40,128]{2,1,0:T(8,128)S(1)} %get-tuple-element.41), channel_id=1, source_target_pairs={{0,28},{4,0},{8,4},{12,8},{16,12},{20,16},{24,20},{28,24},{1,29},{... | collective-permute-start | bytes 307208 | tf_op jit(solution)/shard_map/ppermute | solution.py:566

commit v3 on v2

--- a/solution.py
+++ b/solution.py
@@ -44,6 +44,7 @@
 BLOCK = 128
 GROUP = 4
 FIELDS = 9
+EDGE_ROWS = 80
 VMEM_LIMIT = 40 * 1024 * 1024
 
 
@@ -111,13 +112,34 @@
     return post
 
 
-def edge_kernel(pop_ref, edge_ref):
-    for entry in range(19):
-        edge_ref[entry] = pack_edges(lambda z: pop_ref[entry, 8 * z : 8 * z + 8, :])
-
-
-def flow_kernel(pop_ref, flow_ref):
+def merge_edges(own, left, right):
+    row, lane = iotas()
+    j = lane % 5
+    from_left = (row >= 4) & (j < 2)
+    from_right = (row < 4) & (j >= 2)
+    return jnp.where(from_left, left, jnp.where(from_right, right, turn(own, 4, 0)))
+
+
+def flow_kernel(pop_ref, part_ref, flow_ref, payload_ref, sem):
+    rows = part_ref.shape[0]
+    copy = pltpu.make_async_copy(part_ref, payload_ref.at[pl.ds(0, rows)], sem)
+    copy.start()
     flow_slices(lambda z: [pop_ref[e, 8 * z : 8 * z + 8, :] for e in range(19)], flow_ref)
+    for c in range(3):
+        payload_ref[rows + 8 * c : rows + 8 * c + 8, :] = pack_edges(lambda z: flow_ref[c, 8 * z : 8 * z + 8, :])
+    copy.wait()
+
+
+def edge_kernel(pop_ref, edge_ref, to_right_ref, to_left_ref):
+    row, _ = iotas()
+    edges = []
+    for e in range(19):
+        edges.append(pack_edges(lambda z: pop_ref[e, 8 * z : 8 * z + 8, :]))
+        edge_ref[e] = edges[e]
+    for k in range(10):
+        other = turn(edges[2 * k + 1], 4, 0) if k < 9 else edges[2 * k]
+        to_right_ref[8 * k : 8 * k + 8, :] = jnp.where(row >= 4, edges[2 * k], other)
+        to_left_ref[8 * k : 8 * k + 8, :] = jnp.where(row < 4, edges[2 * k], other)
 
 
 def shifted(tiles, shift):
@@ -244,7 +266,7 @@
         body(step)
 
 
-def finish_force(total_ref, halo_ref, force_ref, force_edge_ref):
+def finish_force(total_ref, halo_ref, force_ref, force_edge_ref, start=0):
     lane = lax.broadcasted_iota(jnp.int32, (DEPTH, 128), 1)
     zero = jnp.zeros((DEPTH, 128), jnp.float32)
     for c in range(3):
@@ -267,7 +289,8 @@
             force_ref[c, pl.ds(4 + x, DEPTH, stride=8), :] = high
             halo_ref[c, pl.ds(4 + x, DEPTH, stride=8), :] = jnp.where(lane >= 64, left, low)
             halo_ref[c, pl.ds(x, DEPTH, stride=8), :] = jnp.where(lane >= 64, high, right)
-        force_edge_ref[8 * c : 8 * c + 8, :] = pack_edges(lambda z: halo_ref[c, 8 * z : 8 * z + 8, :])
+        row = start + 8 * c
+        force_edge_ref[row : row + 8, :] = pack_edges(lambda z: halo_ref[c, 8 * z : 8 * z + 8, :])
 
 
 def flow_slices(load, flow_ref):
@@ -278,18 +301,21 @@
             flow_ref[c, 8 * z : 8 * z + 8, :] = momentum[c] * inverse
 
 
-def flow_edges(edges, halo_ref):
+def edge_flow(edges):
     total, momentum, dens = moments(edges)
     inverse = 1.0 / dens
+    return [momentum[c] * inverse for c in range(3)]
+
+
+def flow_edges(flows, halo_ref):
     for c in range(3):
-        flow = momentum[c] * inverse
+        flow = flows[c]
         for z in range(DEPTH):
             halo_ref[c, 8 * z : 8 * z + 8, :] = turn(flow, -(5 * z + 2), 1)
 
 
-def gather_markers(span_y, slots, filaments, spans_ref, where_ref, stiff_ref, part_refs, places_ref, picked_ref, table_ref):
+def gather_markers(span_y, slots, filaments, share, spans_ref, where_ref, stiff_ref, part_refs, places_ref, picked_ref, table_ref):
     columns = len(part_refs)
-    share = part_refs[0].shape[0] // (3 * filaments)
     blocks = share * columns
     block, lane = iotas((blocks, BLOCK))
     anchor = (where_ref[0] * 4).astype(jnp.float32)
@@ -359,42 +385,54 @@
     put(11, jnp.where(slot < count, 1.0, 0.0))
 
 
-def first_kernel(span_y, slots, filaments, columns, spans_ref, where_ref, stiff_ref, flow_ref, edge_ref, left_ref, right_ref, *refs):
+def first_kernel(span_y, slots, filaments, columns, spans_ref, where_ref, stiff_ref, flow_ref, right_edge_ref, left_edge_ref, *refs):
     part_refs, refs = refs[:columns], refs[columns:]
-    force_ref, force_edge_ref, edges_ref, table_ref = refs[:4]
+    force_ref, to_right_ref, to_left_ref, table_ref = refs[:4]
     halo_ref, matrix_ref, total_ref, speed_ref, places_ref, picked_ref = refs[4:]
+    share = spans_ref.shape[0] // (filaments * columns)
+    to_right_ref[0:EDGE_ROWS, :] = right_edge_ref[...]
+    to_left_ref[0:EDGE_ROWS, :] = left_edge_ref[...]
     gather_markers(
-        span_y, slots, filaments, spans_ref, where_ref, stiff_ref, part_refs, places_ref, picked_ref, table_ref
-    )
-    row, lane = iotas()
-    j = lane % 5
-    from_left = (row >= 4) & (j < 2)
-    from_right = (row < 4) & (j >= 2)
-    edges = []
-    for entry in range(19):
-        own = turn(edge_ref[entry], 4, 0)
-        value = jnp.where(from_left, left_ref[entry], jnp.where(from_right, right_ref[entry], own))
-        edges_ref[entry] = value
-        edges.append(value)
-    flow_edges(edges, halo_ref)
+        span_y, slots, filaments, share, spans_ref, where_ref, stiff_ref, part_refs, places_ref, picked_ref, table_ref
+    )
+    flows = []
+    for c in range(3):
+        start = 3 * share * filaments + 8 * c
+        flows.append(merge_edges(*(part_refs[s][start : start + 8, :] for s in (0, 1, -1))))
+    flow_edges(flows, halo_ref)
     prepare_matrix(flow_ref, halo_ref, matrix_ref)
     couple(slots, table_ref, matrix_ref, total_ref, speed_ref)
-    finish_force(total_ref, halo_ref, force_ref, force_edge_ref)
-
-
-def collide_kernel(split, *refs):
-    dev_refs, refs = refs[: split + 1], refs[split + 1 :]
-    edges_ref, force_ref, force_edge_ref, left_ref, right_ref, post_ref, post_edge_ref, east_ref, west_ref = refs
+    finish_force(total_ref, halo_ref, force_ref, to_right_ref, EDGE_ROWS)
+    to_left_ref[EDGE_ROWS:, :] = to_right_ref[EDGE_ROWS:, :]
+
+
+def collide_kernel(first, *refs):
+    if first:
+        pop_ref, edge_ref = refs[:2]
+        force_ref, own_ref, left_ref, right_ref, post_ref, post_edge_ref, east_ref, west_ref = refs[2:]
+        start = EDGE_ROWS
+        edges = []
+        for e in range(19):
+            part, shift = slice(8 * (e // 2), 8 * (e // 2) + 8), 4 * (e % 2)
+            edges.append(merge_edges(edge_ref[e], turn(left_ref[part, :], shift, 0), turn(right_ref[part, :], shift, 0)))
+    else:
+        still_ref, moving_ref, edges_ref = refs[:3]
+        force_ref, own_ref, left_ref, right_ref, post_ref, post_edge_ref, east_ref, west_ref = refs[3:]
+        start = 0
+        edges = [edges_ref[e] for e in range(19)]
 
     def dev(e, part):
-        if not split:
-            return dev_refs[0][e, part, :]
-        return dev_refs[0][STILL.index(e), part, :] if e in STILL else dev_refs[1][MOVING.index(e), part, :]
+        if first:
+            return pop_ref[e, part, :]
+        return still_ref[STILL.index(e), part, :] if e in STILL else moving_ref[MOVING.index(e), part, :]
+
+    def force_part(ref, c):
+        return ref[start + 8 * c : start + 8 * c + 8, :]
 
     row, lane = iotas()
     force_edge = [
-        force_edge_ref[8 * c : 8 * c + 8, :]
-        + jnp.where(row >= 4, turn(left_ref[8 * c : 8 * c + 8, :], 4, 0), turn(right_ref[8 * c : 8 * c + 8, :], 4, 0))
+        force_part(own_ref, c)
+        + jnp.where(row >= 4, turn(force_part(left_ref, c), 4, 0), turn(force_part(right_ref, c), 4, 0))
         for c in range(3)
     ]
     swapped = [turn(value, 4, 0) for value in force_edge]
@@ -405,7 +443,7 @@
         post = collide([dev(e, part) for e in range(19)], force)
         for e in range(19):
             post_ref[e, part, :] = post[e]
-    post = collide([edges_ref[e] for e in range(19)], force_edge)
+    post = collide(edges, force_edge)
     for e in range(19):
         post_edge_ref[e] = post[e]
     for k in range(5):
@@ -488,7 +526,7 @@
     for k, e in enumerate(STILL):
         edges_ref[e] = still_edge_ref[k]
     flow_slices(lambda z: [dev(e, z) for e in range(19)], flow_ref)
-    flow_edges([edges_ref[e] for e in range(19)], halo_ref)
+    flow_edges(edge_flow([edges_ref[e] for e in range(19)]), halo_ref)
     prepare_matrix(flow_ref, halo_ref, matrix_ref)
     speed_ref[...] = jnp.zeros_like(speed_ref)
     couple(slots, table_ref, matrix_ref, total_ref, speed_ref)
@@ -578,7 +616,6 @@
 
     own_part = fraction.reshape(filaments, 3, share_blocks, BLOCK).transpose(1, 2, 0, 3)
     own_part = own_part.reshape(3 * share_blocks * filaments, BLOCK)
-    parts = [own_part] + [ring(own_part, "gy", s) for s in range(1, columns)]
 
     field = (19, ROWS, 128)
     edge = (19, 8, 128)
@@ -587,10 +624,15 @@
     flat_spans = spans.reshape(-1)
     where = jnp.stack([lax.axis_index("gx"), lax.axis_index("gy")]).astype(jnp.int32)
 
-    (own_edge,) = call(edge_kernel, [edge], [], 0, (pop,))
-    left, right = ring(own_edge, "gy", 1), ring(own_edge, "gy", -1)
     force_shape = (3, ROWS, 128)
-    (flow,) = call(flow_kernel, [force_shape], [], 0, (pop,))
+    share_rows = 3 * share_blocks * filaments
+    inside, anywhere = pl.BlockSpec(memory_space=pltpu.VMEM), pl.BlockSpec(memory_space=pl.ANY)
+    flow, payload = call(
+        flow_kernel, [force_shape, (share_rows + 24, BLOCK)], [pltpu.SemaphoreType.DMA], 0, (pop, own_part),
+        in_specs=[inside, anywhere],
+    )
+    parts = [payload] + [ring(payload, "gy", s) for s in range(1, columns)]
+    own_edge, right_edge, left_edge = call(edge_kernel, [edge, (EDGE_ROWS, 128), (EDGE_ROWS, 128)], [], 0, (pop,))
 
     table_shape = (slots, 16, BLOCK)
     coupling = [
@@ -599,28 +641,27 @@
         pltpu.VMEM((3 * FIELDS * DEPTH, 256), f32),
         pltpu.VMEM((slots, 8, BLOCK), f32),
     ]
-    force, force_edge, edges, table = call(
+    force, to_right, to_left, table = call(
         functools.partial(first_kernel, span_y, slots, filaments, columns),
-        [force_shape, (24, 128), edge, table_shape],
+        [force_shape, (EDGE_ROWS + 24, 128), (EDGE_ROWS + 24, 128), table_shape],
         coupling + [pltpu.VMEM((filaments * blocks * 8, BLOCK), f32), pltpu.VMEM(((slots + 1) * 8, BLOCK), f32)],
         3,
-        (flat_spans, where, stiffness, flow, own_edge, left, right, *parts),
+        (flat_spans, where, stiffness, flow, right_edge, left_edge, *parts),
     )
 
     plane = (5, 40, 128)
     moved = pltpu.VMEM((5, ROWS, 128), f32)
 
-    def collision(dev, edges, force, force_edge, left, right):
+    def collision(first, dev, force, force_edge, left, right):
         post, post_edge, east, west = call(
-            functools.partial(collide_kernel, len(dev) - 1),
-            [field, edge, plane, plane], [], 0, (*dev, edges, force, force_edge, left, right),
+            functools.partial(collide_kernel, first),
+            [field, edge, plane, plane], [], 0, (*dev, force, force_edge, left, right),
         )
         return post, post_edge, ring(east, "gx", 1), ring(west, "gx", -1)
 
-    left, right = ring(force_edge, "gy", 1), ring(force_edge, "gy", -1)
-    post, post_edge, east, west = collision((pop,), edges, force, force_edge, left, right)
+    left, right = ring(to_right, "gy", 1), ring(to_left, "gy", -1)
+    post, post_edge, east, west = collision(True, (pop, own_edge), force, to_right, left, right)
     still, still_edge = call(still_kernel, [(9, ROWS, 128), (9, 8, 128)], [], 0, (post, post_edge))
-    share_rows = 3 * share_blocks * filaments
     dev, edges, force, to_right, to_left, *chunks = call(
         functools.partial(second_kernel, slots, blocks, columns),
         [(10, ROWS, 128), edge, force_shape] + [(24 + share_rows, BLOCK)] * 2 + [(share_rows, BLOCK)] * (columns - 2),
@@ -629,14 +670,12 @@
         (flat_spans, where, post, post_edge, still, still_edge, east, west, table),
     )
     left, right = ring(to_right, "gy", 1), ring(to_left, "gy", -1)
-    post, post_edge, east, west = collision((still, dev), edges, force, to_right, left, right)
+    post, post_edge, east, west = collision(False, (still, dev, edges), force, to_right, left, right)
     speed = chunks[0] + left[24:] + right[24:]
     for s in range(2, columns - 1):
         speed = speed + ring(chunks[s - 1], "gy", s)
     speed = speed.reshape(3, share_blocks, filaments, BLOCK).transpose(2, 0, 1, 3).reshape(fraction.shape)
 
-    anywhere = pl.BlockSpec(memory_space=pl.ANY)
-    inside = pl.BlockSpec(memory_space=pltpu.VMEM)
     (dev,) = call(
         last_still_kernel, [field],
         [pltpu.VMEM((9, ROWS, 128), f32), pltpu.SemaphoreType.DMA((9,))],

time: 49.6 us -> 48 us (0.968)
  starting transfers between devices: 16.3 us -> 14.4 us
  local copies, waits for them, and re-layouts: 1.91 us -> 2.63 us
  waiting for transfers between devices: 12.7 us -> 12 us
    ppermute x14 -> x12, starting transfers between devices: 16.3 us -> 14.4 us  [ring(): lax.ppermute(value, axis, [(i, (i + step) % count) for i in range(count)])]
    unnamed x11, local copies, waits for them, and re-layouts: 1.82 us -> 2.55 us
    ppermute x14 -> x12, waiting for transfers between devices: 12.7 us -> 12 us  [ring(): lax.ppermute(value, axis, [(i, (i + step) % count) for i in range(count)])]
  transfers between devices with their start and end apart: 14 -> 12, of which waited for: 10 -> 10; matrix products, arithmetic and copies ran while one was open for 4% -> 4% of each run, Pallas kernels for 5% -> 5%
where the time goes in v3:
time: 48 us; the launch traced here: 47.8 us
  Pallas kernels  16.5 us (34%)
  starting transfers between devices  14.4 us (30%)
  waiting for transfers between devices  12 us (25%)
  local copies, waits for them, and re-layouts  2.63 us (5%)
  other arithmetic  1.36 us (3%)
  between operations  0.88 us (2%)
    pallas_call x9, Pallas kernels, call(): pl.pallas_call(body, out_shape=[jax.ShapeDtypeStruct(shape, jnp.float32)...  16.5 us
    ppermute x12, starting transfers between devices, ring(): lax.ppermute(value, axis, [(i, (i + step) % count) for i in range(count)])  14.4 us
    ppermute x12, waiting for transfers between devices, ring(): lax.ppermute(value, axis, [(i, (i + step) % count) for i in range(count)])  12 us
    unnamed x11, local copies, waits for them, and re-layouts  2.55 us
  transfers between devices with their start and end apart: 12, of which 10 were waited for; matrix products, arithmetic and copies ran while one was open for 4% of the time, Pallas kernels for 5%

profile of v3, /device:TPU:0, one launch (start us, length us, event | category | flops | bytes accessed | tf_op | source)
XLA Modules:
  0.0 47.8 jit_solution(11678729040929850038)
XLA Ops:
  0.6 1.3 %copy-done = f32[19,16,4,256]{3,2,1,0:T(4,128)S(1)} copy-done((f32[19,16,4,256]{3,2,1,0:T(4,128)S(1)}, f32[19,16,4,256]{3,2,1,0:T(4,128)}, u32[]{:S(2)}) %copy-start) | copy-done | bytes 1245208
  1.9 0.7 %copy-done.2 = f32[2,3,1024]{2,0,1:T(2,128)S(1)} copy-done((f32[2,3,1024]{2,0,1:T(2,128)S(1)}, f32[2,3,1024]{2,0,1:T(2,128)}, u32[]{:S(2)}) %copy-start.2) | copy-done | bytes 24600
  2.7 0.2 shard_map.60
  2.9 2.4 %collective-permute-start.2 = (f32[72,128]{1,0:T(8,128)S(1)}, f32[72,128]{1,0:T(8,128)S(1)}, u32[]{:S(2)}, u32[]{:S(2)}) collective-permute-start(f32[72,128]{1,0:T(8,128)S(1)} %get-tuple-element.32.refs_0_), channel_id=1, source_target_pairs={{0,3},{1,0},{2,1},{3,2},{4,7},{5,4},{6,5},{7,6},{8,11},{9,8},{10,9... | collective-permute-start | bytes 110600 | tf_op jit(solution)/shard_map/ppermute | solution.py:604
  5.3 0.6 %collective-permute-start.1 = (f32[72,128]{1,0:T(8,128)S(1)}, f32[72,128]{1,0:T(8,128)S(1)}, u32[]{:S(2)}, u32[]{:S(2)}) collective-permute-start(f32[72,128]{1,0:T(8,128)S(1)} %get-tuple-element.32.refs_0_), channel_id=1, source_target_pairs={{0,2},{1,3},{2,0},{3,1},{4,6},{5,7},{6,4},{7,5},{8,10},{9,11},{10,... | collective-permute-start | bytes 110600 | tf_op jit(solution)/shard_map/ppermute | solution.py:604
  6.2 0.4 shard_map.59
  6.6 0.5 %broadcast.3 = s32[]{:T(128)} broadcast(s32[]{:T(128)} %constant.20), dimensions={} | broadcast | bytes 8 | tf_op args[2]
  7.1 0.7 %reduce.3 = s32[2,32]{1,0:T(2,128)S(1)} reduce(s32[2,32,1]{1,2,0:T(1,128)S(1)} %copy-done.4, s32[]{:T(128)} %broadcast.3), dimensions={2}, to_apply=%param.6.reduce_sub_computation.3 | reduce | bytes 516 | tf_op args[2]
  7.9 1.7 %collective-permute-done.1.refs_2_ = f32[72,128]{1,0:T(8,128)S(1)} collective-permute-done((f32[72,128]{1,0:T(8,128)S(1)}, f32[72,128]{1,0:T(8,128)S(1)}, u32[]{:S(2)}, u32[]{:S(2)}) %collective-permute-start.1) | collective-permute-done | bytes 36896 | tf_op jit(solution)/shard_map/ppermute | solution.py:604
  9.7 6.0 %shard_map.61 = (f32[3,128,128]{2,1,0:T(8,128)S(1)}, f32[104,128]{1,0:T(8,128)S(1)}, f32[104,128]{1,0:T(8,128)S(1)}, f32[32,16,128]{2,1,0:T(8,128)S(1)}) custom-call(s32[64]{0:T(128)S(1)} %reshape.33.spans_ref, s32[2]{0:T(128)S(1)} %pad_add_fusion.where_ref, s32[2]{0:T(128)S(1)} %copy-done.3, f32[3,128,128]{2,1,0:T(8,128)S(1)} %get-tuple-element.29.flow_ref, ...), custom_call_target="tpu_custom_call" | custom-call | bytes 1130496 | tf_op jit(solution)/shard_map/pallas_call | solution.py:593
  15.8 0.5 %collective-permute-start.3 = (f32[104,128]{1,0:T(8,128)S(1)}, f32[104,128]{1,0:T(8,128)S(1)}, u32[]{:S(2)}, u32[]{:S(2)}) collective-permute-start(f32[104,128]{1,0:T(8,128)S(1)} %get-tuple-element.34.refs_3_), channel_id=1, source_target_pairs={{0,1},{1,2},{2,3},{3,0},{4,5},{5,6},{6,7},{7,4},{8,9},{9,10},{10,1... | collective-permute-start | bytes 159752 | tf_op jit(solution)/shard_map/ppermute | solution.py:604
  16.3 1.3 %collective-permute-done.4.refs_5_ = f32[104,128]{1,0:T(8,128)S(1)} collective-permute-done((f32[104,128]{1,0:T(8,128)S(1)}, f32[104,128]{1,0:T(8,128)S(1)}, u32[]{:S(2)}, u32[]{:S(2)}) %collective-permute-start.4) | collective-permute-done | bytes 53280 | tf_op jit(solution)/shard_map/ppermute | solution.py:604
  17.5 2.1 %collective-permute-done.3.refs_4_ = f32[104,128]{1,0:T(8,128)S(1)} collective-permute-done((f32[104,128]{1,0:T(8,128)S(1)}, f32[104,128]{1,0:T(8,128)S(1)}, u32[]{:S(2)}, u32[]{:S(2)}) %collective-permute-start.3) | collective-permute-done | bytes 53280 | tf_op jit(solution)/shard_map/ppermute | solution.py:604
  19.6 0.6 %shard_map.62 = (f32[19,128,128]{2,1,0:T(8,128)S(1)}, f32[19,8,128]{2,1,0:T(8,128)S(1)}, f32[5,40,128]{2,1,0:T(8,128)S(1)}, f32[5,40,128]{2,1,0:T(8,128)S(1)}) custom-call(f32[19,128,128]{2,1,0:T(8,128)S(1)} %bitcast.25, f32[19,8,128]{2,1,0:T(8,128)S(1)} %get-tuple-element.28.refs_1_, f32[3,128,128]{2,1,0:T(8,128)S(1)} %get-tuple-element.33.refs_2_, ...), custom_call_target="tpu_custom_call" | custom-call | bytes 3055616 | tf_op jit(solution)/shard_map/pallas_call | solution.py:593
  20.2 1.6 %collective-permute-start.5 = (f32[5,40,128]{2,1,0:T(8,128)S(1)}, f32[5,40,128]{2,1,0:T(8,128)S(1)}, u32[]{:S(2)}, u32[]{:S(2)}) collective-permute-start(f32[5,40,128]{2,1,0:T(8,128)S(1)} %get-tuple-element.40), channel_id=1, source_target_pairs={{0,4},{4,8},{8,12},{12,16},{16,20},{20,24},{24,28},{28,0},{1,5},{5... | collective-permute-start | bytes 307208 | tf_op jit(solution)/shard_map/ppermute | solution.py:604
  21.7 3.3 %collective-permute-start.6 = (f32[5,40,128]{2,1,0:T(8,128)S(1)}, f32[5,40,128]{2,1,0:T(8,128)S(1)}, u32[]{:S(2)}, u32[]{:S(2)}) collective-permute-start(f32[5,40,128]{2,1,0:T(8,128)S(1)} %get-tuple-element.41), channel_id=1, source_target_pairs={{0,28},{4,0},{8,4},{12,8},{16,12},{20,16},{24,20},{28,24},{1,29},{... | collective-permute-start | bytes 307208 | tf_op jit(solution)/shard_map/ppermute | solution.py:604
  25.0 0.5 shard_map.63
  25.5 2.2 %collective-permute-done.5.east_ref = f32[5,40,128]{2,1,0:T(8,128)S(1)} collective-permute-done((f32[5,40,128]{2,1,0:T(8,128)S(1)}, f32[5,40,128]{2,1,0:T(8,128)S(1)}, u32[]{:S(2)}, u32[]{:S(2)}) %collective-permute-start.5) | collective-permute-done | bytes 102432 | tf_op jit(solution)/shard_map/ppermute | solution.py:604
  27.7 0.9 %collective-permute-done.6.west_ref = f32[5,40,128]{2,1,0:T(8,128)S(1)} collective-permute-done((f32[5,40,128]{2,1,0:T(8,128)S(1)}, f32[5,40,128]{2,1,0:T(8,128)S(1)}, u32[]{:S(2)}, u32[]{:S(2)}) %collective-permute-start.6) | collective-permute-done | bytes 102432 | tf_op jit(solution)/shard_map/ppermute | solution.py:604
  28.6 6.0 %shard_map.64 = (f32[10,128,128]{2,1,0:T(8,128)S(1)}, f32[19,8,128]{2,1,0:T(8,128)S(1)}, f32[3,128,128]{2,1,0:T(8,128)S(1)}, f32[72,128]{1,0:T(8,128)S(1)}, f32[...) custom-call(s32[64]{0:T(128)S(1)} %reshape.33.spans_ref, s32[2]{0:T(128)S(1)} %pad_add_fusion.where_ref, ...), custom_call_target="tpu_custom_call" | custom-call | bytes 2105344 | tf_op jit(solution)/shard_map/pallas_call | solution.py:593
  34.7 0.5 %collective-permute-start.7 = (f32[72,128]{1,0:T(8,128)S(1)}, f32[72,128]{1,0:T(8,128)S(1)}, u32[]{:S(2)}, u32[]{:S(2)}) collective-permute-start(f32[72,128]{1,0:T(8,128)S(1)} %get-tuple-element.46.refs_4_), channel_id=1, source_target_pairs={{0,1},{1,2},{2,3},{3,0},{4,5},{5,6},{6,7},{7,4},{8,9},{9,10},{10,1... | collective-permute-start | bytes 110600 | tf_op jit(solution)/shard_map/ppermute | solution.py:604
  35.2 0.4 collective-permute-start.11
  35.6 0.9 %collective-permute-done.8.refs_6_ = f32[72,128]{1,0:T(8,128)S(1)} collective-permute-done((f32[72,128]{1,0:T(8,128)S(1)}, f32[72,128]{1,0:T(8,128)S(1)}, u32[]{:S(2)}, u32[]{:S(2)}) %collective-permute-start.8) | collective-permute-done | bytes 36896 | tf_op jit(solution)/shard_map/ppermute | solution.py:604
  36.5 1.6 %collective-permute-done.7.refs_5_ = f32[72,128]{1,0:T(8,128)S(1)} collective-permute-done((f32[72,128]{1,0:T(8,128)S(1)}, f32[72,128]{1,0:T(8,128)S(1)}, u32[]{:S(2)}, u32[]{:S(2)}) %collective-permute-start.7) | collective-permute-done | bytes 36896 | tf_op jit(solution)/shard_map/ppermute | solution.py:604
  38.1 0.6 %shard_map.65 = (f32[19,128,128]{2,1,0:T(8,128)S(1)}, f32[19,8,128]{2,1,0:T(8,128)S(1)}, f32[5,40,128]{2,1,0:T(8,128)S(1)}, f32[5,40,128]{2,1,0:T(8,128)S(1)}) custom-call(f32[9,128,128]{2,1,0:T(8,128)S(1)} %get-tuple-element.38.still_ref.refs_0_, f32[10,128,128]{2,1,0:T(8,128)S(1)} %get-tuple-element.43.refs_1_, ...), custom_call_target="tpu_custom_call" | custom-call | bytes 3055616 | tf_op jit(solution)/shard_map/pallas_call | solution.py:593
  38.7 0.3 collective-permute-start.9
  39.0 4.5 %collective-permute-start.10 = (f32[5,40,128]{2,1,0:T(8,128)S(1)}, f32[5,40,128]{2,1,0:T(8,128)S(1)}, u32[]{:S(2)}, u32[]{:S(2)}) collective-permute-start(f32[5,40,128]{2,1,0:T(8,128)S(1)} %get-tuple-element.51), channel_id=1, source_target_pairs={{0,28},{4,0},{8,4},{12,8},{16,12},{20,16},{24,20},{28,24},{1,29},{... | collective-permute-start | bytes 307208 | tf_op jit(solution)/shard_map/ppermute | solution.py:604
  43.5 0.6 %fusion = f32[48,128]{1,0:T(8,128)} fusion(f32[48,128]{1,0:T(8,128)S(1)} %collective-permute-done.11, f32[72,128]{1,0:T(8,128)S(1)} %collective-permute-done.8.refs_6_, f32[48,128]{1,0:T(8,128)S(1)} %get-tuple-element.52, f32[72,128]{1,0:T(8,128)S(1)} %collective-permute-done.7.refs_5_), kind=kLoop, calls=%fused_computation.1 | loop fusion | flops 18432 | bytes 122880 | tf_op jit(solution)/shard_map/add | solution.py:676
  44.1 1.1 %shard_map.66.old_ref = f32[19,128,128]{2,1,0:T(8,128)} custom-call(f32[19,128,128]{2,1,0:T(8,128)S(1)} %get-tuple-element.48.post_ref, f32[19,8,128]{2,1,0:T(8,128)S(1)} %get-tuple-element.49.post_edge_ref), custom_call_target="tpu_custom_call" | custom-call | bytes 2490368 | tf_op jit(solution)/shard_map/pallas_call | solution.py:593
  45.2 1.0 %collective-permute-done.9.east_ref = f32[5,40,128]{2,1,0:T(8,128)S(1)} collective-permute-done((f32[5,40,128]{2,1,0:T(8,128)S(1)}, f32[5,40,128]{2,1,0:T(8,128)S(1)}, u32[]{:S(2)}, u32[]{:S(2)}) %collective-permute-start.9) | collective-permute-done | bytes 102432 | tf_op jit(solution)/shard_map/ppermute | solution.py:604
  46.2 0.3 collective-permute-done.10.west_ref
  46.5 1.1 %shard_map.67 = f32[19,128,128]{2,1,0:T(8,128)} custom-call(f32[19,128,128]{2,1,0:T(8,128)S(1)} %get-tuple-element.48.post_ref, f32[19,8,128]{2,1,0:T(8,128)S(1)} %get-tuple-element.49.post_edge_ref, f32[5,40,128]{2,1,0:T(8,128)S(1)} %collective-permute-done.9.east_ref, ...), custom_call_target="tpu_custom_call", output_to_operand_aliasing={{}: (4, {})} | custom-call | bytes 2490368 | tf_op jit(solution)/shard_map/pallas_call | solution.py:593
  (16 shorter events, 0.5 us)
Async XLA Ops:
  0.6 1.3 %copy-start = (f32[19,16,4,256]{3,2,1,0:T(4,128)S(1)}, f32[19,16,4,256]{3,2,1,0:T(4,128)}, u32[]{:S(2)}) copy-start(f32[19,16,4,256]{3,2,1,0:T(4,128)} %param.4) | copy-start | bytes 3735556
  1.9 0.7 %copy-start.2 = (f32[2,3,1024]{2,0,1:T(2,128)S(1)}, f32[2,3,1024]{2,0,1:T(2,128)}, u32[]{:S(2)}) copy-start(f32[2,3,1024]{2,0,1:T(2,128)} %param.5) | copy-start | bytes 73732
  2.7 3.6 %copy-start.1 = (f32[19,16,4,256]{3,2,1,0:T(4,128)S(1)}, f32[19,16,4,256]{3,2,1,0:T(4,128)}, u32[]{:S(2)}) copy-start(f32[19,16,4,256]{3,2,1,0:T(4,128)} %param.4) | copy-start | bytes 3735556
  2.7 4.5 %copy-start.4 = (s32[2,32,1]{1,2,0:T(1,128)S(1)}, s32[2,32,1]{1,2,0:T(1,128)}, u32[]{:S(2)}) copy-start(s32[2,32,1]{1,2,0:T(1,128)} %param.6) | copy-start | bytes 772
  2.7 7.0 %copy-start.3 = (s32[2]{0:T(128)S(1)}, s32[2]{0:T(128)}, u32[]{:S(2)}) copy-start(s32[2]{0:T(128)} %stiff_ref.1) | copy-start | bytes 28
  2.9 5.0 %collective-permute-start.2 = (f32[72,128]{1,0:T(8,128)S(1)}, f32[72,128]{1,0:T(8,128)S(1)}, u32[]{:S(2)}, u32[]{:S(2)}) collective-permute-start(f32[72,128]{1,0:T(8,128)S(1)} %get-tuple-element.32.refs_0_), channel_id=1, source_target_pairs={{0,3},{1,0},{2,1},{3,2},{4,7},{5,4},{6,5},{7,6},{8,11},{9,8},{10,9... | collective-permute-start | bytes 110600 | tf_op jit(solution)/shard_map/ppermute | solution.py:604
  5.3 4.3 %collective-permute-start.1 = (f32[72,128]{1,0:T(8,128)S(1)}, f32[72,128]{1,0:T(8,128)S(1)}, u32[]{:S(2)}, u32[]{:S(2)}) collective-permute-start(f32[72,128]{1,0:T(8,128)S(1)} %get-tuple-element.32.refs_0_), channel_id=1, source_target_pairs={{0,2},{1,3},{2,0},{3,1},{4,6},{5,7},{6,4},{7,5},{8,10},{9,11},{10,... | collective-permute-start | bytes 110600 | tf_op jit(solution)/shard_map/ppermute | solution.py:604
  6.0 3.7 %collective-permute-start = (f32[72,128]{1,0:T(8,128)S(1)}, f32[72,128]{1,0:T(8,128)S(1)}, u32[]{:S(2)}, u32[]{:S(2)}) collective-permute-start(f32[72,128]{1,0:T(8,128)S(1)} %get-tuple-element.32.refs_0_), channel_id=1, source_target_pairs={{0,1},{1,2},{2,3},{3,0},{4,5},{5,6},{6,7},{7,4},{8,9},{9,10},{10,1... | collective-permute-start | bytes 110600 | tf_op jit(solution)/shard_map/ppermute | solution.py:604
  15.7 1.8 %collective-permute-start.4 = (f32[104,128]{1,0:T(8,128)S(1)}, f32[104,128]{1,0:T(8,128)S(1)}, u32[]{:S(2)}, u32[]{:S(2)}) collective-permute-start(f32[104,128]{1,0:T(8,128)S(1)} %get-tuple-element.35), channel_id=1, source_target_pairs={{0,3},{1,0},{2,1},{3,2},{4,7},{5,4},{6,5},{7,6},{8,11},{9,8},{10,9... | collective-permute-start | bytes 159752 | tf_op jit(solution)/shard_map/ppermute | solution.py:604
  15.8 3.8 %collective-permute-start.3 = (f32[104,128]{1,0:T(8,128)S(1)}, f32[104,128]{1,0:T(8,128)S(1)}, u32[]{:S(2)}, u32[]{:S(2)}) collective-permute-start(f32[104,128]{1,0:T(8,128)S(1)} %get-tuple-element.34.refs_3_), channel_id=1, source_target_pairs={{0,1},{1,2},{2,3},{3,0},{4,5},{5,6},{6,7},{7,4},{8,9},{9,10},{10,1... | collective-permute-start | bytes 159752 | tf_op jit(solution)/shard_map/ppermute | solution.py:604
  20.2 7.5 %collective-permute-start.5 = (f32[5,40,128]{2,1,0:T(8,128)S(1)}, f32[5,40,128]{2,1,0:T(8,128)S(1)}, u32[]{:S(2)}, u32[]{:S(2)}) collective-permute-start(f32[5,40,128]{2,1,0:T(8,128)S(1)} %get-tuple-element.40), channel_id=1, source_target_pairs={{0,4},{4,8},{8,12},{12,16},{16,20},{20,24},{24,28},{28,0},{1,5},{5... | collective-permute-start | bytes 307208 | tf_op jit(solution)/shard_map/ppermute | solution.py:604
  21.7 6.9 %collective-permute-start.6 = (f32[5,40,128]{2,1,0:T(8,128)S(1)}, f32[5,40,128]{2,1,0:T(8,128)S(1)}, u32[]{:S(2)}, u32[]{:S(2)}) collective-permute-start(f32[5,40,128]{2,1,0:T(8,128)S(1)} %get-tuple-element.41), channel_id=1, source_target_pairs={{0,28},{4,0},{8,4},{12,8},{16,12},{20,16},{24,20},{28,24},{1,29},{... | collective-permute-start | bytes 307208 | tf_op jit(solution)/shard_map/ppermute | solution.py:604
  34.6 1.9 %collective-permute-start.8 = (f32[72,128]{1,0:T(8,128)S(1)}, f32[72,128]{1,0:T(8,128)S(1)}, u32[]{:S(2)}, u32[]{:S(2)}) collective-permute-start(f32[72,128]{1,0:T(8,128)S(1)} %get-tuple-element.47), channel_id=1, source_target_pairs={{0,3},{1,0},{2,1},{3,2},{4,7},{5,4},{6,5},{7,6},{8,11},{9,8},{10,9... | collective-permute-start | bytes 110600 | tf_op jit(solution)/shard_map/ppermute | solution.py:604
  34.7 3.4 %collective-permute-start.7 = (f32[72,128]{1,0:T(8,128)S(1)}, f32[72,128]{1,0:T(8,128)S(1)}, u32[]{:S(2)}, u32[]{:S(2)}) collective-permute-start(f32[72,128]{1,0:T(8,128)S(1)} %get-tuple-element.46.refs_4_), channel_id=1, source_target_pairs={{0,1},{1,2},{2,3},{3,0},{4,5},{5,6},{6,7},{7,4},{8,9},{9,10},{10,1... | collective-permute-start | bytes 110600 | tf_op jit(solution)/shard_map/ppermute | solution.py:604
  35.2 8.3 %collective-permute-start.11 = (f32[48,128]{1,0:T(8,128)S(1)}, f32[48,128]{1,0:T(8,128)S(1)}, u32[]{:S(2)}, u32[]{:S(2)}) collective-permute-start(f32[48,128]{1,0:T(8,128)S(1)} %get-tuple-element.53), channel_id=1, source_target_pairs={{0,2},{1,3},{2,0},{3,1},{4,6},{5,7},{6,4},{7,5},{8,10},{9,11},{10,... | collective-permute-start | bytes 73736 | tf_op jit(solution)/shard_map/ppermute | solution.py:604
  38.7 7.5 %collective-permute-start.9 = (f32[5,40,128]{2,1,0:T(8,128)S(1)}, f32[5,40,128]{2,1,0:T(8,128)S(1)}, u32[]{:S(2)}, u32[]{:S(2)}) collective-permute-start(f32[5,40,128]{2,1,0:T(8,128)S(1)} %get-tuple-element.50), channel_id=1, source_target_pairs={{0,4},{4,8},{8,12},{12,16},{16,20},{20,24},{24,28},{28,0},{1,5},{5... | collective-permute-start | bytes 307208 | tf_op jit(solution)/shard_map/ppermute | solution.py:604
  39.0 7.5 %collective-permute-start.10 = (f32[5,40,128]{2,1,0:T(8,128)S(1)}, f32[5,40,128]{2,1,0:T(8,128)S(1)}, u32[]{:S(2)}, u32[]{:S(2)}) collective-permute-start(f32[5,40,128]{2,1,0:T(8,128)S(1)} %get-tuple-element.51), channel_id=1, source_target_pairs={{0,28},{4,0},{8,4},{12,8},{16,12},{20,16},{24,20},{28,24},{1,29},{... | collective-permute-start | bytes 307208 | tf_op jit(solution)/shard_map/ppermute | solution.py:604

commit v4 on v3

--- a/solution.py
+++ b/solution.py
@@ -42,9 +42,13 @@
 DEPTH = 16
 ROWS = DEPTH * 8
 BLOCK = 128
-GROUP = 4
+GROUP = 32
+PLANE = 160
+PLANE_ROWS = 176
 FIELDS = 9
 EDGE_ROWS = 80
+TINY = 1e-30
+FINE = jnp.float8_e4m3fn
 VMEM_LIMIT = 40 * 1024 * 1024
 
 
@@ -165,46 +169,62 @@
     return one - sine, one + cosine, one + sine, one - cosine
 
 
-def prepare_matrix(flow_ref, halo_ref, matrix_ref):
+def largest(value):
+    return jnp.max(jnp.max(jnp.abs(value), axis=1, keepdims=True), axis=0, keepdims=True)
+
+
+def prepare_matrix(flow_ref, halo_ref, matrix_ref, rest_ref):
+    top = None
+    for c in range(3):
+        for z in range(DEPTH):
+            part = slice(8 * z, 8 * z + 8)
+            both = jnp.maximum(jnp.abs(flow_ref[c, part, :]), jnp.abs(halo_ref[c, part, :]))
+            top = both if top is None else jnp.maximum(top, both)
+    top = jnp.maximum(largest(top), TINY)
+    scale = 2.0**15 / top
     for c in range(3):
         per_x = []
         for x in range(4):
-            per_x.append(
-                [
-                    halo_ref[c, pl.ds(4 + x, DEPTH, stride=8), :],
-                    flow_ref[c, pl.ds(x, DEPTH, stride=8), :],
-                    flow_ref[c, pl.ds(4 + x, DEPTH, stride=8), :],
-                    halo_ref[c, pl.ds(x, DEPTH, stride=8), :],
-                ]
-            )
+            tiles = [
+                halo_ref[c, pl.ds(4 + x, DEPTH, stride=8), :],
+                flow_ref[c, pl.ds(x, DEPTH, stride=8), :],
+                flow_ref[c, pl.ds(4 + x, DEPTH, stride=8), :],
+                halo_ref[c, pl.ds(x, DEPTH, stride=8), :],
+            ]
+            per_x.append([tile * scale for tile in tiles])
         by_basis = [basis_fields([per_x[x][t] for x in range(4)]) for t in range(4)]
         for xf in range(3):
             tiles = [by_basis[t][xf] for t in range(4)]
             four = [shifted(tiles, s) for s in (-1, 0, 1, 2)]
             for half in range(2):
                 fields = basis_fields([four[s][half] for s in range(4)])
+                columns = slice(half * 128, half * 128 + 128)
                 for yf in range(3):
                     row = ((c * 3 + yf) * 3 + xf) * DEPTH
                     high = fields[yf].astype(jnp.bfloat16)
-                    low = (fields[yf] - high.astype(jnp.float32)).astype(jnp.bfloat16)
-                    matrix_ref[row : row + DEPTH, half * 128 : half * 128 + 128] = high
-                    matrix_ref[row : row + DEPTH, 256 + half * 128 : 256 + half * 128 + 128] = low
-
-
-def couple(slots, table_ref, matrix_ref, total_ref, speed_ref):
-    rows = 3 * FIELDS * DEPTH
-    width = GROUP * BLOCK
+                    matrix_ref[row : row + DEPTH, columns] = high
+                    rest_ref[row : row + DEPTH, columns] = fields[yf] - high.astype(jnp.float32)
+    return top
+
+
+def couple(slots, table_ref, matrix_ref, rest_ref, total_ref, speed_ref, top):
+    group = min(GROUP, slots)
+    unscale = top * 2.0**-15
+    bound = jnp.maximum(table_ref[0, 12:13, 0:1] + feedback_gain * top, TINY)
+    scale = 2.0**17 / bound
     total_ref[...] = jnp.zeros_like(total_ref)
-    column = lax.broadcasted_iota(jnp.int32, (256, BLOCK), 0).astype(jnp.float32)
+    column = lax.broadcasted_iota(jnp.int32, (256, BLOCK), 0).astype(jnp.float32).astype(jnp.bfloat16)
+    one, none = jnp.bfloat16(1), jnp.bfloat16(0)
     z_cell = lax.broadcasted_iota(jnp.int32, (DEPTH, BLOCK), 0).astype(jnp.float32)
+    rest = rest_ref[...].astype(FINE)
 
     def body(step):
-        first = step * GROUP
+        first = step * group
         hot, weight_z, coef = [], [], []
-        for g in range(GROUP):
+        for g in range(group):
             slot = first + g
             q = lambda k: table_ref[slot, k : k + 1, :]
-            hot.append(jnp.where(column == q(0), 1.0, 0.0).astype(jnp.bfloat16))
+            hot.append(jnp.where(column == q(0).astype(jnp.bfloat16), one, none))
             gap = z_cell - q(5)
             sine, cosine = q(6), q(7)
             weight_z.append(
@@ -225,12 +245,12 @@
                     for i in range(3)
                 ]
             )
-        hot = jnp.concatenate(hot, axis=1)
-        across = jnp.dot(
-            matrix_ref[...], jnp.concatenate([hot, hot], axis=0), preferred_element_type=jnp.float32
-        )
+        coarse = jnp.concatenate(hot, axis=1)
+        fine = coarse.astype(FINE)
+        across = jnp.dot(matrix_ref[...], coarse, preferred_element_type=jnp.float32)
+        across += jnp.dot(rest, fine, preferred_element_type=jnp.float32)
         spread_high, spread_low = [], []
-        for g in range(GROUP):
+        for g in range(group):
             slot = first + g
             columns = slice(g * BLOCK, (g + 1) * BLOCK)
             pieces = []
@@ -243,9 +263,9 @@
                         factor = coef[g][yf][xf]
                         term = term if factor is None else term * factor
                         sums = term if sums is None else sums + term
-                speed = jnp.sum(sums * weight_z[g], axis=0, keepdims=True)
+                speed = jnp.sum(sums * weight_z[g], axis=0, keepdims=True) * unscale
                 speed_ref[slot, c : c + 1, :] = speed
-                push = (table_ref[slot, 8 + c : 9 + c, :] - feedback_gain * speed) * table_ref[slot, 11:12, :]
+                push = (table_ref[slot, 8 + c : 9 + c, :] - feedback_gain * speed) * table_ref[slot, 11:12, :] * scale
                 for yf in range(3):
                     for xf in range(3):
                         factor = coef[g][yf][xf]
@@ -253,20 +273,20 @@
             piece = jnp.concatenate(pieces, axis=0)
             high = piece.astype(jnp.bfloat16)
             spread_high.append(high)
-            spread_low.append((piece - high.astype(jnp.float32)).astype(jnp.bfloat16))
-        left = jnp.concatenate(spread_high + spread_low, axis=1)
+            spread_low.append((piece - high.astype(jnp.float32)).astype(FINE))
+        across_rows = (((1,), (1,)), ((), ()))
         total_ref[...] += lax.dot_general(
-            left,
-            jnp.concatenate([hot, hot], axis=1),
-            (((1,), (1,)), ((), ())),
-            preferred_element_type=jnp.float32,
+            jnp.concatenate(spread_high, axis=1), coarse, across_rows, preferred_element_type=jnp.float32
+        ) + lax.dot_general(
+            jnp.concatenate(spread_low, axis=1), fine, across_rows, preferred_element_type=jnp.float32
         )
 
-    for step in range(slots // GROUP):
+    for step in range(slots // group):
         body(step)
-
-
-def finish_force(total_ref, halo_ref, force_ref, force_edge_ref, start=0):
+    return bound * 2.0**-21
+
+
+def finish_force(unscale, total_ref, halo_ref, force_ref, force_edge_ref, start=0):
     lane = lax.broadcasted_iota(jnp.int32, (DEPTH, 128), 1)
     zero = jnp.zeros((DEPTH, 128), jnp.float32)
     for c in range(3):
@@ -282,7 +302,7 @@
                 tiles = shifted([zero, zero, cells[0][k], cells[1][k], zero, zero], shift)
                 sums = tiles if sums is None else [a + b for a, b in zip(sums, tiles)]
             by_basis.append(sums)
-        by_x = [basis_cells([by_basis[xf][t] * 0.0625 for xf in range(3)]) for t in range(4)]
+        by_x = [basis_cells([by_basis[xf][t] * unscale for xf in range(3)]) for t in range(4)]
         for x in range(4):
             left, low, high, right = (by_x[t][x] for t in range(4))
             force_ref[c, pl.ds(x, DEPTH, stride=8), :] = low
@@ -380,15 +400,18 @@
     sine, cosine = basis(z - base)
     put(6, sine)
     put(7, cosine)
+    bends = [got(3 + c) for c in range(3)]
     for c in range(3):
-        put(8 + c, got(3 + c))
+        put(8 + c, bends[c])
     put(11, jnp.where(slot < count, 1.0, 0.0))
+    top = largest(jnp.maximum(jnp.maximum(jnp.abs(bends[0]), jnp.abs(bends[1])), jnp.abs(bends[2])))
+    table_ref[0, 12:13, :] = jnp.broadcast_to(top, (1, BLOCK))
 
 
 def first_kernel(span_y, slots, filaments, columns, spans_ref, where_ref, stiff_ref, flow_ref, right_edge_ref, left_edge_ref, *refs):
     part_refs, refs = refs[:columns], refs[columns:]
     force_ref, to_right_ref, to_left_ref, table_ref = refs[:4]
-    halo_ref, matrix_ref, total_ref, speed_ref, places_ref, picked_ref = refs[4:]
+    halo_ref, matrix_ref, rest_ref, total_ref, speed_ref, places_ref, picked_ref = refs[4:]
     share = spans_ref.shape[0] // (filaments * columns)
     to_right_ref[0:EDGE_ROWS, :] = right_edge_ref[...]
     to_left_ref[0:EDGE_ROWS, :] = left_edge_ref[...]
@@ -400,72 +423,76 @@
         start = 3 * share * filaments + 8 * c
         flows.append(merge_edges(*(part_refs[s][start : start + 8, :] for s in (0, 1, -1))))
     flow_edges(flows, halo_ref)
-    prepare_matrix(flow_ref, halo_ref, matrix_ref)
-    couple(slots, table_ref, matrix_ref, total_ref, speed_ref)
-    finish_force(total_ref, halo_ref, force_ref, to_right_ref, EDGE_ROWS)
+    top = prepare_matrix(flow_ref, halo_ref, matrix_ref, rest_ref)
+    unscale = couple(slots, table_ref, matrix_ref, rest_ref, total_ref, speed_ref, top)
+    finish_force(unscale, total_ref, halo_ref, force_ref, to_right_ref, EDGE_ROWS)
     to_left_ref[EDGE_ROWS:, :] = to_right_ref[EDGE_ROWS:, :]
 
 
 def collide_kernel(first, *refs):
-    if first:
-        pop_ref, edge_ref = refs[:2]
-        force_ref, own_ref, left_ref, right_ref, post_ref, post_edge_ref, east_ref, west_ref = refs[2:]
-        start = EDGE_ROWS
-        edges = []
-        for e in range(19):
-            part, shift = slice(8 * (e // 2), 8 * (e // 2) + 8), 4 * (e % 2)
-            edges.append(merge_edges(edge_ref[e], turn(left_ref[part, :], shift, 0), turn(right_ref[part, :], shift, 0)))
-    else:
-        still_ref, moving_ref, edges_ref = refs[:3]
-        force_ref, own_ref, left_ref, right_ref, post_ref, post_edge_ref, east_ref, west_ref = refs[3:]
-        start = 0
-        edges = [edges_ref[e] for e in range(19)]
+    dev_refs, (force_ref, post_ref, east_ref, west_ref) = refs[:-4], refs[-4:]
 
     def dev(e, part):
         if first:
-            return pop_ref[e, part, :]
-        return still_ref[STILL.index(e), part, :] if e in STILL else moving_ref[MOVING.index(e), part, :]
-
-    def force_part(ref, c):
-        return ref[start + 8 * c : start + 8 * c + 8, :]
-
-    row, lane = iotas()
-    force_edge = [
-        force_part(own_ref, c)
-        + jnp.where(row >= 4, turn(force_part(left_ref, c), 4, 0), turn(force_part(right_ref, c), 4, 0))
-        for c in range(3)
-    ]
-    swapped = [turn(value, 4, 0) for value in force_edge]
-    patch = ((row < 4) & (lane < 3)) | ((row >= 4) & (lane >= 126))
+            return dev_refs[0][e, part, :]
+        for ref, entries in zip(dev_refs, (STILL, EAST, WEST)):
+            if e in entries:
+                return ref[entries.index(e), part, :]
+
     for z in range(DEPTH):
         part = slice(8 * z, 8 * z + 8)
-        force = [jnp.where(patch, turn(swapped[c], -(5 * z + 2), 1), force_ref[c, part, :]) for c in range(3)]
-        post = collide([dev(e, part) for e in range(19)], force)
+        post = collide([dev(e, part) for e in range(19)], [force_ref[c, part, :] for c in range(3)])
         for e in range(19):
             post_ref[e, part, :] = post[e]
-    post = collide(edges, force_edge)
+    for k in range(5):
+        east_ref[32 * k : 32 * k + 32, :] = post_ref[EAST[k], pl.ds(3, 32, stride=4), :]
+        west_ref[32 * k : 32 * k + 32, :] = post_ref[WEST[k], pl.ds(0, 32, stride=4), :]
+
+
+def collide_edge_kernel(first, edge_ref, own_ref, left_ref, right_ref, to_east_ref, to_west_ref, post_edge_ref, east_ref, west_ref):
+    row, _ = iotas()
+    start = EDGE_ROWS if first else 0
+    edges = []
+    for e in range(19):
+        value = edge_ref[e]
+        if first:
+            part, shift = slice(8 * (e // 2), 8 * (e // 2) + 8), 4 * (e % 2)
+            value = merge_edges(value, turn(left_ref[part, :], shift, 0), turn(right_ref[part, :], shift, 0))
+        edges.append(value)
+    force = []
+    for c in range(3):
+        part = slice(start + 8 * c, start + 8 * c + 8)
+        force.append(own_ref[part, :] + jnp.where(row >= 4, turn(left_ref[part, :], 4, 0), turn(right_ref[part, :], 4, 0)))
+    post = collide(edges, force)
     for e in range(19):
         post_edge_ref[e] = post[e]
+    east_ref[0:PLANE, :] = to_east_ref[...]
+    west_ref[0:PLANE, :] = to_west_ref[...]
     for k in range(5):
-        east_ref[k, 0:32, :] = post_ref[EAST[k], pl.ds(3, 32, stride=4), :]
-        east_ref[k, 32:40, :] = post[EAST[k]]
-        west_ref[k, 0:32, :] = post_ref[WEST[k], pl.ds(0, 32, stride=4), :]
-        west_ref[k, 32:40, :] = post[WEST[k]]
-
-
-def stream(entries, post_ref, post_edge_ref, east_ref, west_ref, moved_ref, store, store_edge):
+        line = PLANE + 2 * k
+        for half in range(2):
+            at = 4 * half
+            east_ref[line + half : line + half + 1, :] = post[EAST[k]][at + 3 : at + 4, :]
+            west_ref[line + half : line + half + 1, :] = post[WEST[k]][at : at + 1, :]
+    zero = jnp.zeros((PLANE_ROWS - PLANE - 10, 128), jnp.float32)
+    east_ref[PLANE + 10 :, :] = zero
+    west_ref[PLANE + 10 :, :] = zero
+
+
+def stream(entries, post_ref, post_edge_ref, plane_ref, moved_ref, store, store_edge):
     row, lane = iotas()
-    patches = {1: (row < 4) & (lane == 0), -1: (row >= 4) & (lane == 127)}
+    low, high = row < 4, row >= 4
+    same = (low & (lane < 2)) | (high & (lane == 127))
+    patches = {0: same, 1: low & (lane < 3), -1: (low & (lane == 0)) | (high & (lane >= 126))}
     low_wall, high_wall = lane < 5, lane >= 75
     for e in entries:
         cx, cy, cz = velocity_set[e]
         edge = post_edge_ref[e]
-        if cx == 1:
-            k = EAST.index(e)
-            edge = jnp.where(row % 4 == 0, turn(east_ref[k, 32:40, :], 5, 0), turn(edge, 1, 0))
-        elif cx == -1:
-            k = WEST.index(e)
-            edge = jnp.where(row % 4 == 3, turn(west_ref[k, 32:40, :], 3, 0), turn(edge, -1, 0))
+        if cx != 0:
+            k = (EAST if cx == 1 else WEST).index(e)
+            line = PLANE + 2 * k
+            beside = jnp.where(low, plane_ref[line : line + 1, :], plane_ref[line + 1 : line + 2, :])
+            edge = jnp.where(row % 4 == (0 if cx == 1 else 3), beside, turn(edge, cx, 0))
         edge = turn(edge, cy + 5 * cz, 1)
         if cz == 1:
             edge = jnp.where(low_wall, post_edge_ref[opposite(e)], edge)
@@ -475,62 +502,66 @@
         if cx != 0:
             for z in range(DEPTH):
                 moved_ref[k, 8 * z : 8 * z + 8, :] = turn(post_ref[e, 8 * z : 8 * z + 8, :], cx, 0)
-            if cx == 1:
-                moved_ref[k, pl.ds(0, 32, stride=4), :] = east_ref[k, 0:32, :]
-            else:
-                moved_ref[k, pl.ds(3, 32, stride=4), :] = west_ref[k, 0:32, :]
+            moved_ref[k, pl.ds(0 if cx == 1 else 3, 32, stride=4), :] = plane_ref[32 * k : 32 * k + 32, :]
         swapped = turn(edge, 4, 0)
         for z in range(DEPTH):
-            source = z - cz
+            source, patch = z - cz, patches[cy]
             if 0 <= source < DEPTH:
                 part = slice(8 * source, 8 * source + 8)
                 value = post_ref[e, part, :] if cx == 0 else moved_ref[k, part, :]
                 if cy != 0:
                     value = turn(value, cy, 1)
                     value = jnp.where(lane == (0 if cy == 1 else 127), turn(value, 4, 0), value)
-                    value = jnp.where(patches[cy], turn(swapped, -(5 * z + 2), 1), value)
             else:
-                value = post_ref[opposite(e), 8 * z : 8 * z + 8, :]
-            store(e, z, value)
-
-
-def still_kernel(post_ref, post_edge_ref, dev_ref, edges_ref):
+                value, patch = post_ref[opposite(e), 8 * z : 8 * z + 8, :], same
+            store(e, z, jnp.where(patch, turn(swapped, -(5 * z + 2), 1), value))
+
+
+def stream_kernel(entries, post_ref, post_edge_ref, *refs):
+    plane_ref, refs = (None, refs) if entries is STILL else (refs[0], refs[1:])
+    dev_ref, edges_ref = refs[:2]
+    moved_ref = None if entries is STILL else refs[2]
+
     def store(e, z, value):
-        dev_ref[STILL.index(e), 8 * z : 8 * z + 8, :] = value
+        dev_ref[entries.index(e), 8 * z : 8 * z + 8, :] = value
 
     def store_edge(e, value):
-        edges_ref[STILL.index(e)] = value
-
-    stream(STILL, post_ref, post_edge_ref, None, None, None, store, store_edge)
+        edges_ref[entries.index(e)] = value
+
+    stream(entries, post_ref, post_edge_ref, plane_ref, moved_ref, store, store_edge)
 
 
 def second_kernel(
     slots, blocks, columns, spans_ref, where_ref,
-    post_ref, post_edge_ref, still_ref, still_edge_ref, east_ref, west_ref, table_ref, *refs
+    post_ref, post_edge_ref, still_ref, still_edge_ref, east_dev_ref, east_edge_ref, west_ref, table_ref, *refs
 ):
     dev_ref, edges_ref, force_ref, to_right_ref, to_left_ref = refs[:5]
     share_refs, refs = refs[5 : 3 + columns], refs[3 + columns :]
-    moved_ref, flow_ref, halo_ref, matrix_ref, total_ref, speed_ref, spot_ref = refs
+    moved_ref, flow_ref, halo_ref, matrix_ref, rest_ref, total_ref, speed_ref, spot_ref = refs
 
     def store(e, z, value):
-        dev_ref[MOVING.index(e), 8 * z : 8 * z + 8, :] = value
+        dev_ref[WEST.index(e), 8 * z : 8 * z + 8, :] = value
 
     def store_edge(e, value):
         edges_ref[e] = value
 
     def dev(e, z):
         part = slice(8 * z, 8 * z + 8)
-        return still_ref[STILL.index(e), part, :] if e in STILL else dev_ref[MOVING.index(e), part, :]
-
-    stream(MOVING, post_ref, post_edge_ref, east_ref, west_ref, moved_ref, store, store_edge)
+        for ref, entries in ((still_ref, STILL), (east_dev_ref, EAST), (dev_ref, WEST)):
+            if e in entries:
+                return ref[entries.index(e), part, :]
+
+    stream(WEST, post_ref, post_edge_ref, west_ref, moved_ref, store, store_edge)
+    for k, e in enumerate(EAST):
+        edges_ref[e] = east_edge_ref[k]
     for k, e in enumerate(STILL):
         edges_ref[e] = still_edge_ref[k]
     flow_slices(lambda z: [dev(e, z) for e in range(19)], flow_ref)
     flow_edges(edge_flow([edges_ref[e] for e in range(19)]), halo_ref)
-    prepare_matrix(flow_ref, halo_ref, matrix_ref)
+    top = prepare_matrix(flow_ref, halo_ref, matrix_ref, rest_ref)
     speed_ref[...] = jnp.zeros_like(speed_ref)
-    couple(slots, table_ref, matrix_ref, total_ref, speed_ref)
-    finish_force(total_ref, halo_ref, force_ref, to_right_ref)
+    unscale = couple(slots, table_ref, matrix_ref, rest_ref, total_ref, speed_ref, top)
+    finish_force(unscale, total_ref, halo_ref, force_ref, to_right_ref)
     to_left_ref[0:24, :] = to_right_ref[0:24, :]
     mine = where_ref[1]
 
@@ -554,26 +585,19 @@
                     target[row : row + 1, :] = spot_ref[f * blocks + owner * share + k, c : c + 1, :]
 
 
-def last_still_kernel(post_ref, post_edge_ref, dev_ref, kept_ref, sems):
+def last_kernel(entries, post_ref, post_edge_ref, *refs):
+    planes = refs[:2]
+    refs = refs if entries is STILL else refs[3:]
+    dev_ref, kept_ref, sems = refs[:3]
+    moved_ref = None if entries is STILL else refs[3]
+
     def store(e, z, value):
-        kept_ref[STILL.index(e), 8 * z : 8 * z + 8, :] = value
+        kept_ref[entries.index(e), 8 * z : 8 * z + 8, :] = value
 
     copies = []
-    for k, e in enumerate(STILL):
-        stream((e,), post_ref, post_edge_ref, None, None, None, store, lambda e, value: None)
-        copies.append(pltpu.make_async_copy(kept_ref.at[k], dev_ref.at[e], sems.at[k]))
-        copies[-1].start()
-    for copy in copies:
-        copy.wait()
-
-
-def last_kernel(post_ref, post_edge_ref, east_ref, west_ref, old_ref, dev_ref, moved_ref, kept_ref, sems):
-    def store(e, z, value):
-        kept_ref[MOVING.index(e), 8 * z : 8 * z + 8, :] = value
-
-    copies = []
-    for k, e in enumerate(MOVING):
-        stream((e,), post_ref, post_edge_ref, east_ref, west_ref, moved_ref, store, lambda e, value: None)
+    for k, e in enumerate(entries):
+        plane_ref = planes[0 if e in EAST else 1]
+        stream((e,), post_ref, post_edge_ref, plane_ref, moved_ref, store, lambda e, value: None)
         copies.append(pltpu.make_async_copy(kept_ref.at[k], dev_ref.at[e], sems.at[k]))
         copies[-1].start()
     for copy in copies:
@@ -611,7 +635,7 @@
     filaments, _, share = fraction.shape
     blocks = spans.shape[1]
     share_blocks = share // BLOCK
-    slots = max(GROUP, 2 * filaments * blocks // columns)
+    slots = max(8, 2 * filaments * blocks // columns)
     f32 = jnp.float32
 
     own_part = fraction.reshape(filaments, 3, share_blocks, BLOCK).transpose(1, 2, 0, 3)
@@ -637,7 +661,8 @@
     table_shape = (slots, 16, BLOCK)
     coupling = [
         pltpu.VMEM(force_shape, f32),
-        pltpu.VMEM((3 * FIELDS * DEPTH, 512), jnp.bfloat16),
+        pltpu.VMEM((3 * FIELDS * DEPTH, 256), jnp.bfloat16),
+        pltpu.VMEM((3 * FIELDS * DEPTH, 256), f32),
         pltpu.VMEM((3 * FIELDS * DEPTH, 256), f32),
         pltpu.VMEM((slots, 8, BLOCK), f32),
     ]
@@ -649,44 +674,51 @@
         (flat_spans, where, stiffness, flow, right_edge, left_edge, *parts),
     )
 
-    plane = (5, 40, 128)
     moved = pltpu.VMEM((5, ROWS, 128), f32)
-
-    def collision(first, dev, force, force_edge, left, right):
-        post, post_edge, east, west = call(
-            functools.partial(collide_kernel, first),
-            [field, edge, plane, plane], [], 0, (*dev, force, force_edge, left, right),
+    side = (5, ROWS, 128)
+
+    def collision(first, dev, edges, force, to_right, to_left):
+        left, right = ring(to_right, "gy", 1), ring(to_left, "gy", -1)
+        post, east, west = call(
+            functools.partial(collide_kernel, first), [field, (PLANE, 128), (PLANE, 128)], [], 0, (*dev, force)
         )
-        return post, post_edge, ring(east, "gx", 1), ring(west, "gx", -1)
-
-    left, right = ring(to_right, "gy", 1), ring(to_left, "gy", -1)
-    post, post_edge, east, west = collision(True, (pop, own_edge), force, to_right, left, right)
-    still, still_edge = call(still_kernel, [(9, ROWS, 128), (9, 8, 128)], [], 0, (post, post_edge))
+        post_edge, east, west = call(
+            functools.partial(collide_edge_kernel, first), [edge, (PLANE_ROWS, 128), (PLANE_ROWS, 128)], [], 0,
+            (edges, to_right, left, right, east, west),
+        )
+        return post, post_edge, ring(east, "gx", 1), ring(west, "gx", -1), left, right
+
+    post, post_edge, east, west, _, _ = collision(True, (pop,), own_edge, force, to_right, to_left)
+    still, still_edge = call(
+        functools.partial(stream_kernel, STILL), [(9, ROWS, 128), (9, 8, 128)], [], 0, (post, post_edge)
+    )
+    east_dev, east_edge = call(
+        functools.partial(stream_kernel, EAST), [side, (5, 8, 128)], [moved], 0, (post, post_edge, east)
+    )
     dev, edges, force, to_right, to_left, *chunks = call(
         functools.partial(second_kernel, slots, blocks, columns),
-        [(10, ROWS, 128), edge, force_shape] + [(24 + share_rows, BLOCK)] * 2 + [(share_rows, BLOCK)] * (columns - 2),
+        [side, edge, force_shape] + [(24 + share_rows, BLOCK)] * 2 + [(share_rows, BLOCK)] * (columns - 2),
         [moved, pltpu.VMEM(force_shape, f32)] + coupling + [pltpu.VMEM((filaments * blocks, 8, BLOCK), f32)],
         2,
-        (flat_spans, where, post, post_edge, still, still_edge, east, west, table),
-    )
-    left, right = ring(to_right, "gy", 1), ring(to_left, "gy", -1)
-    post, post_edge, east, west = collision(False, (still, dev, edges), force, to_right, left, right)
+        (flat_spans, where, post, post_edge, still, still_edge, east_dev, east_edge, west, table),
+    )
+    post, post_edge, east, west, left, right = collision(
+        False, (still, east_dev, dev), edges, force, to_right, to_left
+    )
     speed = chunks[0] + left[24:] + right[24:]
     for s in range(2, columns - 1):
         speed = speed + ring(chunks[s - 1], "gy", s)
     speed = speed.reshape(3, share_blocks, filaments, BLOCK).transpose(2, 0, 1, 3).reshape(fraction.shape)
 
-    (dev,) = call(
-        last_still_kernel, [field],
-        [pltpu.VMEM((9, ROWS, 128), f32), pltpu.SemaphoreType.DMA((9,))],
-        0, (post, post_edge), out_specs=[anywhere],
-    )
-    (dev,) = call(
-        last_kernel, [field],
-        [moved, pltpu.VMEM((10, ROWS, 128), f32), pltpu.SemaphoreType.DMA((10,))],
-        0, (post, post_edge, east, west, dev),
-        in_specs=[inside] * 4 + [anywhere], out_specs=[anywhere], input_output_aliases={4: 0},
-    )
+    dev = None
+    for entries in (STILL, EAST + WEST):
+        count = len(entries)
+        scratch = [pltpu.VMEM((count, ROWS, 128), f32), pltpu.SemaphoreType.DMA((count,))]
+        extra, args = {}, (post, post_edge)
+        if entries is not STILL:
+            scratch, args = scratch + [moved], args + (east, west, dev)
+            extra = dict(in_specs=[inside] * 4 + [anywhere], input_output_aliases={4: 0})
+        (dev,) = call(functools.partial(last_kernel, entries), [field], scratch, 0, args, out_specs=[anywhere], **extra)
     dev = dev.reshape(19, depth, halves, tile_x, 128).transpose(0, 1, 3, 2, 4).reshape(populations.shape)
     return dev, speed
 

time: 48 us -> 45 us (0.938)
  waiting for transfers between devices: 12 us -> 9.39 us
    ppermute x12, waiting for transfers between devices: 12 us -> 9.39 us  [ring(): lax.ppermute(value, axis, [(i, (i + step) % count) for i in range(count)])]
    pallas_call x9 -> x12, Pallas kernels: 16.5 us -> 16.3 us  [call(): pl.pallas_call(body, out_shape=[jax.ShapeDtypeStruct(shape, jnp.float32)...]
  transfers between devices with their start and end apart: 12 -> 12, of which waited for: 10 -> 9; matrix products, arithmetic and copies ran while one was open for 4% -> 4% of each run, Pallas kernels for 5% -> 8%
where the time goes in v4:
time: 45 us; the launch traced here: 44.8 us
  Pallas kernels  16.3 us (36%)
  starting transfers between devices  14.4 us (32%)
  waiting for transfers between devices  9.39 us (21%)
  local copies, waits for them, and re-layouts  2.63 us (6%)
  other arithmetic  1.36 us (3%)
  between operations  0.74 us (2%)
    pallas_call x12, Pallas kernels, call(): pl.pallas_call(body, out_shape=[jax.ShapeDtypeStruct(shape, jnp.float32)...  16.3 us
    ppermute x12, starting transfers between devices, ring(): lax.ppermute(value, axis, [(i, (i + step) % count) for i in range(count)])  14.4 us
    ppermute x12, waiting for transfers between devices, ring(): lax.ppermute(value, axis, [(i, (i + step) % count) for i in range(count)])  9.39 us
    unnamed x11, local copies, waits for them, and re-layouts  2.55 us
  transfers between devices with their start and end apart: 12, of which 9 were waited for; matrix products, arithmetic and copies ran while one was open for 4% of the time, Pallas kernels for 8%

profile of v4, /device:TPU:0, one launch (start us, length us, event | category | flops | bytes accessed | tf_op | source)
XLA Modules:
  0.0 44.8 jit_solution(13128175630134466052)
XLA Ops:
  0.6 1.3 %copy-done = f32[19,16,4,256]{3,2,1,0:T(4,128)S(1)} copy-done((f32[19,16,4,256]{3,2,1,0:T(4,128)S(1)}, f32[19,16,4,256]{3,2,1,0:T(4,128)}, u32[]{:S(2)}) %copy-start) | copy-done | bytes 1245208
  1.9 0.7 %copy-done.2 = f32[2,3,1024]{2,0,1:T(2,128)S(1)} copy-done((f32[2,3,1024]{2,0,1:T(2,128)S(1)}, f32[2,3,1024]{2,0,1:T(2,128)}, u32[]{:S(2)}) %copy-start.2) | copy-done | bytes 24600
  2.7 0.2 shard_map.59
  2.9 2.4 %collective-permute-start.2 = (f32[72,128]{1,0:T(8,128)S(1)}, f32[72,128]{1,0:T(8,128)S(1)}, u32[]{:S(2)}, u32[]{:S(2)}) collective-permute-start(f32[72,128]{1,0:T(8,128)S(1)} %get-tuple-element.37.refs_0_), channel_id=1, source_target_pairs={{0,3},{1,0},{2,1},{3,2},{4,7},{5,4},{6,5},{7,6},{8,11},{9,8},{10,9... | collective-permute-start | bytes 110600 | tf_op jit(solution)/shard_map/ppermute | solution.py:628
  5.3 0.6 %collective-permute-start.1 = (f32[72,128]{1,0:T(8,128)S(1)}, f32[72,128]{1,0:T(8,128)S(1)}, u32[]{:S(2)}, u32[]{:S(2)}) collective-permute-start(f32[72,128]{1,0:T(8,128)S(1)} %get-tuple-element.37.refs_0_), channel_id=1, source_target_pairs={{0,2},{1,3},{2,0},{3,1},{4,6},{5,7},{6,4},{7,5},{8,10},{9,11},{10,... | collective-permute-start | bytes 110600 | tf_op jit(solution)/shard_map/ppermute | solution.py:628
  6.2 0.4 shard_map.60
  6.6 0.5 %broadcast.3 = s32[]{:T(128)} broadcast(s32[]{:T(128)} %constant.20), dimensions={} | broadcast | bytes 8 | tf_op args[2]
  7.1 0.7 %reduce.3 = s32[2,32]{1,0:T(2,128)S(1)} reduce(s32[2,32,1]{1,2,0:T(1,128)S(1)} %copy-done.4, s32[]{:T(128)} %broadcast.3), dimensions={2}, to_apply=%param.6.reduce_sub_computation.3 | reduce | bytes 516 | tf_op args[2]
  7.9 1.7 %collective-permute-done.1.refs_2_ = f32[72,128]{1,0:T(8,128)S(1)} collective-permute-done((f32[72,128]{1,0:T(8,128)S(1)}, f32[72,128]{1,0:T(8,128)S(1)}, u32[]{:S(2)}, u32[]{:S(2)}) %collective-permute-start.1) | collective-permute-done | bytes 36896 | tf_op jit(solution)/shard_map/ppermute | solution.py:628
  9.7 5.7 %shard_map.61 = (f32[3,128,128]{2,1,0:T(8,128)S(1)}, f32[104,128]{1,0:T(8,128)S(1)}, f32[104,128]{1,0:T(8,128)S(1)}, f32[32,16,128]{2,1,0:T(8,128)S(1)}) custom-call(s32[64]{0:T(128)S(1)} %reshape.33.spans_ref, s32[2]{0:T(128)S(1)} %pad_add_fusion.where_ref, s32[2]{0:T(128)S(1)} %copy-done.3, f32[3,128,128]{2,1,0:T(8,128)S(1)} %get-tuple-element.34.flow_ref, ...), custom_call_target="tpu_custom_call" | custom-call | bytes 1130496 | tf_op jit(solution)/shard_map/pallas_call | solution.py:617
  15.5 0.5 %collective-permute-start.3 = (f32[104,128]{1,0:T(8,128)S(1)}, f32[104,128]{1,0:T(8,128)S(1)}, u32[]{:S(2)}, u32[]{:S(2)}) collective-permute-start(f32[104,128]{1,0:T(8,128)S(1)} %get-tuple-element.41.own_ref), channel_id=1, source_target_pairs={{0,1},{1,2},{2,3},{3,0},{4,5},{5,6},{6,7},{7,4},{8,9},{9,10},{10,1... | collective-permute-start | bytes 159752 | tf_op jit(solution)/shard_map/ppermute | solution.py:628
  16.0 0.5 %shard_map.62 = (f32[19,128,128]{2,1,0:T(8,128)S(1)}, f32[160,128]{1,0:T(8,128)S(1)}, f32[160,128]{1,0:T(8,128)S(1)}) custom-call(f32[19,128,128]{2,1,0:T(8,128)S(1)} %bitcast.25, f32[3,128,128]{2,1,0:T(8,128)S(1)} %get-tuple-element.38.refs_1_), custom_call_target="tpu_custom_call" | custom-call | bytes 2818048 | tf_op jit(solution)/shard_map/pallas_call | solution.py:617
  16.5 0.8 %collective-permute-done.4.right_ref = f32[104,128]{1,0:T(8,128)S(1)} collective-permute-done((f32[104,128]{1,0:T(8,128)S(1)}, f32[104,128]{1,0:T(8,128)S(1)}, u32[]{:S(2)}, u32[]{:S(2)}) %collective-permute-start.4) | collective-permute-done | bytes 53280 | tf_op jit(solution)/shard_map/ppermute | solution.py:628
  17.3 2.1 %collective-permute-done.3.left_ref = f32[104,128]{1,0:T(8,128)S(1)} collective-permute-done((f32[104,128]{1,0:T(8,128)S(1)}, f32[104,128]{1,0:T(8,128)S(1)}, u32[]{:S(2)}, u32[]{:S(2)}) %collective-permute-start.3) | collective-permute-done | bytes 53280 | tf_op jit(solution)/shard_map/ppermute | solution.py:628
  19.4 1.6 %collective-permute-start.5 = (f32[176,128]{1,0:T(8,128)S(1)}, f32[176,128]{1,0:T(8,128)S(1)}, u32[]{:S(2)}, u32[]{:S(2)}) collective-permute-start(f32[176,128]{1,0:T(8,128)S(1)} %get-tuple-element.47), channel_id=1, source_target_pairs={{0,4},{4,8},{8,12},{12,16},{16,20},{20,24},{24,28},{28,0},{1,5},{5... | collective-permute-start | bytes 270344 | tf_op jit(solution)/shard_map/ppermute | solution.py:628
  21.0 3.2 %collective-permute-start.6 = (f32[176,128]{1,0:T(8,128)S(1)}, f32[176,128]{1,0:T(8,128)S(1)}, u32[]{:S(2)}, u32[]{:S(2)}) collective-permute-start(f32[176,128]{1,0:T(8,128)S(1)} %get-tuple-element.51), channel_id=1, source_target_pairs={{0,28},{4,0},{8,4},{12,8},{16,12},{20,16},{24,20},{28,24},{1,29},{... | collective-permute-start | bytes 270344 | tf_op jit(solution)/shard_map/ppermute | solution.py:628
  24.2 0.6 %shard_map.64 = (f32[9,128,128]{2,1,0:T(8,128)S(1)}, f32[9,8,128]{2,1,0:T(8,128)S(1)}) custom-call(f32[19,128,128]{2,1,0:T(8,128)S(1)} %get-tuple-element.39.post_ref, f32[19,8,128]{2,1,0:T(8,128)S(1)} %get-tuple-element.45.post_edge_ref), custom_call_target="tpu_custom_call" | custom-call | bytes 1253376 | tf_op jit(solution)/shard_map/pallas_call | solution.py:617
  24.8 1.9 %collective-permute-done.5.refs_0_ = f32[176,128]{1,0:T(8,128)S(1)} collective-permute-done((f32[176,128]{1,0:T(8,128)S(1)}, f32[176,128]{1,0:T(8,128)S(1)}, u32[]{:S(2)}, u32[]{:S(2)}) %collective-permute-start.5) | collective-permute-done | bytes 90144 | tf_op jit(solution)/shard_map/ppermute | solution.py:628
  26.7 0.3 shard_map.65
  27.0 0.4 collective-permute-done.6.west_ref
  27.4 5.2 %shard_map.66 = (f32[5,128,128]{2,1,0:T(8,128)S(1)}, f32[19,8,128]{2,1,0:T(8,128)S(1)}, f32[3,128,128]{2,1,0:T(8,128)S(1)}, f32[72,128]{1,0:T(8,128)S(1)}, f32[7...) custom-call(s32[64]{0:T(128)S(1)} %reshape.33.spans_ref, s32[2]{0:T(128)S(1)} %pad_add_fusion.where_ref, ...), custom_call_target="tpu_custom_call" | custom-call | bytes 1449984 | tf_op jit(solution)/shard_map/pallas_call | solution.py:617
  32.7 0.5 %collective-permute-start.7 = (f32[72,128]{1,0:T(8,128)S(1)}, f32[72,128]{1,0:T(8,128)S(1)}, u32[]{:S(2)}, u32[]{:S(2)}) collective-permute-start(f32[72,128]{1,0:T(8,128)S(1)} %get-tuple-element.57.own_ref), channel_id=1, source_target_pairs={{0,1},{1,2},{2,3},{3,0},{4,5},{5,6},{6,7},{7,4},{8,9},{9,10},{10,1... | collective-permute-start | bytes 110600 | tf_op jit(solution)/shard_map/ppermute | solution.py:628
  33.2 0.5 %collective-permute-start.11 = (f32[48,128]{1,0:T(8,128)S(1)}, f32[48,128]{1,0:T(8,128)S(1)}, u32[]{:S(2)}, u32[]{:S(2)}) collective-permute-start(f32[48,128]{1,0:T(8,128)S(1)} %get-tuple-element.65), channel_id=1, source_target_pairs={{0,2},{1,3},{2,0},{3,1},{4,6},{5,7},{6,4},{7,5},{8,10},{9,11},{10,... | collective-permute-start | bytes 73736 | tf_op jit(solution)/shard_map/ppermute | solution.py:628
  33.7 0.5 %shard_map.67 = (f32[19,128,128]{2,1,0:T(8,128)S(1)}, f32[160,128]{1,0:T(8,128)S(1)}, f32[160,128]{1,0:T(8,128)S(1)}) custom-call(f32[9,128,128]{2,1,0:T(8,128)S(1)} %get-tuple-element.46.still_ref.refs_0_, f32[5,128,128]{2,1,0:T(8,128)S(1)} %get-tuple-element.48.east_dev_ref.refs_1_, f32[5,128,128]{2,1,0:T(8,128)S(1)} %get-tuple-element.53.refs_2_, ...), custom_call_target="tpu_custom_call" | custom-call | bytes 2818048 | tf_op jit(solution)/shard_map/pallas_call | solution.py:617
  34.2 0.3 collective-permute-done.8.right_ref
  34.5 1.6 %collective-permute-done.7.left_ref = f32[72,128]{1,0:T(8,128)S(1)} collective-permute-done((f32[72,128]{1,0:T(8,128)S(1)}, f32[72,128]{1,0:T(8,128)S(1)}, u32[]{:S(2)}, u32[]{:S(2)}) %collective-permute-start.7) | collective-permute-done | bytes 36896 | tf_op jit(solution)/shard_map/ppermute | solution.py:628
  36.2 0.5 %collective-permute-start.9 = (f32[176,128]{1,0:T(8,128)S(1)}, f32[176,128]{1,0:T(8,128)S(1)}, u32[]{:S(2)}, u32[]{:S(2)}) collective-permute-start(f32[176,128]{1,0:T(8,128)S(1)} %get-tuple-element.62), channel_id=1, source_target_pairs={{0,4},{4,8},{8,12},{12,16},{16,20},{20,24},{24,28},{28,0},{1,5},{5... | collective-permute-start | bytes 270344 | tf_op jit(solution)/shard_map/ppermute | solution.py:628
  36.7 4.2 %collective-permute-start.10 = (f32[176,128]{1,0:T(8,128)S(1)}, f32[176,128]{1,0:T(8,128)S(1)}, u32[]{:S(2)}, u32[]{:S(2)}) collective-permute-start(f32[176,128]{1,0:T(8,128)S(1)} %get-tuple-element.63), channel_id=1, source_target_pairs={{0,28},{4,0},{8,4},{12,8},{16,12},{20,16},{24,20},{28,24},{1,29},{... | collective-permute-start | bytes 270344 | tf_op jit(solution)/shard_map/ppermute | solution.py:628
  41.0 0.6 %fusion = f32[48,128]{1,0:T(8,128)} fusion(f32[48,128]{1,0:T(8,128)S(1)} %collective-permute-done.11, f32[72,128]{1,0:T(8,128)S(1)} %collective-permute-done.8.right_ref, f32[48,128]{1,0:T(8,128)S(1)} %get-tuple-element.64, f32[72,128]{1,0:T(8,128)S(1)} %collective-permute-done.7.left_ref), kind=kLoop, calls=%fused_computation.1 | loop fusion | flops 18432 | bytes 122880 | tf_op jit(solution)/shard_map/add | solution.py:710
  41.6 1.4 %shard_map.69.refs_2_ = f32[19,128,128]{2,1,0:T(8,128)} custom-call(f32[19,128,128]{2,1,0:T(8,128)S(1)} %get-tuple-element.55.post_ref, f32[19,8,128]{2,1,0:T(8,128)S(1)} %get-tuple-element.61.post_edge_ref), custom_call_target="tpu_custom_call" | custom-call | bytes 2490368 | tf_op jit(solution)/shard_map/pallas_call | solution.py:617
  42.9 0.5 %collective-permute-done.9.refs_0_ = f32[176,128]{1,0:T(8,128)S(1)} collective-permute-done((f32[176,128]{1,0:T(8,128)S(1)}, f32[176,128]{1,0:T(8,128)S(1)}, u32[]{:S(2)}, u32[]{:S(2)}) %collective-permute-start.9) | collective-permute-done | bytes 90144 | tf_op jit(solution)/shard_map/ppermute | solution.py:628
  43.5 1.3 %shard_map.70 = f32[19,128,128]{2,1,0:T(8,128)} custom-call(f32[19,128,128]{2,1,0:T(8,128)S(1)} %get-tuple-element.55.post_ref, f32[19,8,128]{2,1,0:T(8,128)S(1)} %get-tuple-element.61.post_edge_ref, f32[176,128]{1,0:T(8,128)S(1)} %collective-permute-done.9.refs_0_, f32[176,128]{1,0:T(8,128)S(1)} %collective-permute-done.10.refs_1_, ...), custom_call_target="tpu_custom_call", output_to_operand_aliasing={{}: (4, {})} | custom-call | bytes 2490368 | tf_op jit(solution)/shard_map/pallas_call | solution.py:617
  (19 shorter events, 0.6 us)
Async XLA Ops:
  0.6 1.3 %copy-start = (f32[19,16,4,256]{3,2,1,0:T(4,128)S(1)}, f32[19,16,4,256]{3,2,1,0:T(4,128)}, u32[]{:S(2)}) copy-start(f32[19,16,4,256]{3,2,1,0:T(4,128)} %param.4) | copy-start | bytes 3735556
  1.9 0.7 %copy-start.2 = (f32[2,3,1024]{2,0,1:T(2,128)S(1)}, f32[2,3,1024]{2,0,1:T(2,128)}, u32[]{:S(2)}) copy-start(f32[2,3,1024]{2,0,1:T(2,128)} %param.5) | copy-start | bytes 73732
  2.7 3.6 %copy-start.1 = (f32[19,16,4,256]{3,2,1,0:T(4,128)S(1)}, f32[19,16,4,256]{3,2,1,0:T(4,128)}, u32[]{:S(2)}) copy-start(f32[19,16,4,256]{3,2,1,0:T(4,128)} %param.4) | copy-start | bytes 3735556
  2.7 4.5 %copy-start.4 = (s32[2,32,1]{1,2,0:T(1,128)S(1)}, s32[2,32,1]{1,2,0:T(1,128)}, u32[]{:S(2)}) copy-start(s32[2,32,1]{1,2,0:T(1,128)} %param.6) | copy-start | bytes 772
  2.7 7.0 %copy-start.3 = (s32[2]{0:T(128)S(1)}, s32[2]{0:T(128)}, u32[]{:S(2)}) copy-start(s32[2]{0:T(128)} %stiff_ref.1) | copy-start | bytes 28
  2.9 5.0 %collective-permute-start.2 = (f32[72,128]{1,0:T(8,128)S(1)}, f32[72,128]{1,0:T(8,128)S(1)}, u32[]{:S(2)}, u32[]{:S(2)}) collective-permute-start(f32[72,128]{1,0:T(8,128)S(1)} %get-tuple-element.37.refs_0_), channel_id=1, source_target_pairs={{0,3},{1,0},{2,1},{3,2},{4,7},{5,4},{6,5},{7,6},{8,11},{9,8},{10,9... | collective-permute-start | bytes 110600 | tf_op jit(solution)/shard_map/ppermute | solution.py:628
  5.3 4.3 %collective-permute-start.1 = (f32[72,128]{1,0:T(8,128)S(1)}, f32[72,128]{1,0:T(8,128)S(1)}, u32[]{:S(2)}, u32[]{:S(2)}) collective-permute-start(f32[72,128]{1,0:T(8,128)S(1)} %get-tuple-element.37.refs_0_), channel_id=1, source_target_pairs={{0,2},{1,3},{2,0},{3,1},{4,6},{5,7},{6,4},{7,5},{8,10},{9,11},{10,... | collective-permute-start | bytes 110600 | tf_op jit(solution)/shard_map/ppermute | solution.py:628
  6.0 3.7 %collective-permute-start = (f32[72,128]{1,0:T(8,128)S(1)}, f32[72,128]{1,0:T(8,128)S(1)}, u32[]{:S(2)}, u32[]{:S(2)}) collective-permute-start(f32[72,128]{1,0:T(8,128)S(1)} %get-tuple-element.37.refs_0_), channel_id=1, source_target_pairs={{0,1},{1,2},{2,3},{3,0},{4,5},{5,6},{6,7},{7,4},{8,9},{9,10},{10,1... | collective-permute-start | bytes 110600 | tf_op jit(solution)/shard_map/ppermute | solution.py:628
  15.4 1.8 %collective-permute-start.4 = (f32[104,128]{1,0:T(8,128)S(1)}, f32[104,128]{1,0:T(8,128)S(1)}, u32[]{:S(2)}, u32[]{:S(2)}) collective-permute-start(f32[104,128]{1,0:T(8,128)S(1)} %get-tuple-element.42), channel_id=1, source_target_pairs={{0,3},{1,0},{2,1},{3,2},{4,7},{5,4},{6,5},{7,6},{8,11},{9,8},{10,9... | collective-permute-start | bytes 159752 | tf_op jit(solution)/shard_map/ppermute | solution.py:628
  15.5 3.8 %collective-permute-start.3 = (f32[104,128]{1,0:T(8,128)S(1)}, f32[104,128]{1,0:T(8,128)S(1)}, u32[]{:S(2)}, u32[]{:S(2)}) collective-permute-start(f32[104,128]{1,0:T(8,128)S(1)} %get-tuple-element.41.own_ref), channel_id=1, source_target_pairs={{0,1},{1,2},{2,3},{3,0},{4,5},{5,6},{6,7},{7,4},{8,9},{9,10},{10,1... | collective-permute-start | bytes 159752 | tf_op jit(solution)/shard_map/ppermute | solution.py:628
  19.4 7.3 %collective-permute-start.5 = (f32[176,128]{1,0:T(8,128)S(1)}, f32[176,128]{1,0:T(8,128)S(1)}, u32[]{:S(2)}, u32[]{:S(2)}) collective-permute-start(f32[176,128]{1,0:T(8,128)S(1)} %get-tuple-element.47), channel_id=1, source_target_pairs={{0,4},{4,8},{8,12},{12,16},{16,20},{20,24},{24,28},{28,0},{1,5},{5... | collective-permute-start | bytes 270344 | tf_op jit(solution)/shard_map/ppermute | solution.py:628
  21.0 6.5 %collective-permute-start.6 = (f32[176,128]{1,0:T(8,128)S(1)}, f32[176,128]{1,0:T(8,128)S(1)}, u32[]{:S(2)}, u32[]{:S(2)}) collective-permute-start(f32[176,128]{1,0:T(8,128)S(1)} %get-tuple-element.51), channel_id=1, source_target_pairs={{0,28},{4,0},{8,4},{12,8},{16,12},{20,16},{24,20},{28,24},{1,29},{... | collective-permute-start | bytes 270344 | tf_op jit(solution)/shard_map/ppermute | solution.py:628
  32.6 1.9 %collective-permute-start.8 = (f32[72,128]{1,0:T(8,128)S(1)}, f32[72,128]{1,0:T(8,128)S(1)}, u32[]{:S(2)}, u32[]{:S(2)}) collective-permute-start(f32[72,128]{1,0:T(8,128)S(1)} %get-tuple-element.58), channel_id=1, source_target_pairs={{0,3},{1,0},{2,1},{3,2},{4,7},{5,4},{6,5},{7,6},{8,11},{9,8},{10,9... | collective-permute-start | bytes 110600 | tf_op jit(solution)/shard_map/ppermute | solution.py:628
  32.7 3.4 %collective-permute-start.7 = (f32[72,128]{1,0:T(8,128)S(1)}, f32[72,128]{1,0:T(8,128)S(1)}, u32[]{:S(2)}, u32[]{:S(2)}) collective-permute-start(f32[72,128]{1,0:T(8,128)S(1)} %get-tuple-element.57.own_ref), channel_id=1, source_target_pairs={{0,1},{1,2},{2,3},{3,0},{4,5},{5,6},{6,7},{7,4},{8,9},{9,10},{10,1... | collective-permute-start | bytes 110600 | tf_op jit(solution)/shard_map/ppermute | solution.py:628
  33.2 7.8 %collective-permute-start.11 = (f32[48,128]{1,0:T(8,128)S(1)}, f32[48,128]{1,0:T(8,128)S(1)}, u32[]{:S(2)}, u32[]{:S(2)}) collective-permute-start(f32[48,128]{1,0:T(8,128)S(1)} %get-tuple-element.65), channel_id=1, source_target_pairs={{0,2},{1,3},{2,0},{3,1},{4,6},{5,7},{6,4},{7,5},{8,10},{9,11},{10,... | collective-permute-start | bytes 73736 | tf_op jit(solution)/shard_map/ppermute | solution.py:628
  36.2 7.3 %collective-permute-start.9 = (f32[176,128]{1,0:T(8,128)S(1)}, f32[176,128]{1,0:T(8,128)S(1)}, u32[]{:S(2)}, u32[]{:S(2)}) collective-permute-start(f32[176,128]{1,0:T(8,128)S(1)} %get-tuple-element.62), channel_id=1, source_target_pairs={{0,4},{4,8},{8,12},{12,16},{16,20},{20,24},{24,28},{28,0},{1,5},{5... | collective-permute-start | bytes 270344 | tf_op jit(solution)/shard_map/ppermute | solution.py:628
  36.7 6.7 %collective-permute-start.10 = (f32[176,128]{1,0:T(8,128)S(1)}, f32[176,128]{1,0:T(8,128)S(1)}, u32[]{:S(2)}, u32[]{:S(2)}) collective-permute-start(f32[176,128]{1,0:T(8,128)S(1)} %get-tuple-element.63), channel_id=1, source_target_pairs={{0,28},{4,0},{8,4},{12,8},{16,12},{20,16},{24,20},{28,24},{1,29},{... | collective-permute-start | bytes 270344 | tf_op jit(solution)/shard_map/ppermute | solution.py:628

commit v5 on v4

--- a/solution.py
+++ b/solution.py
@@ -134,8 +134,18 @@
     copy.wait()
 
 
-def edge_kernel(pop_ref, edge_ref, to_right_ref, to_left_ref):
+def edge_kernel(spans_ref, where_ref, pop_ref, edge_ref, to_right_ref, to_left_ref, chosen_ref):
     row, _ = iotas()
+    filaments, _, blocks = spans_ref.shape
+    slots, mine = chosen_ref.shape[0] - 8, where_ref[1]
+    count = jnp.int32(0)
+    for f in range(filaments):
+        for k in range(blocks):
+            chosen_ref[count] = f * blocks + k
+            count = count + (spans_ref[f, 0, k] == mine).astype(jnp.int32)
+    for n in range(slots):
+        chosen_ref[n] = jnp.where(n < count, chosen_ref[n], filaments * blocks)
+    chosen_ref[slots] = count
     edges = []
     for e in range(19):
         edges.append(pack_edges(lambda z: pop_ref[e, 8 * z : 8 * z + 8, :]))
@@ -191,7 +201,7 @@
                 flow_ref[c, pl.ds(4 + x, DEPTH, stride=8), :],
                 halo_ref[c, pl.ds(x, DEPTH, stride=8), :],
             ]
-            per_x.append([tile * scale for tile in tiles])
+            per_x.append(tiles)
         by_basis = [basis_fields([per_x[x][t] for x in range(4)]) for t in range(4)]
         for xf in range(3):
             tiles = [by_basis[t][xf] for t in range(4)]
@@ -201,9 +211,10 @@
                 columns = slice(half * 128, half * 128 + 128)
                 for yf in range(3):
                     row = ((c * 3 + yf) * 3 + xf) * DEPTH
-                    high = fields[yf].astype(jnp.bfloat16)
+                    value = fields[yf] * scale
+                    high = value.astype(jnp.bfloat16)
                     matrix_ref[row : row + DEPTH, columns] = high
-                    rest_ref[row : row + DEPTH, columns] = fields[yf] - high.astype(jnp.float32)
+                    rest_ref[row : row + DEPTH, columns] = value - high.astype(jnp.float32)
     return top
 
 
@@ -334,7 +345,7 @@
             halo_ref[c, 8 * z : 8 * z + 8, :] = turn(flow, -(5 * z + 2), 1)
 
 
-def gather_markers(span_y, slots, filaments, share, spans_ref, where_ref, stiff_ref, part_refs, places_ref, picked_ref, table_ref):
+def gather_markers(span_y, slots, filaments, share, spans_ref, where_ref, chosen_ref, stiff_ref, part_refs, places_ref, picked_ref, table_ref):
     columns = len(part_refs)
     blocks = share * columns
     block, lane = iotas((blocks, BLOCK))
@@ -346,7 +357,7 @@
         for f in range(filaments):
             for k in range(share):
                 index = f * blocks + source * share + k
-                span = (spans_ref[index] * 256).astype(jnp.float32)
+                span = (spans_ref[f, 0, source * share + k] * 256).astype(jnp.float32)
                 row = lambda c: part_refs[s][(c * share + k) * filaments + f][None, :]
                 start = pl.multiple_of(index * 8, 8)
                 three = [anchor + 1.0 + row(0) * (4 - 3.01), span + row(1) * 256.0, 1.0 + row(2) * (DEPTH - 3.01)]
@@ -367,15 +378,11 @@
             places_ref[pl.ds(start + 3 + c, blocks, stride=8), :] = (ahead - behind) * factor
         places_ref[pl.ds(start, blocks, stride=8), :] = places[0] - anchor
         places_ref[pl.ds(start + 1, blocks, stride=8), :] = places[1] - tile_start
-    picked_ref[...] = jnp.zeros_like(picked_ref)
-
-    def pick(index, count):
-        source = pl.multiple_of(index * 8, 8)
-        target = pl.multiple_of(count * 8, 8)
-        picked_ref[pl.ds(target, 8), :] = places_ref[pl.ds(source, 8), :]
-        return count + (spans_ref[index] == mine).astype(jnp.int32)
-
-    count = lax.fori_loop(0, filaments * blocks, pick, jnp.int32(0), unroll=8)
+    total = filaments * blocks
+    places_ref[pl.ds(total * 8, 8), :] = jnp.zeros((8, BLOCK), jnp.float32)
+    for n in range(slots):
+        picked_ref[8 * n : 8 * n + 8, :] = places_ref[pl.ds(pl.multiple_of(chosen_ref[n] * 8, 8), 8), :]
+    count = chosen_ref[slots]
     got = lambda k: picked_ref[pl.ds(k, slots, stride=8), :]
     slot, _ = iotas((slots, BLOCK))
 
@@ -383,7 +390,13 @@
         table_ref[:, k, :] = value
 
     def basis(t):
-        return jnp.cos((0.5 * math.pi) * (1.0 - t)), jnp.cos((0.5 * math.pi) * t)
+        square = t * t
+        sine = cosine = None
+        for k in range(6, -1, -1):
+            a, b = ((-1) ** k * (0.5 * math.pi) ** n / math.factorial(n) for n in (2 * k + 1, 2 * k))
+            sine = a if sine is None else sine * square + a
+            cosine = b if cosine is None else cosine * square + b
+        return sine * t, cosine
 
     y = got(1)
     base = jnp.minimum(jnp.floor(y), 255.0)
@@ -408,15 +421,15 @@
     table_ref[0, 12:13, :] = jnp.broadcast_to(top, (1, BLOCK))
 
 
-def first_kernel(span_y, slots, filaments, columns, spans_ref, where_ref, stiff_ref, flow_ref, right_edge_ref, left_edge_ref, *refs):
+def first_kernel(span_y, slots, filaments, columns, spans_ref, where_ref, chosen_ref, stiff_ref, flow_ref, right_edge_ref, left_edge_ref, *refs):
     part_refs, refs = refs[:columns], refs[columns:]
     force_ref, to_right_ref, to_left_ref, table_ref = refs[:4]
     halo_ref, matrix_ref, rest_ref, total_ref, speed_ref, places_ref, picked_ref = refs[4:]
-    share = spans_ref.shape[0] // (filaments * columns)
+    share = spans_ref.shape[2] // columns
     to_right_ref[0:EDGE_ROWS, :] = right_edge_ref[...]
     to_left_ref[0:EDGE_ROWS, :] = left_edge_ref[...]
     gather_markers(
-        span_y, slots, filaments, share, spans_ref, where_ref, stiff_ref, part_refs, places_ref, picked_ref, table_ref
+        span_y, slots, filaments, share, spans_ref, where_ref, chosen_ref, stiff_ref, part_refs, places_ref, picked_ref, table_ref
     )
     flows = []
     for c in range(3):
@@ -532,7 +545,7 @@
 
 
 def second_kernel(
-    slots, blocks, columns, spans_ref, where_ref,
+    slots, blocks, columns, where_ref, chosen_ref,
     post_ref, post_edge_ref, still_ref, still_edge_ref, east_dev_ref, east_edge_ref, west_ref, table_ref, *refs
 ):
     dev_ref, edges_ref, force_ref, to_right_ref, to_left_ref = refs[:5]
@@ -559,19 +572,15 @@
     flow_slices(lambda z: [dev(e, z) for e in range(19)], flow_ref)
     flow_edges(edge_flow([edges_ref[e] for e in range(19)]), halo_ref)
     top = prepare_matrix(flow_ref, halo_ref, matrix_ref, rest_ref)
-    speed_ref[...] = jnp.zeros_like(speed_ref)
     unscale = couple(slots, table_ref, matrix_ref, rest_ref, total_ref, speed_ref, top)
     finish_force(unscale, total_ref, halo_ref, force_ref, to_right_ref)
     to_left_ref[0:24, :] = to_right_ref[0:24, :]
     mine = where_ref[1]
 
-    def place(index, count):
-        here = spans_ref[index] == mine
-        spot_ref[index] = jnp.where(here, speed_ref[jnp.minimum(count, slots - 1)], 0.0)
-        return count + here.astype(jnp.int32)
-
-    total = spans_ref.shape[0]
-    lax.fori_loop(0, total, place, jnp.int32(0), unroll=8)
+    total = spot_ref.shape[0] - 1
+    spot_ref[...] = jnp.zeros_like(spot_ref)
+    for n in range(slots):
+        spot_ref[chosen_ref[n]] = speed_ref[n]
     filaments = total // blocks
     share = blocks // columns
     others = iter(share_refs)
@@ -607,7 +616,8 @@
 def call(body, outs, scratch, n_smem, args, flops=0, **extra):
     spec = [pl.BlockSpec(memory_space=pltpu.SMEM)] * n_smem
     spec += [pl.BlockSpec(memory_space=pltpu.VMEM)] * (len(args) - n_smem)
-    moved = 4 * sum(math.prod(shape) for shape in outs)
+    outs = [out if isinstance(out[-1], type) else (out, jnp.float32) for out in outs]
+    moved = 4 * sum(math.prod(shape) for shape, _ in outs)
     options = dict(
         in_specs=spec,
         out_specs=[pl.BlockSpec(memory_space=pltpu.VMEM)] * len(outs),
@@ -616,7 +626,7 @@
     options.update(extra)
     return pl.pallas_call(
         body,
-        out_shape=[jax.ShapeDtypeStruct(shape, jnp.float32) for shape in outs],
+        out_shape=[jax.ShapeDtypeStruct(*out) for out in outs],
         scratch_shapes=scratch,
         compiler_params=pltpu.CompilerParams(vmem_limit_bytes=VMEM_LIMIT),
         **options,
@@ -645,7 +655,7 @@
     edge = (19, 8, 128)
     halves = tile_y // 128
     pop = populations.reshape(19, depth, tile_x, halves, 128).transpose(0, 1, 3, 2, 4).reshape(field)
-    flat_spans = spans.reshape(-1)
+    flat_spans = spans.transpose(0, 2, 1)
     where = jnp.stack([lax.axis_index("gx"), lax.axis_index("gy")]).astype(jnp.int32)
 
     force_shape = (3, ROWS, 128)
@@ -656,7 +666,11 @@
         in_specs=[inside, anywhere],
     )
     parts = [payload] + [ring(payload, "gy", s) for s in range(1, columns)]
-    own_edge, right_edge, left_edge = call(edge_kernel, [edge, (EDGE_ROWS, 128), (EDGE_ROWS, 128)], [], 0, (pop,))
+    edge_shapes = [edge, (EDGE_ROWS, 128), (EDGE_ROWS, 128)]
+    own_edge, right_edge, left_edge, chosen = call(
+        edge_kernel, edge_shapes + [((slots + 8,), jnp.int32)], [], 2, (flat_spans, where, pop),
+        out_specs=[inside] * 3 + [pl.BlockSpec(memory_space=pltpu.SMEM)],
+    )
 
     table_shape = (slots, 16, BLOCK)
     coupling = [
@@ -669,9 +683,9 @@
     force, to_right, to_left, table = call(
         functools.partial(first_kernel, span_y, slots, filaments, columns),
         [force_shape, (EDGE_ROWS + 24, 128), (EDGE_ROWS + 24, 128), table_shape],
-        coupling + [pltpu.VMEM((filaments * blocks * 8, BLOCK), f32), pltpu.VMEM(((slots + 1) * 8, BLOCK), f32)],
-        3,
-        (flat_spans, where, stiffness, flow, right_edge, left_edge, *parts),
+        coupling + [pltpu.VMEM((filaments * blocks * 8 + 8, BLOCK), f32), pltpu.VMEM((slots * 8, BLOCK), f32)],
+        4,
+        (flat_spans, where, chosen, stiffness, flow, right_edge, left_edge, *parts),
     )
 
     moved = pltpu.VMEM((5, ROWS, 128), f32)
@@ -698,9 +712,9 @@
     dev, edges, force, to_right, to_left, *chunks = call(
         functools.partial(second_kernel, slots, blocks, columns),
         [side, edge, force_shape] + [(24 + share_rows, BLOCK)] * 2 + [(share_rows, BLOCK)] * (columns - 2),
-        [moved, pltpu.VMEM(force_shape, f32)] + coupling + [pltpu.VMEM((filaments * blocks, 8, BLOCK), f32)],
+        [moved, pltpu.VMEM(force_shape, f32)] + coupling + [pltpu.VMEM((filaments * blocks + 1, 8, BLOCK), f32)],
         2,
-        (flat_spans, where, post, post_edge, still, still_edge, east_dev, east_edge, west, table),
+        (where, chosen, post, post_edge, still, still_edge, east_dev, east_edge, west, table),
     )
     post, post_edge, east, west, left, right = collision(
         False, (still, east_dev, dev), edges, force, to_right, to_left

time: 45 us -> 43.9 us (0.976)
  other arithmetic: 1.36 us -> 0.69 us
  local copies, waits for them, and re-layouts: 2.63 us -> 2.04 us
    unnamed x1 -> x0, other arithmetic: 0.66 us -> none
    unnamed x11 -> x10, local copies, waits for them, and re-layouts: 2.55 us -> 2.04 us
  transfers between devices with their start and end apart: 12 -> 12, of which waited for: 9 -> 9; matrix products, arithmetic and copies ran while one was open for 4% -> 2% of each run, Pallas kernels for 8% -> 11%
where the time goes in v5:
time: 43.9 us; the launch traced here: 43.7 us
  Pallas kernels  16.4 us (37%)
  starting transfers between devices  14.4 us (33%)
  waiting for transfers between devices  9.4 us (21%)
  local copies, waits for them, and re-layouts  2.04 us (5%)
  between operations  0.75 us (2%)
  other arithmetic  0.69 us (2%)
    pallas_call x12, Pallas kernels, call(): pl.pallas_call(body, out_shape=[jax.ShapeDtypeStruct(*out) for out in out...  16.4 us
    ppermute x12, starting transfers between devices, ring(): lax.ppermute(value, axis, [(i, (i + step) % count) for i in range(count)])  14.4 us
    ppermute x12, waiting for transfers between devices, ring(): lax.ppermute(value, axis, [(i, (i + step) % count) for i in range(count)])  9.4 us
    unnamed x10, local copies, waits for them, and re-layouts  2.04 us
  transfers between devices with their start and end apart: 12, of which 9 were waited for; matrix products, arithmetic and copies ran while one was open for 2% of the time, Pallas kernels for 11%

profile of v5, /device:TPU:0, one launch (start us, length us, event | category | flops | bytes accessed | tf_op | source)
XLA Modules:
  0.0 43.7 jit_solution(9898085867253136757)
XLA Ops:
  0.7 1.3 %copy-done = f32[19,16,4,256]{3,2,1,0:T(4,128)S(1)} copy-done((f32[19,16,4,256]{3,2,1,0:T(4,128)S(1)}, f32[19,16,4,256]{3,2,1,0:T(4,128)}, u32[]{:S(2)}) %copy-start) | copy-done | bytes 1245208
  1.9 0.7 %copy-done.2 = f32[2,3,1024]{2,0,1:T(2,128)S(1)} copy-done((f32[2,3,1024]{2,0,1:T(2,128)S(1)}, f32[2,3,1024]{2,0,1:T(2,128)}, u32[]{:S(2)}) %copy-start.2) | copy-done | bytes 24600
  2.7 0.2 shard_map.60
  2.9 2.4 %collective-permute-start.2 = (f32[72,128]{1,0:T(8,128)S(1)}, f32[72,128]{1,0:T(8,128)S(1)}, u32[]{:S(2)}, u32[]{:S(2)}) collective-permute-start(f32[72,128]{1,0:T(8,128)S(1)} %get-tuple-element.39.refs_0_), channel_id=1, source_target_pairs={{0,3},{1,0},{2,1},{3,2},{4,7},{5,4},{6,5},{7,6},{8,11},{9,8},{10,9... | collective-permute-start | bytes 110600 | tf_op jit(solution)/shard_map/ppermute | solution.py:638
  5.3 0.6 %collective-permute-start.1 = (f32[72,128]{1,0:T(8,128)S(1)}, f32[72,128]{1,0:T(8,128)S(1)}, u32[]{:S(2)}, u32[]{:S(2)}) collective-permute-start(f32[72,128]{1,0:T(8,128)S(1)} %get-tuple-element.39.refs_0_), channel_id=1, source_target_pairs={{0,2},{1,3},{2,0},{3,1},{4,6},{5,7},{6,4},{7,5},{8,10},{9,11},{10,... | collective-permute-start | bytes 110600 | tf_op jit(solution)/shard_map/ppermute | solution.py:638
  6.0 0.2 collective-permute-start
  6.1 0.1 pad_add_fusion.where_ref
  6.2 1.6 %shard_map.59 = (f32[19,8,128]{2,1,0:T(8,128)S(1)}, f32[80,128]{1,0:T(8,128)S(1)}, f32[80,128]{1,0:T(8,128)S(1)}, s32[40]{0:T(128)S(1)}) custom-call(s32[2,1,32]{2,1,0:T(1,128)S(1)} %bitcast.29, s32[2]{0:T(128)S(1)} %pad_add_fusion.where_ref, f32[19,128,128]{2,1,0:T(8,128)S(1)} %bitcast.26), custom_call_target="tpu_custom_call" | custom-call | bytes 319808 | tf_op jit(solution)/shard_map/pallas_call | solution.py:627
  7.9 1.8 %collective-permute-done.1.refs_2_ = f32[72,128]{1,0:T(8,128)S(1)} collective-permute-done((f32[72,128]{1,0:T(8,128)S(1)}, f32[72,128]{1,0:T(8,128)S(1)}, u32[]{:S(2)}, u32[]{:S(2)}) %collective-permute-start.1) | collective-permute-done | bytes 36896 | tf_op jit(solution)/shard_map/ppermute | solution.py:638
  9.7 4.9 %shard_map.61 = (f32[3,128,128]{2,1,0:T(8,128)S(1)}, f32[104,128]{1,0:T(8,128)S(1)}, f32[104,128]{1,0:T(8,128)S(1)}, f32[32,16,128]{2,1,0:T(8,128)S(1)}) custom-call(s32[2,1,32]{2,1,0:T(1,128)S(1)} %bitcast.30, s32[2]{0:T(128)S(1)} %pad_add_fusion.where_ref, s32[40]{0:T(128)S(1)} %get-tuple-element.35.chosen_ref, s32[2]{0:T(128)S(1)} %copy-done.4, ...), custom_call_target="tpu_custom_call" | custom-call | bytes 1130496 | tf_op jit(solution)/shard_map/pallas_call | solution.py:627
  14.7 0.5 %collective-permute-start.3 = (f32[104,128]{1,0:T(8,128)S(1)}, f32[104,128]{1,0:T(8,128)S(1)}, u32[]{:S(2)}, u32[]{:S(2)}) collective-permute-start(f32[104,128]{1,0:T(8,128)S(1)} %get-tuple-element.43.own_ref), channel_id=1, source_target_pairs={{0,1},{1,2},{2,3},{3,0},{4,5},{5,6},{6,7},{7,4},{8,9},{9,10},{10,1... | collective-permute-start | bytes 159752 | tf_op jit(solution)/shard_map/ppermute | solution.py:638
  15.2 0.5 %shard_map.62 = (f32[19,128,128]{2,1,0:T(8,128)S(1)}, f32[160,128]{1,0:T(8,128)S(1)}, f32[160,128]{1,0:T(8,128)S(1)}) custom-call(f32[19,128,128]{2,1,0:T(8,128)S(1)} %bitcast.27, f32[3,128,128]{2,1,0:T(8,128)S(1)} %get-tuple-element.40.refs_1_), custom_call_target="tpu_custom_call" | custom-call | bytes 2818048 | tf_op jit(solution)/shard_map/pallas_call | solution.py:627
  15.7 0.8 %collective-permute-done.4.right_ref = f32[104,128]{1,0:T(8,128)S(1)} collective-permute-done((f32[104,128]{1,0:T(8,128)S(1)}, f32[104,128]{1,0:T(8,128)S(1)}, u32[]{:S(2)}, u32[]{:S(2)}) %collective-permute-start.4) | collective-permute-done | bytes 53280 | tf_op jit(solution)/shard_map/ppermute | solution.py:638
  16.5 2.0 %collective-permute-done.3.left_ref = f32[104,128]{1,0:T(8,128)S(1)} collective-permute-done((f32[104,128]{1,0:T(8,128)S(1)}, f32[104,128]{1,0:T(8,128)S(1)}, u32[]{:S(2)}, u32[]{:S(2)}) %collective-permute-start.3) | collective-permute-done | bytes 53280 | tf_op jit(solution)/shard_map/ppermute | solution.py:638
  18.6 1.6 %collective-permute-start.5 = (f32[176,128]{1,0:T(8,128)S(1)}, f32[176,128]{1,0:T(8,128)S(1)}, u32[]{:S(2)}, u32[]{:S(2)}) collective-permute-start(f32[176,128]{1,0:T(8,128)S(1)} %get-tuple-element.49), channel_id=1, source_target_pairs={{0,4},{4,8},{8,12},{12,16},{16,20},{20,24},{24,28},{28,0},{1,5},{5... | collective-permute-start | bytes 270344 | tf_op jit(solution)/shard_map/ppermute | solution.py:638
  20.1 3.2 %collective-permute-start.6 = (f32[176,128]{1,0:T(8,128)S(1)}, f32[176,128]{1,0:T(8,128)S(1)}, u32[]{:S(2)}, u32[]{:S(2)}) collective-permute-start(f32[176,128]{1,0:T(8,128)S(1)} %get-tuple-element.53), channel_id=1, source_target_pairs={{0,28},{4,0},{8,4},{12,8},{16,12},{20,16},{24,20},{28,24},{1,29},{... | collective-permute-start | bytes 270344 | tf_op jit(solution)/shard_map/ppermute | solution.py:638
  23.4 0.6 %shard_map.64 = (f32[9,128,128]{2,1,0:T(8,128)S(1)}, f32[9,8,128]{2,1,0:T(8,128)S(1)}) custom-call(f32[19,128,128]{2,1,0:T(8,128)S(1)} %get-tuple-element.41.post_ref, f32[19,8,128]{2,1,0:T(8,128)S(1)} %get-tuple-element.47.post_edge_ref), custom_call_target="tpu_custom_call" | custom-call | bytes 1253376 | tf_op jit(solution)/shard_map/pallas_call | solution.py:627
  24.0 2.0 %collective-permute-done.5.refs_0_ = f32[176,128]{1,0:T(8,128)S(1)} collective-permute-done((f32[176,128]{1,0:T(8,128)S(1)}, f32[176,128]{1,0:T(8,128)S(1)}, u32[]{:S(2)}, u32[]{:S(2)}) %collective-permute-start.5) | collective-permute-done | bytes 90144 | tf_op jit(solution)/shard_map/ppermute | solution.py:638
  25.9 0.3 shard_map.65
  26.2 0.4 collective-permute-done.6.west_ref
  26.6 4.9 %shard_map.66 = (f32[5,128,128]{2,1,0:T(8,128)S(1)}, f32[19,8,128]{2,1,0:T(8,128)S(1)}, f32[3,128,128]{2,1,0:T(8,128)S(1)}, f32[72,128]{1,0:T(8,128)S(1)}, f32[7...) custom-call(s32[2]{0:T(128)S(1)} %pad_add_fusion.where_ref, s32[40]{0:T(128)S(1)} %get-tuple-element.35.chosen_ref, ...), custom_call_target="tpu_custom_call" | custom-call | bytes 1449984 | tf_op jit(solution)/shard_map/pallas_call | solution.py:627
  31.6 0.5 %collective-permute-start.7 = (f32[72,128]{1,0:T(8,128)S(1)}, f32[72,128]{1,0:T(8,128)S(1)}, u32[]{:S(2)}, u32[]{:S(2)}) collective-permute-start(f32[72,128]{1,0:T(8,128)S(1)} %get-tuple-element.59.own_ref), channel_id=1, source_target_pairs={{0,1},{1,2},{2,3},{3,0},{4,5},{5,6},{6,7},{7,4},{8,9},{9,10},{10,1... | collective-permute-start | bytes 110600 | tf_op jit(solution)/shard_map/ppermute | solution.py:638
  32.1 0.5 %collective-permute-start.11 = (f32[48,128]{1,0:T(8,128)S(1)}, f32[48,128]{1,0:T(8,128)S(1)}, u32[]{:S(2)}, u32[]{:S(2)}) collective-permute-start(f32[48,128]{1,0:T(8,128)S(1)} %get-tuple-element.67), channel_id=1, source_target_pairs={{0,2},{1,3},{2,0},{3,1},{4,6},{5,7},{6,4},{7,5},{8,10},{9,11},{10,... | collective-permute-start | bytes 73736 | tf_op jit(solution)/shard_map/ppermute | solution.py:638
  32.6 0.5 %shard_map.67 = (f32[19,128,128]{2,1,0:T(8,128)S(1)}, f32[160,128]{1,0:T(8,128)S(1)}, f32[160,128]{1,0:T(8,128)S(1)}) custom-call(f32[9,128,128]{2,1,0:T(8,128)S(1)} %get-tuple-element.48.still_ref.refs_0_, f32[5,128,128]{2,1,0:T(8,128)S(1)} %get-tuple-element.50.east_dev_ref.refs_1_, f32[5,128,128]{2,1,0:T(8,128)S(1)} %get-tuple-element.55.refs_2_, ...), custom_call_target="tpu_custom_call" | custom-call | bytes 2818048 | tf_op jit(solution)/shard_map/pallas_call | solution.py:627
  33.2 0.3 collective-permute-done.8.right_ref
  33.5 1.6 %collective-permute-done.7.left_ref = f32[72,128]{1,0:T(8,128)S(1)} collective-permute-done((f32[72,128]{1,0:T(8,128)S(1)}, f32[72,128]{1,0:T(8,128)S(1)}, u32[]{:S(2)}, u32[]{:S(2)}) %collective-permute-start.7) | collective-permute-done | bytes 36896 | tf_op jit(solution)/shard_map/ppermute | solution.py:638
  35.1 0.5 %collective-permute-start.9 = (f32[176,128]{1,0:T(8,128)S(1)}, f32[176,128]{1,0:T(8,128)S(1)}, u32[]{:S(2)}, u32[]{:S(2)}) collective-permute-start(f32[176,128]{1,0:T(8,128)S(1)} %get-tuple-element.64), channel_id=1, source_target_pairs={{0,4},{4,8},{8,12},{12,16},{16,20},{20,24},{24,28},{28,0},{1,5},{5... | collective-permute-start | bytes 270344 | tf_op jit(solution)/shard_map/ppermute | solution.py:638
  35.6 4.2 %collective-permute-start.10 = (f32[176,128]{1,0:T(8,128)S(1)}, f32[176,128]{1,0:T(8,128)S(1)}, u32[]{:S(2)}, u32[]{:S(2)}) collective-permute-start(f32[176,128]{1,0:T(8,128)S(1)} %get-tuple-element.65), channel_id=1, source_target_pairs={{0,28},{4,0},{8,4},{12,8},{16,12},{20,16},{24,20},{28,24},{1,29},{... | collective-permute-start | bytes 270344 | tf_op jit(solution)/shard_map/ppermute | solution.py:638
  39.9 0.6 %fusion = f32[48,128]{1,0:T(8,128)} fusion(f32[48,128]{1,0:T(8,128)S(1)} %collective-permute-done.11, f32[72,128]{1,0:T(8,128)S(1)} %collective-permute-done.8.right_ref, f32[48,128]{1,0:T(8,128)S(1)} %get-tuple-element.66, f32[72,128]{1,0:T(8,128)S(1)} %collective-permute-done.7.left_ref), kind=kLoop, calls=%fused_computation.1 | loop fusion | flops 18432 | bytes 122880 | tf_op jit(solution)/shard_map/add | solution.py:724
  40.5 1.4 %shard_map.69.refs_2_ = f32[19,128,128]{2,1,0:T(8,128)} custom-call(f32[19,128,128]{2,1,0:T(8,128)S(1)} %get-tuple-element.57.post_ref, f32[19,8,128]{2,1,0:T(8,128)S(1)} %get-tuple-element.63.post_edge_ref), custom_call_target="tpu_custom_call" | custom-call | bytes 2490368 | tf_op jit(solution)/shard_map/pallas_call | solution.py:627
  41.9 0.5 %collective-permute-done.9.refs_0_ = f32[176,128]{1,0:T(8,128)S(1)} collective-permute-done((f32[176,128]{1,0:T(8,128)S(1)}, f32[176,128]{1,0:T(8,128)S(1)}, u32[]{:S(2)}, u32[]{:S(2)}) %collective-permute-start.9) | collective-permute-done | bytes 90144 | tf_op jit(solution)/shard_map/ppermute | solution.py:638
  42.4 1.3 %shard_map.70 = f32[19,128,128]{2,1,0:T(8,128)} custom-call(f32[19,128,128]{2,1,0:T(8,128)S(1)} %get-tuple-element.57.post_ref, f32[19,8,128]{2,1,0:T(8,128)S(1)} %get-tuple-element.63.post_edge_ref, f32[176,128]{1,0:T(8,128)S(1)} %collective-permute-done.9.refs_0_, f32[176,128]{1,0:T(8,128)S(1)} %collective-permute-done.10.refs_1_, ...), custom_call_target="tpu_custom_call", output_to_operand_aliasing={{}: (4, {})} | custom-call | bytes 2490368 | tf_op jit(solution)/shard_map/pallas_call | solution.py:627
  (16 shorter events, 0.3 us)
Async XLA Ops:
  0.6 5.6 %copy-start.3 = (s32[2,32,1]{1,2,0:T(1,128)S(1)}, s32[2,32,1]{1,2,0:T(1,128)}, u32[]{:S(2)}) copy-start(s32[2,32,1]{1,2,0:T(1,128)} %param.6) | copy-start | bytes 772
  0.6 1.3 %copy-start = (f32[19,16,4,256]{3,2,1,0:T(4,128)S(1)}, f32[19,16,4,256]{3,2,1,0:T(4,128)}, u32[]{:S(2)}) copy-start(f32[19,16,4,256]{3,2,1,0:T(4,128)} %param.4) | copy-start | bytes 3735556
  1.9 0.7 %copy-start.2 = (f32[2,3,1024]{2,0,1:T(2,128)S(1)}, f32[2,3,1024]{2,0,1:T(2,128)}, u32[]{:S(2)}) copy-start(f32[2,3,1024]{2,0,1:T(2,128)} %param.5) | copy-start | bytes 73732
  2.7 3.5 %copy-start.1 = (f32[19,16,4,256]{3,2,1,0:T(4,128)S(1)}, f32[19,16,4,256]{3,2,1,0:T(4,128)}, u32[]{:S(2)}) copy-start(f32[19,16,4,256]{3,2,1,0:T(4,128)} %param.4) | copy-start | bytes 3735556
  2.7 7.0 %copy-start.4 = (s32[2]{0:T(128)S(1)}, s32[2]{0:T(128)}, u32[]{:S(2)}) copy-start(s32[2]{0:T(128)} %stiff_ref.1) | copy-start | bytes 28
  2.9 4.9 %collective-permute-start.2 = (f32[72,128]{1,0:T(8,128)S(1)}, f32[72,128]{1,0:T(8,128)S(1)}, u32[]{:S(2)}, u32[]{:S(2)}) collective-permute-start(f32[72,128]{1,0:T(8,128)S(1)} %get-tuple-element.39.refs_0_), channel_id=1, source_target_pairs={{0,3},{1,0},{2,1},{3,2},{4,7},{5,4},{6,5},{7,6},{8,11},{9,8},{10,9... | collective-permute-start | bytes 110600 | tf_op jit(solution)/shard_map/ppermute | solution.py:638
  5.3 4.3 %collective-permute-start.1 = (f32[72,128]{1,0:T(8,128)S(1)}, f32[72,128]{1,0:T(8,128)S(1)}, u32[]{:S(2)}, u32[]{:S(2)}) collective-permute-start(f32[72,128]{1,0:T(8,128)S(1)} %get-tuple-element.39.refs_0_), channel_id=1, source_target_pairs={{0,2},{1,3},{2,0},{3,1},{4,6},{5,7},{6,4},{7,5},{8,10},{9,11},{10,... | collective-permute-start | bytes 110600 | tf_op jit(solution)/shard_map/ppermute | solution.py:638
  6.0 3.7 %collective-permute-start = (f32[72,128]{1,0:T(8,128)S(1)}, f32[72,128]{1,0:T(8,128)S(1)}, u32[]{:S(2)}, u32[]{:S(2)}) collective-permute-start(f32[72,128]{1,0:T(8,128)S(1)} %get-tuple-element.39.refs_0_), channel_id=1, source_target_pairs={{0,1},{1,2},{2,3},{3,0},{4,5},{5,6},{6,7},{7,4},{8,9},{9,10},{10,1... | collective-permute-start | bytes 110600 | tf_op jit(solution)/shard_map/ppermute | solution.py:638
  14.6 1.8 %collective-permute-start.4 = (f32[104,128]{1,0:T(8,128)S(1)}, f32[104,128]{1,0:T(8,128)S(1)}, u32[]{:S(2)}, u32[]{:S(2)}) collective-permute-start(f32[104,128]{1,0:T(8,128)S(1)} %get-tuple-element.44), channel_id=1, source_target_pairs={{0,3},{1,0},{2,1},{3,2},{4,7},{5,4},{6,5},{7,6},{8,11},{9,8},{10,9... | collective-permute-start | bytes 159752 | tf_op jit(solution)/shard_map/ppermute | solution.py:638
  14.7 3.8 %collective-permute-start.3 = (f32[104,128]{1,0:T(8,128)S(1)}, f32[104,128]{1,0:T(8,128)S(1)}, u32[]{:S(2)}, u32[]{:S(2)}) collective-permute-start(f32[104,128]{1,0:T(8,128)S(1)} %get-tuple-element.43.own_ref), channel_id=1, source_target_pairs={{0,1},{1,2},{2,3},{3,0},{4,5},{5,6},{6,7},{7,4},{8,9},{9,10},{10,1... | collective-permute-start | bytes 159752 | tf_op jit(solution)/shard_map/ppermute | solution.py:638
  18.6 7.4 %collective-permute-start.5 = (f32[176,128]{1,0:T(8,128)S(1)}, f32[176,128]{1,0:T(8,128)S(1)}, u32[]{:S(2)}, u32[]{:S(2)}) collective-permute-start(f32[176,128]{1,0:T(8,128)S(1)} %get-tuple-element.49), channel_id=1, source_target_pairs={{0,4},{4,8},{8,12},{12,16},{16,20},{20,24},{24,28},{28,0},{1,5},{5... | collective-permute-start | bytes 270344 | tf_op jit(solution)/shard_map/ppermute | solution.py:638
  20.1 6.5 %collective-permute-start.6 = (f32[176,128]{1,0:T(8,128)S(1)}, f32[176,128]{1,0:T(8,128)S(1)}, u32[]{:S(2)}, u32[]{:S(2)}) collective-permute-start(f32[176,128]{1,0:T(8,128)S(1)} %get-tuple-element.53), channel_id=1, source_target_pairs={{0,28},{4,0},{8,4},{12,8},{16,12},{20,16},{24,20},{28,24},{1,29},{... | collective-permute-start | bytes 270344 | tf_op jit(solution)/shard_map/ppermute | solution.py:638
  31.5 1.9 %collective-permute-start.8 = (f32[72,128]{1,0:T(8,128)S(1)}, f32[72,128]{1,0:T(8,128)S(1)}, u32[]{:S(2)}, u32[]{:S(2)}) collective-permute-start(f32[72,128]{1,0:T(8,128)S(1)} %get-tuple-element.60), channel_id=1, source_target_pairs={{0,3},{1,0},{2,1},{3,2},{4,7},{5,4},{6,5},{7,6},{8,11},{9,8},{10,9... | collective-permute-start | bytes 110600 | tf_op jit(solution)/shard_map/ppermute | solution.py:638
  31.6 3.4 %collective-permute-start.7 = (f32[72,128]{1,0:T(8,128)S(1)}, f32[72,128]{1,0:T(8,128)S(1)}, u32[]{:S(2)}, u32[]{:S(2)}) collective-permute-start(f32[72,128]{1,0:T(8,128)S(1)} %get-tuple-element.59.own_ref), channel_id=1, source_target_pairs={{0,1},{1,2},{2,3},{3,0},{4,5},{5,6},{6,7},{7,4},{8,9},{9,10},{10,1... | collective-permute-start | bytes 110600 | tf_op jit(solution)/shard_map/ppermute | solution.py:638
  32.1 7.8 %collective-permute-start.11 = (f32[48,128]{1,0:T(8,128)S(1)}, f32[48,128]{1,0:T(8,128)S(1)}, u32[]{:S(2)}, u32[]{:S(2)}) collective-permute-start(f32[48,128]{1,0:T(8,128)S(1)} %get-tuple-element.67), channel_id=1, source_target_pairs={{0,2},{1,3},{2,0},{3,1},{4,6},{5,7},{6,4},{7,5},{8,10},{9,11},{10,... | collective-permute-start | bytes 73736 | tf_op jit(solution)/shard_map/ppermute | solution.py:638
  35.1 7.3 %collective-permute-start.9 = (f32[176,128]{1,0:T(8,128)S(1)}, f32[176,128]{1,0:T(8,128)S(1)}, u32[]{:S(2)}, u32[]{:S(2)}) collective-permute-start(f32[176,128]{1,0:T(8,128)S(1)} %get-tuple-element.64), channel_id=1, source_target_pairs={{0,4},{4,8},{8,12},{12,16},{16,20},{20,24},{24,28},{28,0},{1,5},{5... | collective-permute-start | bytes 270344 | tf_op jit(solution)/shard_map/ppermute | solution.py:638
  35.6 6.7 %collective-permute-start.10 = (f32[176,128]{1,0:T(8,128)S(1)}, f32[176,128]{1,0:T(8,128)S(1)}, u32[]{:S(2)}, u32[]{:S(2)}) collective-permute-start(f32[176,128]{1,0:T(8,128)S(1)} %get-tuple-element.65), channel_id=1, source_target_pairs={{0,28},{4,0},{8,4},{12,8},{16,12},{20,16},{24,20},{28,24},{1,29},{... | collective-permute-start | bytes 270344 | tf_op jit(solution)/shard_map/ppermute | solution.py:638

commit v6 on v5

--- a/solution.py
+++ b/solution.py
@@ -69,7 +69,8 @@
     _, lane = iotas()
     total = jnp.zeros((8, 128), jnp.float32)
     for z in range(DEPTH):
-        total = jnp.where((lane >= 5 * z) & (lane < 5 * z + 5), turn(slices(z), 5 * z + 2, 1), total)
+        at = 5 * (DEPTH - 1 - z)
+        total = jnp.where((lane >= at) & (lane < at + 5), turn(slices(z), at + 2, 1), total)
     return total
 
 
@@ -223,7 +224,6 @@
     unscale = top * 2.0**-15
     bound = jnp.maximum(table_ref[0, 12:13, 0:1] + feedback_gain * top, TINY)
     scale = 2.0**17 / bound
-    total_ref[...] = jnp.zeros_like(total_ref)
     column = lax.broadcasted_iota(jnp.int32, (256, BLOCK), 0).astype(jnp.float32).astype(jnp.bfloat16)
     one, none = jnp.bfloat16(1), jnp.bfloat16(0)
     z_cell = lax.broadcasted_iota(jnp.int32, (DEPTH, BLOCK), 0).astype(jnp.float32)
@@ -286,11 +286,12 @@
             spread_high.append(high)
             spread_low.append((piece - high.astype(jnp.float32)).astype(FINE))
         across_rows = (((1,), (1,)), ((), ()))
-        total_ref[...] += lax.dot_general(
+        total = lax.dot_general(
             jnp.concatenate(spread_high, axis=1), coarse, across_rows, preferred_element_type=jnp.float32
         ) + lax.dot_general(
             jnp.concatenate(spread_low, axis=1), fine, across_rows, preferred_element_type=jnp.float32
         )
+        total_ref[...] = total if step == 0 else total_ref[...] + total
 
     for step in range(slots // group):
         body(step)
@@ -342,7 +343,7 @@
     for c in range(3):
         flow = flows[c]
         for z in range(DEPTH):
-            halo_ref[c, 8 * z : 8 * z + 8, :] = turn(flow, -(5 * z + 2), 1)
+            halo_ref[c, 8 * z : 8 * z + 8, :] = turn(flow, -(5 * (DEPTH - 1 - z) + 2), 1)
 
 
 def gather_markers(span_y, slots, filaments, share, spans_ref, where_ref, chosen_ref, stiff_ref, part_refs, places_ref, picked_ref, table_ref):
@@ -448,9 +449,7 @@
     def dev(e, part):
         if first:
             return dev_refs[0][e, part, :]
-        for ref, entries in zip(dev_refs, (STILL, EAST, WEST)):
-            if e in entries:
-                return ref[entries.index(e), part, :]
+        return dev_refs[0][e, part, :] if e in STILL else dev_refs[1][MOVING.index(e), part, :]
 
     for z in range(DEPTH):
         part = slice(8 * z, 8 * z + 8)
@@ -492,83 +491,108 @@
     west_ref[PLANE + 10 :, :] = zero
 
 
-def stream(entries, post_ref, post_edge_ref, plane_ref, moved_ref, store, store_edge):
+def stream(entries, post_ref, post_edge_ref, moved_ref, store, store_edge):
     row, lane = iotas()
     low, high = row < 4, row >= 4
     same = (low & (lane < 2)) | (high & (lane == 127))
     patches = {0: same, 1: low & (lane < 3), -1: (low & (lane == 0)) | (high & (lane >= 126))}
-    low_wall, high_wall = lane < 5, lane >= 75
+    low_wall, high_wall = lane >= 75, lane < 5
     for e in entries:
         cx, cy, cz = velocity_set[e]
-        edge = post_edge_ref[e]
-        if cx != 0:
-            k = (EAST if cx == 1 else WEST).index(e)
-            line = PLANE + 2 * k
-            beside = jnp.where(low, plane_ref[line : line + 1, :], plane_ref[line + 1 : line + 2, :])
-            edge = jnp.where(row % 4 == (0 if cx == 1 else 3), beside, turn(edge, cx, 0))
-        edge = turn(edge, cy + 5 * cz, 1)
+        edge = turn(turn(post_edge_ref[e], cx, 0), cy - 5 * cz, 1)
         if cz == 1:
             edge = jnp.where(low_wall, post_edge_ref[opposite(e)], edge)
         elif cz == -1:
             edge = jnp.where(high_wall, post_edge_ref[opposite(e)], edge)
         store_edge(e, edge)
-        if cx != 0:
-            for z in range(DEPTH):
-                moved_ref[k, 8 * z : 8 * z + 8, :] = turn(post_ref[e, 8 * z : 8 * z + 8, :], cx, 0)
-            moved_ref[k, pl.ds(0 if cx == 1 else 3, 32, stride=4), :] = plane_ref[32 * k : 32 * k + 32, :]
         swapped = turn(edge, 4, 0)
         for z in range(DEPTH):
             source, patch = z - cz, patches[cy]
             if 0 <= source < DEPTH:
-                part = slice(8 * source, 8 * source + 8)
-                value = post_ref[e, part, :] if cx == 0 else moved_ref[k, part, :]
+                value = turn(post_ref[e, 8 * source : 8 * source + 8, :], cx, 0)
                 if cy != 0:
                     value = turn(value, cy, 1)
                     value = jnp.where(lane == (0 if cy == 1 else 127), turn(value, 4, 0), value)
             else:
                 value, patch = post_ref[opposite(e), 8 * z : 8 * z + 8, :], same
-            store(e, z, jnp.where(patch, turn(swapped, -(5 * z + 2), 1), value))
-
-
-def stream_kernel(entries, post_ref, post_edge_ref, *refs):
-    plane_ref, refs = (None, refs) if entries is STILL else (refs[0], refs[1:])
-    dev_ref, edges_ref = refs[:2]
-    moved_ref = None if entries is STILL else refs[2]
-
+            store(e, z, jnp.where(patch, turn(swapped, -(5 * (DEPTH - 1 - z) + 2), 1), value))
+
+
+def join(e, plane_ref, post_ref, post_edge_ref, before, before_edge, moved_ref, store, store_edge):
+    cx, cy, cz = velocity_set[e]
+    k, x = (EAST if cx == 1 else WEST).index(e), 0 if cx == 1 else 3
+    row, lane = iotas((DEPTH, 128))
+    _, single = iotas((1, 128))
+    edges = []
+    for half in range(2):
+        line, at = PLANE + 2 * k + half, 4 * half + x
+        edge = turn(plane_ref[line : line + 1, :], cy - 5 * cz, 1)
+        if cz != 0:
+            edge = jnp.where(single >= 75 if cz == 1 else single < 5, post_edge_ref[opposite(e), at : at + 1, :], edge)
+        edges.append(edge)
+    tiles = [plane_ref[pl.ds(32 * k + half, DEPTH, stride=2), :] for half in range(2)]
+    if cy != 0:
+        turned = [turn(tile, cy, 1) for tile in tiles]
+        tiles = [turned[0], jnp.where(lane == 0, turned[0], turned[1])]
+        if cy == -1:
+            tiles = [jnp.where(lane == 127, turned[1], turned[0]), turned[1]]
+    wall = row == (0 if cz == 1 else DEPTH - 1)
+    place = MOVING.index(e)
+    for half in range(2):
+        tile = tiles[half]
+        same = lane < 2 if half == 0 else lane == 127
+        patch = {
+            0: same, 1: lane < 3 if half == 0 else lane < 0, -1: lane == 0 if half == 0 else lane >= 126
+        }[cy]
+        if cz != 0:
+            at = (0 if cz == 1 else 8 * DEPTH - 8) + 4 * half + x
+            tile = jnp.where(wall, post_ref[opposite(e), at : at + 1, :], turn(tile, cz, 0))
+            patch = (wall & same) | (jnp.logical_not(wall) & patch)
+        shown = pltpu.roll(jnp.broadcast_to(edges[1 - half], (DEPTH, 128)), 51, 1, stride=5, stride_axis=0)
+        moved_ref[place, pl.ds(4 * half + x, DEPTH, stride=8), :] = jnp.where(patch, shown, tile)
+    row, _ = iotas()
+    for z in range(DEPTH):
+        part = slice(8 * z, 8 * z + 8)
+        store(e, z, jnp.where(row % 4 == x, moved_ref[place, part, :], before[part, :]))
+    if store_edge is not None:
+        store_edge(e, jnp.where(row == x, edges[0], jnp.where(row == 4 + x, edges[1], before_edge[...])))
+
+
+def stream_kernel(post_ref, post_edge_ref, dev_ref, edges_ref):
     def store(e, z, value):
-        dev_ref[entries.index(e), 8 * z : 8 * z + 8, :] = value
+        dev_ref[e, 8 * z : 8 * z + 8, :] = value
 
     def store_edge(e, value):
-        edges_ref[entries.index(e)] = value
-
-    stream(entries, post_ref, post_edge_ref, plane_ref, moved_ref, store, store_edge)
+        edges_ref[e] = value
+
+    stream(range(19), post_ref, post_edge_ref, None, store, store_edge)
 
 
 def second_kernel(
     slots, blocks, columns, where_ref, chosen_ref,
-    post_ref, post_edge_ref, still_ref, still_edge_ref, east_dev_ref, east_edge_ref, west_ref, table_ref, *refs
+    post_ref, post_edge_ref, streamed_ref, streamed_edge_ref, east_ref, west_ref, table_ref, *refs
 ):
     dev_ref, edges_ref, force_ref, to_right_ref, to_left_ref = refs[:5]
     share_refs, refs = refs[5 : 3 + columns], refs[3 + columns :]
     moved_ref, flow_ref, halo_ref, matrix_ref, rest_ref, total_ref, speed_ref, spot_ref = refs
 
     def store(e, z, value):
-        dev_ref[WEST.index(e), 8 * z : 8 * z + 8, :] = value
+        dev_ref[MOVING.index(e), 8 * z : 8 * z + 8, :] = value
 
     def store_edge(e, value):
         edges_ref[e] = value
 
     def dev(e, z):
         part = slice(8 * z, 8 * z + 8)
-        for ref, entries in ((still_ref, STILL), (east_dev_ref, EAST), (dev_ref, WEST)):
-            if e in entries:
-                return ref[entries.index(e), part, :]
-
-    stream(WEST, post_ref, post_edge_ref, west_ref, moved_ref, store, store_edge)
-    for k, e in enumerate(EAST):
-        edges_ref[e] = east_edge_ref[k]
-    for k, e in enumerate(STILL):
-        edges_ref[e] = still_edge_ref[k]
+        return streamed_ref[e, part, :] if e in STILL else dev_ref[MOVING.index(e), part, :]
+
+    for e in MOVING:
+        join(
+            e, east_ref if e in EAST else west_ref, post_ref, post_edge_ref,
+            streamed_ref.at[e], streamed_edge_ref.at[e], moved_ref, store, store_edge,
+        )
+    for e in STILL:
+        edges_ref[e] = streamed_edge_ref[e]
     flow_slices(lambda z: [dev(e, z) for e in range(19)], flow_ref)
     flow_edges(edge_flow([edges_ref[e] for e in range(19)]), halo_ref)
     top = prepare_matrix(flow_ref, halo_ref, matrix_ref, rest_ref)
@@ -594,19 +618,34 @@
                     target[row : row + 1, :] = spot_ref[f * blocks + owner * share + k, c : c + 1, :]
 
 
-def last_kernel(entries, post_ref, post_edge_ref, *refs):
-    planes = refs[:2]
-    refs = refs if entries is STILL else refs[3:]
-    dev_ref, kept_ref, sems = refs[:3]
-    moved_ref = None if entries is STILL else refs[3]
-
+def last_still_kernel(post_ref, post_edge_ref, dev_ref, before_ref, kept_ref, sems):
     def store(e, z, value):
-        kept_ref[entries.index(e), 8 * z : 8 * z + 8, :] = value
+        if e in STILL:
+            kept_ref[STILL.index(e), 8 * z : 8 * z + 8, :] = value
+        else:
+            before_ref[MOVING.index(e), 8 * z : 8 * z + 8, :] = value
 
     copies = []
-    for k, e in enumerate(entries):
-        plane_ref = planes[0 if e in EAST else 1]
-        stream((e,), post_ref, post_edge_ref, plane_ref, moved_ref, store, lambda e, value: None)
+    for k, e in enumerate(STILL):
+        stream((e,), post_ref, post_edge_ref, None, store, lambda e, value: None)
+        copies.append(pltpu.make_async_copy(kept_ref.at[k], dev_ref.at[e], sems.at[k]))
+        copies[-1].start()
+    stream(MOVING, post_ref, post_edge_ref, None, store, lambda e, value: None)
+    for copy in copies:
+        copy.wait()
+
+
+def last_kernel(
+    post_ref, post_edge_ref, before_ref, east_ref, west_ref, home_ref, old_ref, dev_ref, speed_ref, moved_ref, kept_ref, sems
+):
+    def store(e, z, value):
+        kept_ref[MOVING.index(e), 8 * z : 8 * z + 8, :] = value
+
+    copies = [pltpu.make_async_copy(home_ref, speed_ref, sems.at[10])]
+    copies[0].start()
+    for k, e in enumerate(MOVING):
+        plane_ref = east_ref if e in EAST else west_ref
+        join(e, plane_ref, post_ref, post_edge_ref, before_ref.at[k], None, moved_ref, store, None)
         copies.append(pltpu.make_async_copy(kept_ref.at[k], dev_ref.at[e], sems.at[k]))
         copies[-1].start()
     for copy in copies:
@@ -688,8 +727,8 @@
         (flat_spans, where, chosen, stiffness, flow, right_edge, left_edge, *parts),
     )
 
-    moved = pltpu.VMEM((5, ROWS, 128), f32)
-    side = (5, ROWS, 128)
+    moving = (len(MOVING), ROWS, 128)
+    moved = pltpu.VMEM(moving, f32)
 
     def collision(first, dev, edges, force, to_right, to_left):
         left, right = ring(to_right, "gy", 1), ring(to_left, "gy", -1)
@@ -703,36 +742,33 @@
         return post, post_edge, ring(east, "gx", 1), ring(west, "gx", -1), left, right
 
     post, post_edge, east, west, _, _ = collision(True, (pop,), own_edge, force, to_right, to_left)
-    still, still_edge = call(
-        functools.partial(stream_kernel, STILL), [(9, ROWS, 128), (9, 8, 128)], [], 0, (post, post_edge)
-    )
-    east_dev, east_edge = call(
-        functools.partial(stream_kernel, EAST), [side, (5, 8, 128)], [moved], 0, (post, post_edge, east)
-    )
+    streamed, streamed_edge = call(stream_kernel, [field, edge], [], 0, (post, post_edge))
     dev, edges, force, to_right, to_left, *chunks = call(
         functools.partial(second_kernel, slots, blocks, columns),
-        [side, edge, force_shape] + [(24 + share_rows, BLOCK)] * 2 + [(share_rows, BLOCK)] * (columns - 2),
+        [moving, edge, force_shape] + [(24 + share_rows, BLOCK)] * 2 + [(share_rows, BLOCK)] * (columns - 2),
         [moved, pltpu.VMEM(force_shape, f32)] + coupling + [pltpu.VMEM((filaments * blocks + 1, 8, BLOCK), f32)],
         2,
-        (where, chosen, post, post_edge, still, still_edge, east_dev, east_edge, west, table),
+        (where, chosen, post, post_edge, streamed, streamed_edge, east, west, table),
     )
     post, post_edge, east, west, left, right = collision(
-        False, (still, east_dev, dev), edges, force, to_right, to_left
+        False, (streamed, dev), edges, force, to_right, to_left
     )
     speed = chunks[0] + left[24:] + right[24:]
     for s in range(2, columns - 1):
         speed = speed + ring(chunks[s - 1], "gy", s)
+
+    dev, before = call(
+        last_still_kernel, [field, moving],
+        [pltpu.VMEM((9, ROWS, 128), f32), pltpu.SemaphoreType.DMA((9,))],
+        0, (post, post_edge), out_specs=[anywhere, inside],
+    )
+    dev, speed = call(
+        last_kernel, [field, (share_rows, BLOCK)],
+        [moved, pltpu.VMEM(moving, f32), pltpu.SemaphoreType.DMA((11,))],
+        0, (post, post_edge, before, east, west, speed, dev),
+        in_specs=[inside] * 6 + [anywhere], out_specs=[anywhere] * 2, input_output_aliases={6: 0},
+    )
     speed = speed.reshape(3, share_blocks, filaments, BLOCK).transpose(2, 0, 1, 3).reshape(fraction.shape)
-
-    dev = None
-    for entries in (STILL, EAST + WEST):
-        count = len(entries)
-        scratch = [pltpu.VMEM((count, ROWS, 128), f32), pltpu.SemaphoreType.DMA((count,))]
-        extra, args = {}, (post, post_edge)
-        if entries is not STILL:
-            scratch, args = scratch + [moved], args + (east, west, dev)
-            extra = dict(in_specs=[inside] * 4 + [anywhere], input_output_aliases={4: 0})
-        (dev,) = call(functools.partial(last_kernel, entries), [field], scratch, 0, args, out_specs=[anywhere], **extra)
     dev = dev.reshape(19, depth, halves, tile_x, 128).transpose(0, 1, 3, 2, 4).reshape(populations.shape)
     return dev, speed
 

time: 43.9 us -> 43.6 us (level)
  waiting for transfers between devices: 9.4 us -> 8.79 us
  other arithmetic: 0.69 us -> 0.08 us
  Pallas kernels: 16.4 us -> 16.9 us
    ppermute x12, waiting for transfers between devices: 9.4 us -> 8.79 us  [ring(): lax.ppermute(value, axis, [(i, (i + step) % count) for i in range(count)])]
    add x1, other arithmetic: 0.62 us -> 0.01 us  [per_device(): speed = speed + ring(chunks[s - 1], 'gy', s)]
    pallas_call x12 -> x11, Pallas kernels: 16.4 us -> 16.9 us  [call(): pl.pallas_call(body, out_shape=[jax.ShapeDtypeStruct(*out) for out in out...]
  transfers between devices with their start and end apart: 12 -> 12, of which waited for: 9 -> 8; matrix products, arithmetic and copies ran while one was open for 2% -> 0% of each run, Pallas kernels for 11% -> 13%
where the time goes in v6:
time: 43.6 us; the launch traced here: 43.4 us
  Pallas kernels  16.9 us (39%)
  starting transfers between devices  14.8 us (34%)
  waiting for transfers between devices  8.79 us (20%)
  local copies, waits for them, and re-layouts  2.04 us (5%)
  between operations  0.76 us (2%)
    pallas_call x11, Pallas kernels, call(): pl.pallas_call(body, out_shape=[jax.ShapeDtypeStruct(*out) for out in out...  16.9 us
    ppermute x12, starting transfers between devices, ring(): lax.ppermute(value, axis, [(i, (i + step) % count) for i in range(count)])  14.8 us
    ppermute x12, waiting for transfers between devices, ring(): lax.ppermute(value, axis, [(i, (i + step) % count) for i in range(count)])  8.79 us
    unnamed x10, local copies, waits for them, and re-layouts  2.04 us
  transfers between devices with their start and end apart: 12, of which 8 were waited for; matrix products, arithmetic and copies ran while one was open for 0% of the time, Pallas kernels for 13%

profile of v6, /device:TPU:0, one launch (start us, length us, event | category | flops | bytes accessed | tf_op | source)
XLA Modules:
  0.0 43.4 jit_solution(15101039605341514326)
XLA Ops:
  0.7 1.3 %copy-done = f32[19,16,4,256]{3,2,1,0:T(4,128)S(1)} copy-done((f32[19,16,4,256]{3,2,1,0:T(4,128)S(1)}, f32[19,16,4,256]{3,2,1,0:T(4,128)}, u32[]{:S(2)}) %copy-start) | copy-done | bytes 1245208
  1.9 0.7 %copy-done.2 = f32[2,3,1024]{2,0,1:T(2,128)S(1)} copy-done((f32[2,3,1024]{2,0,1:T(2,128)S(1)}, f32[2,3,1024]{2,0,1:T(2,128)}, u32[]{:S(2)}) %copy-start.2) | copy-done | bytes 24600
  2.7 0.2 shard_map.60
  2.9 2.4 %collective-permute-start.2 = (f32[72,128]{1,0:T(8,128)S(1)}, f32[72,128]{1,0:T(8,128)S(1)}, u32[]{:S(2)}, u32[]{:S(2)}) collective-permute-start(f32[72,128]{1,0:T(8,128)S(1)} %get-tuple-element.41.refs_0_), channel_id=1, source_target_pairs={{0,3},{1,0},{2,1},{3,2},{4,7},{5,4},{6,5},{7,6},{8,11},{9,8},{10,9... | collective-permute-start | bytes 110600 | tf_op jit(solution)/shard_map/ppermute | solution.py:677
  5.3 0.6 %collective-permute-start.1 = (f32[72,128]{1,0:T(8,128)S(1)}, f32[72,128]{1,0:T(8,128)S(1)}, u32[]{:S(2)}, u32[]{:S(2)}) collective-permute-start(f32[72,128]{1,0:T(8,128)S(1)} %get-tuple-element.41.refs_0_), channel_id=1, source_target_pairs={{0,2},{1,3},{2,0},{3,1},{4,6},{5,7},{6,4},{7,5},{8,10},{9,11},{10,... | collective-permute-start | bytes 110600 | tf_op jit(solution)/shard_map/ppermute | solution.py:677
  6.0 0.2 collective-permute-start
  6.1 0.1 pad_add_fusion.where_ref
  6.2 1.5 %shard_map.59 = (f32[19,8,128]{2,1,0:T(8,128)S(1)}, f32[80,128]{1,0:T(8,128)S(1)}, f32[80,128]{1,0:T(8,128)S(1)}, s32[40]{0:T(128)S(1)}) custom-call(s32[2,1,32]{2,1,0:T(1,128)S(1)} %bitcast.29, s32[2]{0:T(128)S(1)} %pad_add_fusion.where_ref, f32[19,128,128]{2,1,0:T(8,128)S(1)} %bitcast.26), custom_call_target="tpu_custom_call" | custom-call | bytes 319808 | tf_op jit(solution)/shard_map/pallas_call | solution.py:666
  7.8 1.9 %collective-permute-done.1.refs_2_ = f32[72,128]{1,0:T(8,128)S(1)} collective-permute-done((f32[72,128]{1,0:T(8,128)S(1)}, f32[72,128]{1,0:T(8,128)S(1)}, u32[]{:S(2)}, u32[]{:S(2)}) %collective-permute-start.1) | collective-permute-done | bytes 36896 | tf_op jit(solution)/shard_map/ppermute | solution.py:677
  9.6 0.1 collective-permute-done.refs_1_
  9.7 4.9 %shard_map.61 = (f32[3,128,128]{2,1,0:T(8,128)S(1)}, f32[104,128]{1,0:T(8,128)S(1)}, f32[104,128]{1,0:T(8,128)S(1)}, f32[32,16,128]{2,1,0:T(8,128)S(1)}) custom-call(s32[2,1,32]{2,1,0:T(1,128)S(1)} %bitcast.30, s32[2]{0:T(128)S(1)} %pad_add_fusion.where_ref, s32[40]{0:T(128)S(1)} %get-tuple-element.37.chosen_ref, s32[2]{0:T(128)S(1)} %copy-done.4, ...), custom_call_target="tpu_custom_call" | custom-call | bytes 1130496 | tf_op jit(solution)/shard_map/pallas_call | solution.py:666
  14.7 0.5 %collective-permute-start.3 = (f32[104,128]{1,0:T(8,128)S(1)}, f32[104,128]{1,0:T(8,128)S(1)}, u32[]{:S(2)}, u32[]{:S(2)}) collective-permute-start(f32[104,128]{1,0:T(8,128)S(1)} %get-tuple-element.45.own_ref), channel_id=1, source_target_pairs={{0,1},{1,2},{2,3},{3,0},{4,5},{5,6},{6,7},{7,4},{8,9},{9,10},{10,1... | collective-permute-start | bytes 159752 | tf_op jit(solution)/shard_map/ppermute | solution.py:677
  15.2 0.5 %shard_map.62 = (f32[19,128,128]{2,1,0:T(8,128)S(1)}, f32[160,128]{1,0:T(8,128)S(1)}, f32[160,128]{1,0:T(8,128)S(1)}) custom-call(f32[19,128,128]{2,1,0:T(8,128)S(1)} %bitcast.27, f32[3,128,128]{2,1,0:T(8,128)S(1)} %get-tuple-element.42.refs_1_), custom_call_target="tpu_custom_call" | custom-call | bytes 2818048 | tf_op jit(solution)/shard_map/pallas_call | solution.py:666
  15.7 0.8 %collective-permute-done.4.right_ref = f32[104,128]{1,0:T(8,128)S(1)} collective-permute-done((f32[104,128]{1,0:T(8,128)S(1)}, f32[104,128]{1,0:T(8,128)S(1)}, u32[]{:S(2)}, u32[]{:S(2)}) %collective-permute-start.4) | collective-permute-done | bytes 53280 | tf_op jit(solution)/shard_map/ppermute | solution.py:677
  16.5 1.9 %collective-permute-done.3.left_ref = f32[104,128]{1,0:T(8,128)S(1)} collective-permute-done((f32[104,128]{1,0:T(8,128)S(1)}, f32[104,128]{1,0:T(8,128)S(1)}, u32[]{:S(2)}, u32[]{:S(2)}) %collective-permute-start.3) | collective-permute-done | bytes 53280 | tf_op jit(solution)/shard_map/ppermute | solution.py:677
  18.4 0.1 shard_map.63
  18.5 1.6 %collective-permute-start.5 = (f32[176,128]{1,0:T(8,128)S(1)}, f32[176,128]{1,0:T(8,128)S(1)}, u32[]{:S(2)}, u32[]{:S(2)}) collective-permute-start(f32[176,128]{1,0:T(8,128)S(1)} %get-tuple-element.52), channel_id=1, source_target_pairs={{0,4},{4,8},{8,12},{12,16},{16,20},{20,24},{24,28},{28,0},{1,5},{5... | collective-permute-start | bytes 270344 | tf_op jit(solution)/shard_map/ppermute | solution.py:677
  20.1 3.2 %collective-permute-start.6 = (f32[176,128]{1,0:T(8,128)S(1)}, f32[176,128]{1,0:T(8,128)S(1)}, u32[]{:S(2)}, u32[]{:S(2)}) collective-permute-start(f32[176,128]{1,0:T(8,128)S(1)} %get-tuple-element.53), channel_id=1, source_target_pairs={{0,28},{4,0},{8,4},{12,8},{16,12},{20,16},{24,20},{28,24},{1,29},{... | collective-permute-start | bytes 270344 | tf_op jit(solution)/shard_map/ppermute | solution.py:677
  23.3 1.3 %shard_map.64 = (f32[19,128,128]{2,1,0:T(8,128)S(1)}, f32[19,8,128]{2,1,0:T(8,128)S(1)}) custom-call(f32[19,128,128]{2,1,0:T(8,128)S(1)} %get-tuple-element.43.post_ref, f32[19,8,128]{2,1,0:T(8,128)S(1)} %get-tuple-element.49.post_edge_ref), custom_call_target="tpu_custom_call" | custom-call | bytes 2646016 | tf_op jit(solution)/shard_map/pallas_call | solution.py:666
  24.6 1.2 %collective-permute-done.5.east_ref = f32[176,128]{1,0:T(8,128)S(1)} collective-permute-done((f32[176,128]{1,0:T(8,128)S(1)}, f32[176,128]{1,0:T(8,128)S(1)}, u32[]{:S(2)}, u32[]{:S(2)}) %collective-permute-start.5) | collective-permute-done | bytes 90144 | tf_op jit(solution)/shard_map/ppermute | solution.py:677
  25.8 0.7 %collective-permute-done.6.west_ref = f32[176,128]{1,0:T(8,128)S(1)} collective-permute-done((f32[176,128]{1,0:T(8,128)S(1)}, f32[176,128]{1,0:T(8,128)S(1)}, u32[]{:S(2)}, u32[]{:S(2)}) %collective-permute-start.6) | collective-permute-done | bytes 90144 | tf_op jit(solution)/shard_map/ppermute | solution.py:677
  26.5 5.0 %shard_map.65 = (f32[10,128,128]{2,1,0:T(8,128)S(1)}, f32[19,8,128]{2,1,0:T(8,128)S(1)}, f32[3,128,128]{2,1,0:T(8,128)S(1)}, f32[72,128]{1,0:T(8,128)S(1)}, f32[...) custom-call(s32[2]{0:T(128)S(1)} %pad_add_fusion.where_ref, s32[40]{0:T(128)S(1)} %get-tuple-element.37.chosen_ref, ...), custom_call_target="tpu_custom_call" | custom-call | bytes 2105344 | tf_op jit(solution)/shard_map/pallas_call | solution.py:666
  31.5 0.1 collective-permute-start.8
  31.6 0.5 %collective-permute-start.7 = (f32[72,128]{1,0:T(8,128)S(1)}, f32[72,128]{1,0:T(8,128)S(1)}, u32[]{:S(2)}, u32[]{:S(2)}) collective-permute-start(f32[72,128]{1,0:T(8,128)S(1)} %get-tuple-element.59.own_ref), channel_id=1, source_target_pairs={{0,1},{1,2},{2,3},{3,0},{4,5},{5,6},{6,7},{7,4},{8,9},{9,10},{10,1... | collective-permute-start | bytes 110600 | tf_op jit(solution)/shard_map/ppermute | solution.py:677
  32.1 0.9 %collective-permute-start.11 = (f32[48,128]{1,0:T(8,128)S(1)}, f32[48,128]{1,0:T(8,128)S(1)}, u32[]{:S(2)}, u32[]{:S(2)}) collective-permute-start(f32[48,128]{1,0:T(8,128)S(1)} %get-tuple-element.68), channel_id=1, source_target_pairs={{0,2},{1,3},{2,0},{3,1},{4,6},{5,7},{6,4},{7,5},{8,10},{9,11},{10,... | collective-permute-start | bytes 73736 | tf_op jit(solution)/shard_map/ppermute | solution.py:677
  33.0 0.5 %shard_map.66 = (f32[19,128,128]{2,1,0:T(8,128)S(1)}, f32[160,128]{1,0:T(8,128)S(1)}, f32[160,128]{1,0:T(8,128)S(1)}) custom-call(f32[19,128,128]{2,1,0:T(8,128)S(1)} %get-tuple-element.50.streamed_ref.refs_0_, f32[10,128,128]{2,1,0:T(8,128)S(1)} %get-tuple-element.55.refs_1_, f32[3,128,128]{2,1,0:T(8,128)S(1)} %get-tuple-element.56.refs_2_), custom_call_target="tpu_custom_call" | custom-call | bytes 2818048 | tf_op jit(solution)/shard_map/pallas_call | solution.py:666
  33.6 1.5 %collective-permute-done.7.left_ref = f32[72,128]{1,0:T(8,128)S(1)} collective-permute-done((f32[72,128]{1,0:T(8,128)S(1)}, f32[72,128]{1,0:T(8,128)S(1)}, u32[]{:S(2)}, u32[]{:S(2)}) %collective-permute-start.7) | collective-permute-done | bytes 36896 | tf_op jit(solution)/shard_map/ppermute | solution.py:677
  35.1 0.5 %collective-permute-start.9 = (f32[176,128]{1,0:T(8,128)S(1)}, f32[176,128]{1,0:T(8,128)S(1)}, u32[]{:S(2)}, u32[]{:S(2)}) collective-permute-start(f32[176,128]{1,0:T(8,128)S(1)} %get-tuple-element.65), channel_id=1, source_target_pairs={{0,4},{4,8},{8,12},{12,16},{16,20},{20,24},{24,28},{28,0},{1,5},{5... | collective-permute-start | bytes 270344 | tf_op jit(solution)/shard_map/ppermute | solution.py:677
  35.6 4.2 %collective-permute-start.10 = (f32[176,128]{1,0:T(8,128)S(1)}, f32[176,128]{1,0:T(8,128)S(1)}, u32[]{:S(2)}, u32[]{:S(2)}) collective-permute-start(f32[176,128]{1,0:T(8,128)S(1)} %get-tuple-element.66), channel_id=1, source_target_pairs={{0,28},{4,0},{8,4},{12,8},{16,12},{20,16},{24,20},{28,24},{1,29},{... | collective-permute-start | bytes 270344 | tf_op jit(solution)/shard_map/ppermute | solution.py:677
  39.9 1.8 %shard_map.68 = (f32[19,128,128]{2,1,0:T(8,128)}, f32[10,128,128]{2,1,0:T(8,128)S(1)}) custom-call(f32[19,128,128]{2,1,0:T(8,128)S(1)} %get-tuple-element.57.post_ref, f32[19,8,128]{2,1,0:T(8,128)S(1)} %get-tuple-element.63.post_edge_ref), custom_call_target="tpu_custom_call" | custom-call | bytes 3801088 | tf_op jit(solution)/shard_map/pallas_call | solution.py:666
  41.7 0.7 %collective-permute-done.9.east_ref = f32[176,128]{1,0:T(8,128)S(1)} collective-permute-done((f32[176,128]{1,0:T(8,128)S(1)}, f32[176,128]{1,0:T(8,128)S(1)}, u32[]{:S(2)}, u32[]{:S(2)}) %collective-permute-start.9) | collective-permute-done | bytes 90144 | tf_op jit(solution)/shard_map/ppermute | solution.py:677
  42.4 1.1 %shard_map.69 = (f32[19,128,128]{2,1,0:T(8,128)}, f32[48,128]{1,0:T(8,128)}) custom-call(f32[19,128,128]{2,1,0:T(8,128)S(1)} %get-tuple-element.57.post_ref, f32[19,8,128]{2,1,0:T(8,128)S(1)} %get-tuple-element.63.post_edge_ref, f32[10,128,128]{2,1,0:T(8,128)S(1)} %get-tuple-element.64.before_ref, ...), custom_call_target="tpu_custom_call", output_to_operand_aliasing={{0}: (6, {})} | custom-call | bytes 2539520 | tf_op jit(solution)/shard_map/pallas_call | solution.py:666
  (15 shorter events, 0.1 us)
Async XLA Ops:
  0.6 5.6 %copy-start.3 = (s32[2,32,1]{1,2,0:T(1,128)S(1)}, s32[2,32,1]{1,2,0:T(1,128)}, u32[]{:S(2)}) copy-start(s32[2,32,1]{1,2,0:T(1,128)} %param.6) | copy-start | bytes 772
  0.6 1.3 %copy-start = (f32[19,16,4,256]{3,2,1,0:T(4,128)S(1)}, f32[19,16,4,256]{3,2,1,0:T(4,128)}, u32[]{:S(2)}) copy-start(f32[19,16,4,256]{3,2,1,0:T(4,128)} %param.4) | copy-start | bytes 3735556
  1.9 0.7 %copy-start.2 = (f32[2,3,1024]{2,0,1:T(2,128)S(1)}, f32[2,3,1024]{2,0,1:T(2,128)}, u32[]{:S(2)}) copy-start(f32[2,3,1024]{2,0,1:T(2,128)} %param.5) | copy-start | bytes 73732
  2.7 3.5 %copy-start.1 = (f32[19,16,4,256]{3,2,1,0:T(4,128)S(1)}, f32[19,16,4,256]{3,2,1,0:T(4,128)}, u32[]{:S(2)}) copy-start(f32[19,16,4,256]{3,2,1,0:T(4,128)} %param.4) | copy-start | bytes 3735556
  2.7 7.0 %copy-start.4 = (s32[2]{0:T(128)S(1)}, s32[2]{0:T(128)}, u32[]{:S(2)}) copy-start(s32[2]{0:T(128)} %stiff_ref.1) | copy-start | bytes 28
  2.9 4.8 %collective-permute-start.2 = (f32[72,128]{1,0:T(8,128)S(1)}, f32[72,128]{1,0:T(8,128)S(1)}, u32[]{:S(2)}, u32[]{:S(2)}) collective-permute-start(f32[72,128]{1,0:T(8,128)S(1)} %get-tuple-element.41.refs_0_), channel_id=1, source_target_pairs={{0,3},{1,0},{2,1},{3,2},{4,7},{5,4},{6,5},{7,6},{8,11},{9,8},{10,9... | collective-permute-start | bytes 110600 | tf_op jit(solution)/shard_map/ppermute | solution.py:677
  5.3 4.3 %collective-permute-start.1 = (f32[72,128]{1,0:T(8,128)S(1)}, f32[72,128]{1,0:T(8,128)S(1)}, u32[]{:S(2)}, u32[]{:S(2)}) collective-permute-start(f32[72,128]{1,0:T(8,128)S(1)} %get-tuple-element.41.refs_0_), channel_id=1, source_target_pairs={{0,2},{1,3},{2,0},{3,1},{4,6},{5,7},{6,4},{7,5},{8,10},{9,11},{10,... | collective-permute-start | bytes 110600 | tf_op jit(solution)/shard_map/ppermute | solution.py:677
  6.0 3.7 %collective-permute-start = (f32[72,128]{1,0:T(8,128)S(1)}, f32[72,128]{1,0:T(8,128)S(1)}, u32[]{:S(2)}, u32[]{:S(2)}) collective-permute-start(f32[72,128]{1,0:T(8,128)S(1)} %get-tuple-element.41.refs_0_), channel_id=1, source_target_pairs={{0,1},{1,2},{2,3},{3,0},{4,5},{5,6},{6,7},{7,4},{8,9},{9,10},{10,1... | collective-permute-start | bytes 110600 | tf_op jit(solution)/shard_map/ppermute | solution.py:677
  14.6 1.8 %collective-permute-start.4 = (f32[104,128]{1,0:T(8,128)S(1)}, f32[104,128]{1,0:T(8,128)S(1)}, u32[]{:S(2)}, u32[]{:S(2)}) collective-permute-start(f32[104,128]{1,0:T(8,128)S(1)} %get-tuple-element.46), channel_id=1, source_target_pairs={{0,3},{1,0},{2,1},{3,2},{4,7},{5,4},{6,5},{7,6},{8,11},{9,8},{10,9... | collective-permute-start | bytes 159752 | tf_op jit(solution)/shard_map/ppermute | solution.py:677
  14.7 3.7 %collective-permute-start.3 = (f32[104,128]{1,0:T(8,128)S(1)}, f32[104,128]{1,0:T(8,128)S(1)}, u32[]{:S(2)}, u32[]{:S(2)}) collective-permute-start(f32[104,128]{1,0:T(8,128)S(1)} %get-tuple-element.45.own_ref), channel_id=1, source_target_pairs={{0,1},{1,2},{2,3},{3,0},{4,5},{5,6},{6,7},{7,4},{8,9},{9,10},{10,1... | collective-permute-start | bytes 159752 | tf_op jit(solution)/shard_map/ppermute | solution.py:677
  18.5 7.3 %collective-permute-start.5 = (f32[176,128]{1,0:T(8,128)S(1)}, f32[176,128]{1,0:T(8,128)S(1)}, u32[]{:S(2)}, u32[]{:S(2)}) collective-permute-start(f32[176,128]{1,0:T(8,128)S(1)} %get-tuple-element.52), channel_id=1, source_target_pairs={{0,4},{4,8},{8,12},{12,16},{16,20},{20,24},{24,28},{28,0},{1,5},{5... | collective-permute-start | bytes 270344 | tf_op jit(solution)/shard_map/ppermute | solution.py:677
  20.1 6.5 %collective-permute-start.6 = (f32[176,128]{1,0:T(8,128)S(1)}, f32[176,128]{1,0:T(8,128)S(1)}, u32[]{:S(2)}, u32[]{:S(2)}) collective-permute-start(f32[176,128]{1,0:T(8,128)S(1)} %get-tuple-element.53), channel_id=1, source_target_pairs={{0,28},{4,0},{8,4},{12,8},{16,12},{20,16},{24,20},{28,24},{1,29},{... | collective-permute-start | bytes 270344 | tf_op jit(solution)/shard_map/ppermute | solution.py:677
  31.5 2.0 %collective-permute-start.8 = (f32[72,128]{1,0:T(8,128)S(1)}, f32[72,128]{1,0:T(8,128)S(1)}, u32[]{:S(2)}, u32[]{:S(2)}) collective-permute-start(f32[72,128]{1,0:T(8,128)S(1)} %get-tuple-element.60), channel_id=1, source_target_pairs={{0,3},{1,0},{2,1},{3,2},{4,7},{5,4},{6,5},{7,6},{8,11},{9,8},{10,9... | collective-permute-start | bytes 110600 | tf_op jit(solution)/shard_map/ppermute | solution.py:677
  31.6 3.4 %collective-permute-start.7 = (f32[72,128]{1,0:T(8,128)S(1)}, f32[72,128]{1,0:T(8,128)S(1)}, u32[]{:S(2)}, u32[]{:S(2)}) collective-permute-start(f32[72,128]{1,0:T(8,128)S(1)} %get-tuple-element.59.own_ref), channel_id=1, source_target_pairs={{0,1},{1,2},{2,3},{3,0},{4,5},{5,6},{6,7},{7,4},{8,9},{9,10},{10,1... | collective-permute-start | bytes 110600 | tf_op jit(solution)/shard_map/ppermute | solution.py:677
  32.1 7.8 %collective-permute-start.11 = (f32[48,128]{1,0:T(8,128)S(1)}, f32[48,128]{1,0:T(8,128)S(1)}, u32[]{:S(2)}, u32[]{:S(2)}) collective-permute-start(f32[48,128]{1,0:T(8,128)S(1)} %get-tuple-element.68), channel_id=1, source_target_pairs={{0,2},{1,3},{2,0},{3,1},{4,6},{5,7},{6,4},{7,5},{8,10},{9,11},{10,... | collective-permute-start | bytes 73736 | tf_op jit(solution)/shard_map/ppermute | solution.py:677
  35.1 7.3 %collective-permute-start.9 = (f32[176,128]{1,0:T(8,128)S(1)}, f32[176,128]{1,0:T(8,128)S(1)}, u32[]{:S(2)}, u32[]{:S(2)}) collective-permute-start(f32[176,128]{1,0:T(8,128)S(1)} %get-tuple-element.65), channel_id=1, source_target_pairs={{0,4},{4,8},{8,12},{12,16},{16,20},{20,24},{24,28},{28,0},{1,5},{5... | collective-permute-start | bytes 270344 | tf_op jit(solution)/shard_map/ppermute | solution.py:677
  35.6 6.7 %collective-permute-start.10 = (f32[176,128]{1,0:T(8,128)S(1)}, f32[176,128]{1,0:T(8,128)S(1)}, u32[]{:S(2)}, u32[]{:S(2)}) collective-permute-start(f32[176,128]{1,0:T(8,128)S(1)} %get-tuple-element.66), channel_id=1, source_target_pairs={{0,28},{4,0},{8,4},{12,8},{16,12},{20,16},{24,20},{28,24},{1,29},{... | collective-permute-start | bytes 270344 | tf_op jit(solution)/shard_map/ppermute | solution.py:677

commit v7 on v6

--- a/solution.py
+++ b/solution.py
@@ -311,7 +311,15 @@
             cells = [basis_cells([field[yf][half] for yf in range(3)]) for half in range(2)]
             sums = None
             for k, shift in enumerate((1, 0, -1, -2)):
-                tiles = shifted([zero, zero, cells[0][k], cells[1][k], zero, zero], shift)
+                low, high = (turn(cells[half][k], -shift, 1) for half in range(2))
+                if shift == 1:
+                    last = lane == 127
+                    tiles = [jnp.where(last, low, zero), jnp.where(last, high, low), jnp.where(last, zero, high), zero]
+                elif shift == 0:
+                    tiles = [zero, low, high, zero]
+                else:
+                    begin = lane < -shift
+                    tiles = [zero, jnp.where(begin, zero, low), jnp.where(begin, low, high), jnp.where(begin, high, zero)]
                 sums = tiles if sums is None else [a + b for a, b in zip(sums, tiles)]
             by_basis.append(sums)
         by_x = [basis_cells([by_basis[xf][t] * unscale for xf in range(3)]) for t in range(4)]

time: 43.6 us -> 43.6 us (level)
  no operation moved by 1% of the time
where the time goes in v7:
time: 43.6 us; the launch traced here: 43.4 us
  Pallas kernels  16.9 us (39%)
  starting transfers between devices  14.8 us (34%)
  waiting for transfers between devices  8.81 us (20%)
  local copies, waits for them, and re-layouts  2.04 us (5%)
  between operations  0.76 us (2%)
    pallas_call x11, Pallas kernels, call(): pl.pallas_call(body, out_shape=[jax.ShapeDtypeStruct(*out) for out in out...  16.9 us
    ppermute x12, starting transfers between devices, ring(): lax.ppermute(value, axis, [(i, (i + step) % count) for i in range(count)])  14.8 us
    ppermute x12, waiting for transfers between devices, ring(): lax.ppermute(value, axis, [(i, (i + step) % count) for i in range(count)])  8.81 us
    unnamed x10, local copies, waits for them, and re-layouts  2.04 us
  transfers between devices with their start and end apart: 12, of which 8 were waited for; matrix products, arithmetic and copies ran while one was open for 0% of the time, Pallas kernels for 13%

profile of v7, /device:TPU:0, one launch (start us, length us, event | category | flops | bytes accessed | tf_op | source)
XLA Modules:
  0.0 43.4 jit_solution(16132634765358077322)
XLA Ops:
  0.7 1.3 %copy-done = f32[19,16,4,256]{3,2,1,0:T(4,128)S(1)} copy-done((f32[19,16,4,256]{3,2,1,0:T(4,128)S(1)}, f32[19,16,4,256]{3,2,1,0:T(4,128)}, u32[]{:S(2)}) %copy-start) | copy-done | bytes 1245208
  1.9 0.7 %copy-done.2 = f32[2,3,1024]{2,0,1:T(2,128)S(1)} copy-done((f32[2,3,1024]{2,0,1:T(2,128)S(1)}, f32[2,3,1024]{2,0,1:T(2,128)}, u32[]{:S(2)}) %copy-start.2) | copy-done | bytes 24600
  2.7 0.2 shard_map.60
  2.9 2.4 %collective-permute-start.2 = (f32[72,128]{1,0:T(8,128)S(1)}, f32[72,128]{1,0:T(8,128)S(1)}, u32[]{:S(2)}, u32[]{:S(2)}) collective-permute-start(f32[72,128]{1,0:T(8,128)S(1)} %get-tuple-element.41.refs_0_), channel_id=1, source_target_pairs={{0,3},{1,0},{2,1},{3,2},{4,7},{5,4},{6,5},{7,6},{8,11},{9,8},{10,9... | collective-permute-start | bytes 110600 | tf_op jit(solution)/shard_map/ppermute | solution.py:685
  5.3 0.6 %collective-permute-start.1 = (f32[72,128]{1,0:T(8,128)S(1)}, f32[72,128]{1,0:T(8,128)S(1)}, u32[]{:S(2)}, u32[]{:S(2)}) collective-permute-start(f32[72,128]{1,0:T(8,128)S(1)} %get-tuple-element.41.refs_0_), channel_id=1, source_target_pairs={{0,2},{1,3},{2,0},{3,1},{4,6},{5,7},{6,4},{7,5},{8,10},{9,11},{10,... | collective-permute-start | bytes 110600 | tf_op jit(solution)/shard_map/ppermute | solution.py:685
  6.0 0.2 collective-permute-start
  6.1 0.1 pad_add_fusion.where_ref
  6.2 1.5 %shard_map.59 = (f32[19,8,128]{2,1,0:T(8,128)S(1)}, f32[80,128]{1,0:T(8,128)S(1)}, f32[80,128]{1,0:T(8,128)S(1)}, s32[40]{0:T(128)S(1)}) custom-call(s32[2,1,32]{2,1,0:T(1,128)S(1)} %bitcast.29, s32[2]{0:T(128)S(1)} %pad_add_fusion.where_ref, f32[19,128,128]{2,1,0:T(8,128)S(1)} %bitcast.26), custom_call_target="tpu_custom_call" | custom-call | bytes 319808 | tf_op jit(solution)/shard_map/pallas_call | solution.py:674
  7.8 1.9 %collective-permute-done.1.refs_2_ = f32[72,128]{1,0:T(8,128)S(1)} collective-permute-done((f32[72,128]{1,0:T(8,128)S(1)}, f32[72,128]{1,0:T(8,128)S(1)}, u32[]{:S(2)}, u32[]{:S(2)}) %collective-permute-start.1) | collective-permute-done | bytes 36896 | tf_op jit(solution)/shard_map/ppermute | solution.py:685
  9.6 0.1 collective-permute-done.refs_1_
  9.7 4.9 %shard_map.61 = (f32[3,128,128]{2,1,0:T(8,128)S(1)}, f32[104,128]{1,0:T(8,128)S(1)}, f32[104,128]{1,0:T(8,128)S(1)}, f32[32,16,128]{2,1,0:T(8,128)S(1)}) custom-call(s32[2,1,32]{2,1,0:T(1,128)S(1)} %bitcast.30, s32[2]{0:T(128)S(1)} %pad_add_fusion.where_ref, s32[40]{0:T(128)S(1)} %get-tuple-element.37.chosen_ref, s32[2]{0:T(128)S(1)} %copy-done.4, ...), custom_call_target="tpu_custom_call" | custom-call | bytes 1130496 | tf_op jit(solution)/shard_map/pallas_call | solution.py:674
  14.6 0.1 collective-permute-start.4
  14.7 0.5 %collective-permute-start.3 = (f32[104,128]{1,0:T(8,128)S(1)}, f32[104,128]{1,0:T(8,128)S(1)}, u32[]{:S(2)}, u32[]{:S(2)}) collective-permute-start(f32[104,128]{1,0:T(8,128)S(1)} %get-tuple-element.45.own_ref), channel_id=1, source_target_pairs={{0,1},{1,2},{2,3},{3,0},{4,5},{5,6},{6,7},{7,4},{8,9},{9,10},{10,1... | collective-permute-start | bytes 159752 | tf_op jit(solution)/shard_map/ppermute | solution.py:685
  15.2 0.5 %shard_map.62 = (f32[19,128,128]{2,1,0:T(8,128)S(1)}, f32[160,128]{1,0:T(8,128)S(1)}, f32[160,128]{1,0:T(8,128)S(1)}) custom-call(f32[19,128,128]{2,1,0:T(8,128)S(1)} %bitcast.27, f32[3,128,128]{2,1,0:T(8,128)S(1)} %get-tuple-element.42.refs_1_), custom_call_target="tpu_custom_call" | custom-call | bytes 2818048 | tf_op jit(solution)/shard_map/pallas_call | solution.py:674
  15.7 0.8 %collective-permute-done.4.right_ref = f32[104,128]{1,0:T(8,128)S(1)} collective-permute-done((f32[104,128]{1,0:T(8,128)S(1)}, f32[104,128]{1,0:T(8,128)S(1)}, u32[]{:S(2)}, u32[]{:S(2)}) %collective-permute-start.4) | collective-permute-done | bytes 53280 | tf_op jit(solution)/shard_map/ppermute | solution.py:685
  16.5 2.0 %collective-permute-done.3.left_ref = f32[104,128]{1,0:T(8,128)S(1)} collective-permute-done((f32[104,128]{1,0:T(8,128)S(1)}, f32[104,128]{1,0:T(8,128)S(1)}, u32[]{:S(2)}, u32[]{:S(2)}) %collective-permute-start.3) | collective-permute-done | bytes 53280 | tf_op jit(solution)/shard_map/ppermute | solution.py:685
  18.4 0.1 shard_map.63
  18.5 1.6 %collective-permute-start.5 = (f32[176,128]{1,0:T(8,128)S(1)}, f32[176,128]{1,0:T(8,128)S(1)}, u32[]{:S(2)}, u32[]{:S(2)}) collective-permute-start(f32[176,128]{1,0:T(8,128)S(1)} %get-tuple-element.52), channel_id=1, source_target_pairs={{0,4},{4,8},{8,12},{12,16},{16,20},{20,24},{24,28},{28,0},{1,5},{5... | collective-permute-start | bytes 270344 | tf_op jit(solution)/shard_map/ppermute | solution.py:685
  20.1 3.2 %collective-permute-start.6 = (f32[176,128]{1,0:T(8,128)S(1)}, f32[176,128]{1,0:T(8,128)S(1)}, u32[]{:S(2)}, u32[]{:S(2)}) collective-permute-start(f32[176,128]{1,0:T(8,128)S(1)} %get-tuple-element.53), channel_id=1, source_target_pairs={{0,28},{4,0},{8,4},{12,8},{16,12},{20,16},{24,20},{28,24},{1,29},{... | collective-permute-start | bytes 270344 | tf_op jit(solution)/shard_map/ppermute | solution.py:685
  23.3 1.3 %shard_map.64 = (f32[19,128,128]{2,1,0:T(8,128)S(1)}, f32[19,8,128]{2,1,0:T(8,128)S(1)}) custom-call(f32[19,128,128]{2,1,0:T(8,128)S(1)} %get-tuple-element.43.post_ref, f32[19,8,128]{2,1,0:T(8,128)S(1)} %get-tuple-element.49.post_edge_ref), custom_call_target="tpu_custom_call" | custom-call | bytes 2646016 | tf_op jit(solution)/shard_map/pallas_call | solution.py:674
  24.6 1.3 %collective-permute-done.5.east_ref = f32[176,128]{1,0:T(8,128)S(1)} collective-permute-done((f32[176,128]{1,0:T(8,128)S(1)}, f32[176,128]{1,0:T(8,128)S(1)}, u32[]{:S(2)}, u32[]{:S(2)}) %collective-permute-start.5) | collective-permute-done | bytes 90144 | tf_op jit(solution)/shard_map/ppermute | solution.py:685
  25.8 0.7 %collective-permute-done.6.west_ref = f32[176,128]{1,0:T(8,128)S(1)} collective-permute-done((f32[176,128]{1,0:T(8,128)S(1)}, f32[176,128]{1,0:T(8,128)S(1)}, u32[]{:S(2)}, u32[]{:S(2)}) %collective-permute-start.6) | collective-permute-done | bytes 90144 | tf_op jit(solution)/shard_map/ppermute | solution.py:685
  26.5 5.0 %shard_map.65 = (f32[10,128,128]{2,1,0:T(8,128)S(1)}, f32[19,8,128]{2,1,0:T(8,128)S(1)}, f32[3,128,128]{2,1,0:T(8,128)S(1)}, f32[72,128]{1,0:T(8,128)S(1)}, f32[...) custom-call(s32[2]{0:T(128)S(1)} %pad_add_fusion.where_ref, s32[40]{0:T(128)S(1)} %get-tuple-element.37.chosen_ref, ...), custom_call_target="tpu_custom_call" | custom-call | bytes 2105344 | tf_op jit(solution)/shard_map/pallas_call | solution.py:674
  31.6 0.5 %collective-permute-start.7 = (f32[72,128]{1,0:T(8,128)S(1)}, f32[72,128]{1,0:T(8,128)S(1)}, u32[]{:S(2)}, u32[]{:S(2)}) collective-permute-start(f32[72,128]{1,0:T(8,128)S(1)} %get-tuple-element.59.own_ref), channel_id=1, source_target_pairs={{0,1},{1,2},{2,3},{3,0},{4,5},{5,6},{6,7},{7,4},{8,9},{9,10},{10,1... | collective-permute-start | bytes 110600 | tf_op jit(solution)/shard_map/ppermute | solution.py:685
  32.1 0.9 %collective-permute-start.11 = (f32[48,128]{1,0:T(8,128)S(1)}, f32[48,128]{1,0:T(8,128)S(1)}, u32[]{:S(2)}, u32[]{:S(2)}) collective-permute-start(f32[48,128]{1,0:T(8,128)S(1)} %get-tuple-element.68), channel_id=1, source_target_pairs={{0,2},{1,3},{2,0},{3,1},{4,6},{5,7},{6,4},{7,5},{8,10},{9,11},{10,... | collective-permute-start | bytes 73736 | tf_op jit(solution)/shard_map/ppermute | solution.py:685
  33.0 0.5 %shard_map.66 = (f32[19,128,128]{2,1,0:T(8,128)S(1)}, f32[160,128]{1,0:T(8,128)S(1)}, f32[160,128]{1,0:T(8,128)S(1)}) custom-call(f32[19,128,128]{2,1,0:T(8,128)S(1)} %get-tuple-element.50.streamed_ref.refs_0_, f32[10,128,128]{2,1,0:T(8,128)S(1)} %get-tuple-element.55.refs_1_, f32[3,128,128]{2,1,0:T(8,128)S(1)} %get-tuple-element.56.refs_2_), custom_call_target="tpu_custom_call" | custom-call | bytes 2818048 | tf_op jit(solution)/shard_map/pallas_call | solution.py:674
  33.6 1.5 %collective-permute-done.7.left_ref = f32[72,128]{1,0:T(8,128)S(1)} collective-permute-done((f32[72,128]{1,0:T(8,128)S(1)}, f32[72,128]{1,0:T(8,128)S(1)}, u32[]{:S(2)}, u32[]{:S(2)}) %collective-permute-start.7) | collective-permute-done | bytes 36896 | tf_op jit(solution)/shard_map/ppermute | solution.py:685
  35.1 0.5 %collective-permute-start.9 = (f32[176,128]{1,0:T(8,128)S(1)}, f32[176,128]{1,0:T(8,128)S(1)}, u32[]{:S(2)}, u32[]{:S(2)}) collective-permute-start(f32[176,128]{1,0:T(8,128)S(1)} %get-tuple-element.65), channel_id=1, source_target_pairs={{0,4},{4,8},{8,12},{12,16},{16,20},{20,24},{24,28},{28,0},{1,5},{5... | collective-permute-start | bytes 270344 | tf_op jit(solution)/shard_map/ppermute | solution.py:685
  35.7 4.2 %collective-permute-start.10 = (f32[176,128]{1,0:T(8,128)S(1)}, f32[176,128]{1,0:T(8,128)S(1)}, u32[]{:S(2)}, u32[]{:S(2)}) collective-permute-start(f32[176,128]{1,0:T(8,128)S(1)} %get-tuple-element.66), channel_id=1, source_target_pairs={{0,28},{4,0},{8,4},{12,8},{16,12},{20,16},{24,20},{28,24},{1,29},{... | collective-permute-start | bytes 270344 | tf_op jit(solution)/shard_map/ppermute | solution.py:685
  39.9 1.8 %shard_map.68 = (f32[19,128,128]{2,1,0:T(8,128)}, f32[10,128,128]{2,1,0:T(8,128)S(1)}) custom-call(f32[19,128,128]{2,1,0:T(8,128)S(1)} %get-tuple-element.57.post_ref, f32[19,8,128]{2,1,0:T(8,128)S(1)} %get-tuple-element.63.post_edge_ref), custom_call_target="tpu_custom_call" | custom-call | bytes 3801088 | tf_op jit(solution)/shard_map/pallas_call | solution.py:674
  41.7 0.7 %collective-permute-done.9.east_ref = f32[176,128]{1,0:T(8,128)S(1)} collective-permute-done((f32[176,128]{1,0:T(8,128)S(1)}, f32[176,128]{1,0:T(8,128)S(1)}, u32[]{:S(2)}, u32[]{:S(2)}) %collective-permute-start.9) | collective-permute-done | bytes 90144 | tf_op jit(solution)/shard_map/ppermute | solution.py:685
  42.4 1.1 %shard_map.69 = (f32[19,128,128]{2,1,0:T(8,128)}, f32[48,128]{1,0:T(8,128)}) custom-call(f32[19,128,128]{2,1,0:T(8,128)S(1)} %get-tuple-element.57.post_ref, f32[19,8,128]{2,1,0:T(8,128)S(1)} %get-tuple-element.63.post_edge_ref, f32[10,128,128]{2,1,0:T(8,128)S(1)} %get-tuple-element.64.before_ref, ...), custom_call_target="tpu_custom_call", output_to_operand_aliasing={{0}: (6, {})} | custom-call | bytes 2539520 | tf_op jit(solution)/shard_map/pallas_call | solution.py:674
  (15 shorter events, 0.1 us)
Async XLA Ops:
  0.6 5.6 %copy-start.3 = (s32[2,32,1]{1,2,0:T(1,128)S(1)}, s32[2,32,1]{1,2,0:T(1,128)}, u32[]{:S(2)}) copy-start(s32[2,32,1]{1,2,0:T(1,128)} %param.6) | copy-start | bytes 772
  0.6 1.3 %copy-start = (f32[19,16,4,256]{3,2,1,0:T(4,128)S(1)}, f32[19,16,4,256]{3,2,1,0:T(4,128)}, u32[]{:S(2)}) copy-start(f32[19,16,4,256]{3,2,1,0:T(4,128)} %param.4) | copy-start | bytes 3735556
  1.9 0.7 %copy-start.2 = (f32[2,3,1024]{2,0,1:T(2,128)S(1)}, f32[2,3,1024]{2,0,1:T(2,128)}, u32[]{:S(2)}) copy-start(f32[2,3,1024]{2,0,1:T(2,128)} %param.5) | copy-start | bytes 73732
  2.7 3.5 %copy-start.1 = (f32[19,16,4,256]{3,2,1,0:T(4,128)S(1)}, f32[19,16,4,256]{3,2,1,0:T(4,128)}, u32[]{:S(2)}) copy-start(f32[19,16,4,256]{3,2,1,0:T(4,128)} %param.4) | copy-start | bytes 3735556
  2.7 7.0 %copy-start.4 = (s32[2]{0:T(128)S(1)}, s32[2]{0:T(128)}, u32[]{:S(2)}) copy-start(s32[2]{0:T(128)} %stiff_ref.1) | copy-start | bytes 28
  2.9 4.8 %collective-permute-start.2 = (f32[72,128]{1,0:T(8,128)S(1)}, f32[72,128]{1,0:T(8,128)S(1)}, u32[]{:S(2)}, u32[]{:S(2)}) collective-permute-start(f32[72,128]{1,0:T(8,128)S(1)} %get-tuple-element.41.refs_0_), channel_id=1, source_target_pairs={{0,3},{1,0},{2,1},{3,2},{4,7},{5,4},{6,5},{7,6},{8,11},{9,8},{10,9... | collective-permute-start | bytes 110600 | tf_op jit(solution)/shard_map/ppermute | solution.py:685
  5.3 4.3 %collective-permute-start.1 = (f32[72,128]{1,0:T(8,128)S(1)}, f32[72,128]{1,0:T(8,128)S(1)}, u32[]{:S(2)}, u32[]{:S(2)}) collective-permute-start(f32[72,128]{1,0:T(8,128)S(1)} %get-tuple-element.41.refs_0_), channel_id=1, source_target_pairs={{0,2},{1,3},{2,0},{3,1},{4,6},{5,7},{6,4},{7,5},{8,10},{9,11},{10,... | collective-permute-start | bytes 110600 | tf_op jit(solution)/shard_map/ppermute | solution.py:685
  6.0 3.7 %collective-permute-start = (f32[72,128]{1,0:T(8,128)S(1)}, f32[72,128]{1,0:T(8,128)S(1)}, u32[]{:S(2)}, u32[]{:S(2)}) collective-permute-start(f32[72,128]{1,0:T(8,128)S(1)} %get-tuple-element.41.refs_0_), channel_id=1, source_target_pairs={{0,1},{1,2},{2,3},{3,0},{4,5},{5,6},{6,7},{7,4},{8,9},{9,10},{10,1... | collective-permute-start | bytes 110600 | tf_op jit(solution)/shard_map/ppermute | solution.py:685
  14.6 1.8 %collective-permute-start.4 = (f32[104,128]{1,0:T(8,128)S(1)}, f32[104,128]{1,0:T(8,128)S(1)}, u32[]{:S(2)}, u32[]{:S(2)}) collective-permute-start(f32[104,128]{1,0:T(8,128)S(1)} %get-tuple-element.46), channel_id=1, source_target_pairs={{0,3},{1,0},{2,1},{3,2},{4,7},{5,4},{6,5},{7,6},{8,11},{9,8},{10,9... | collective-permute-start | bytes 159752 | tf_op jit(solution)/shard_map/ppermute | solution.py:685
  14.7 3.7 %collective-permute-start.3 = (f32[104,128]{1,0:T(8,128)S(1)}, f32[104,128]{1,0:T(8,128)S(1)}, u32[]{:S(2)}, u32[]{:S(2)}) collective-permute-start(f32[104,128]{1,0:T(8,128)S(1)} %get-tuple-element.45.own_ref), channel_id=1, source_target_pairs={{0,1},{1,2},{2,3},{3,0},{4,5},{5,6},{6,7},{7,4},{8,9},{9,10},{10,1... | collective-permute-start | bytes 159752 | tf_op jit(solution)/shard_map/ppermute | solution.py:685
  18.5 7.3 %collective-permute-start.5 = (f32[176,128]{1,0:T(8,128)S(1)}, f32[176,128]{1,0:T(8,128)S(1)}, u32[]{:S(2)}, u32[]{:S(2)}) collective-permute-start(f32[176,128]{1,0:T(8,128)S(1)} %get-tuple-element.52), channel_id=1, source_target_pairs={{0,4},{4,8},{8,12},{12,16},{16,20},{20,24},{24,28},{28,0},{1,5},{5... | collective-permute-start | bytes 270344 | tf_op jit(solution)/shard_map/ppermute | solution.py:685
  20.1 6.5 %collective-permute-start.6 = (f32[176,128]{1,0:T(8,128)S(1)}, f32[176,128]{1,0:T(8,128)S(1)}, u32[]{:S(2)}, u32[]{:S(2)}) collective-permute-start(f32[176,128]{1,0:T(8,128)S(1)} %get-tuple-element.53), channel_id=1, source_target_pairs={{0,28},{4,0},{8,4},{12,8},{16,12},{20,16},{24,20},{28,24},{1,29},{... | collective-permute-start | bytes 270344 | tf_op jit(solution)/shard_map/ppermute | solution.py:685
  31.6 2.0 %collective-permute-start.8 = (f32[72,128]{1,0:T(8,128)S(1)}, f32[72,128]{1,0:T(8,128)S(1)}, u32[]{:S(2)}, u32[]{:S(2)}) collective-permute-start(f32[72,128]{1,0:T(8,128)S(1)} %get-tuple-element.60), channel_id=1, source_target_pairs={{0,3},{1,0},{2,1},{3,2},{4,7},{5,4},{6,5},{7,6},{8,11},{9,8},{10,9... | collective-permute-start | bytes 110600 | tf_op jit(solution)/shard_map/ppermute | solution.py:685
  31.6 3.4 %collective-permute-start.7 = (f32[72,128]{1,0:T(8,128)S(1)}, f32[72,128]{1,0:T(8,128)S(1)}, u32[]{:S(2)}, u32[]{:S(2)}) collective-permute-start(f32[72,128]{1,0:T(8,128)S(1)} %get-tuple-element.59.own_ref), channel_id=1, source_target_pairs={{0,1},{1,2},{2,3},{3,0},{4,5},{5,6},{6,7},{7,4},{8,9},{9,10},{10,1... | collective-permute-start | bytes 110600 | tf_op jit(solution)/shard_map/ppermute | solution.py:685
  32.1 7.8 %collective-permute-start.11 = (f32[48,128]{1,0:T(8,128)S(1)}, f32[48,128]{1,0:T(8,128)S(1)}, u32[]{:S(2)}, u32[]{:S(2)}) collective-permute-start(f32[48,128]{1,0:T(8,128)S(1)} %get-tuple-element.68), channel_id=1, source_target_pairs={{0,2},{1,3},{2,0},{3,1},{4,6},{5,7},{6,4},{7,5},{8,10},{9,11},{10,... | collective-permute-start | bytes 73736 | tf_op jit(solution)/shard_map/ppermute | solution.py:685
  35.1 7.3 %collective-permute-start.9 = (f32[176,128]{1,0:T(8,128)S(1)}, f32[176,128]{1,0:T(8,128)S(1)}, u32[]{:S(2)}, u32[]{:S(2)}) collective-permute-start(f32[176,128]{1,0:T(8,128)S(1)} %get-tuple-element.65), channel_id=1, source_target_pairs={{0,4},{4,8},{8,12},{12,16},{16,20},{20,24},{24,28},{28,0},{1,5},{5... | collective-permute-start | bytes 270344 | tf_op jit(solution)/shard_map/ppermute | solution.py:685
  35.7 6.7 %collective-permute-start.10 = (f32[176,128]{1,0:T(8,128)S(1)}, f32[176,128]{1,0:T(8,128)S(1)}, u32[]{:S(2)}, u32[]{:S(2)}) collective-permute-start(f32[176,128]{1,0:T(8,128)S(1)} %get-tuple-element.66), channel_id=1, source_target_pairs={{0,28},{4,0},{8,4},{12,8},{16,12},{20,16},{24,20},{28,24},{1,29},{... | collective-permute-start | bytes 270344 | tf_op jit(solution)/shard_map/ppermute | solution.py:685

commit v8 on v7

--- a/solution.py
+++ b/solution.py
@@ -139,13 +139,14 @@
     row, _ = iotas()
     filaments, _, blocks = spans_ref.shape
     slots, mine = chosen_ref.shape[0] - 8, where_ref[1]
+    for n in range(slots):
+        chosen_ref[n] = filaments * blocks
     count = jnp.int32(0)
     for f in range(filaments):
         for k in range(blocks):
             chosen_ref[count] = f * blocks + k
             count = count + (spans_ref[f, 0, k] == mine).astype(jnp.int32)
-    for n in range(slots):
-        chosen_ref[n] = jnp.where(n < count, chosen_ref[n], filaments * blocks)
+    chosen_ref[count] = filaments * blocks
     chosen_ref[slots] = count
     edges = []
     for e in range(19):

time: 43.6 us -> 43.6 us (level)
  no operation moved by 1% of the time
where the time goes in v8:
time: 43.6 us; the launch traced here: 43.4 us
  Pallas kernels  16.9 us (39%)
  starting transfers between devices  14.8 us (34%)
  waiting for transfers between devices  8.81 us (20%)
  local copies, waits for them, and re-layouts  2.04 us (5%)
  between operations  0.76 us (2%)
    pallas_call x11, Pallas kernels, call(): pl.pallas_call(body, out_shape=[jax.ShapeDtypeStruct(*out) for out in out...  16.9 us
    ppermute x12, starting transfers between devices, ring(): lax.ppermute(value, axis, [(i, (i + step) % count) for i in range(count)])  14.8 us
    ppermute x12, waiting for transfers between devices, ring(): lax.ppermute(value, axis, [(i, (i + step) % count) for i in range(count)])  8.81 us
    unnamed x10, local copies, waits for them, and re-layouts  2.04 us
  transfers between devices with their start and end apart: 12, of which 8 were waited for; matrix products, arithmetic and copies ran while one was open for 0% of the time, Pallas kernels for 13%

profile of v8, /device:TPU:0, one launch (start us, length us, event | category | flops | bytes accessed | tf_op | source)
XLA Modules:
  0.0 43.4 jit_solution(14383656610634889980)
XLA Ops:
  0.7 1.3 %copy-done = f32[19,16,4,256]{3,2,1,0:T(4,128)S(1)} copy-done((f32[19,16,4,256]{3,2,1,0:T(4,128)S(1)}, f32[19,16,4,256]{3,2,1,0:T(4,128)}, u32[]{:S(2)}) %copy-start) | copy-done | bytes 1245208
  1.9 0.7 %copy-done.2 = f32[2,3,1024]{2,0,1:T(2,128)S(1)} copy-done((f32[2,3,1024]{2,0,1:T(2,128)S(1)}, f32[2,3,1024]{2,0,1:T(2,128)}, u32[]{:S(2)}) %copy-start.2) | copy-done | bytes 24600
  2.7 0.2 shard_map.60
  2.9 2.4 %collective-permute-start.2 = (f32[72,128]{1,0:T(8,128)S(1)}, f32[72,128]{1,0:T(8,128)S(1)}, u32[]{:S(2)}, u32[]{:S(2)}) collective-permute-start(f32[72,128]{1,0:T(8,128)S(1)} %get-tuple-element.41.refs_0_), channel_id=1, source_target_pairs={{0,3},{1,0},{2,1},{3,2},{4,7},{5,4},{6,5},{7,6},{8,11},{9,8},{10,9... | collective-permute-start | bytes 110600 | tf_op jit(solution)/shard_map/ppermute | solution.py:686
  5.3 0.6 %collective-permute-start.1 = (f32[72,128]{1,0:T(8,128)S(1)}, f32[72,128]{1,0:T(8,128)S(1)}, u32[]{:S(2)}, u32[]{:S(2)}) collective-permute-start(f32[72,128]{1,0:T(8,128)S(1)} %get-tuple-element.41.refs_0_), channel_id=1, source_target_pairs={{0,2},{1,3},{2,0},{3,1},{4,6},{5,7},{6,4},{7,5},{8,10},{9,11},{10,... | collective-permute-start | bytes 110600 | tf_op jit(solution)/shard_map/ppermute | solution.py:686
  6.0 0.2 collective-permute-start
  6.1 0.1 pad_add_fusion.where_ref
  6.2 1.5 %shard_map.59 = (f32[19,8,128]{2,1,0:T(8,128)S(1)}, f32[80,128]{1,0:T(8,128)S(1)}, f32[80,128]{1,0:T(8,128)S(1)}, s32[40]{0:T(128)S(1)}) custom-call(s32[2,1,32]{2,1,0:T(1,128)S(1)} %bitcast.29, s32[2]{0:T(128)S(1)} %pad_add_fusion.where_ref, f32[19,128,128]{2,1,0:T(8,128)S(1)} %bitcast.26), custom_call_target="tpu_custom_call" | custom-call | bytes 319808 | tf_op jit(solution)/shard_map/pallas_call | solution.py:675
  7.7 1.9 %collective-permute-done.1.refs_2_ = f32[72,128]{1,0:T(8,128)S(1)} collective-permute-done((f32[72,128]{1,0:T(8,128)S(1)}, f32[72,128]{1,0:T(8,128)S(1)}, u32[]{:S(2)}, u32[]{:S(2)}) %collective-permute-start.1) | collective-permute-done | bytes 36896 | tf_op jit(solution)/shard_map/ppermute | solution.py:686
  9.6 0.1 collective-permute-done.refs_1_
  9.7 4.9 %shard_map.61 = (f32[3,128,128]{2,1,0:T(8,128)S(1)}, f32[104,128]{1,0:T(8,128)S(1)}, f32[104,128]{1,0:T(8,128)S(1)}, f32[32,16,128]{2,1,0:T(8,128)S(1)}) custom-call(s32[2,1,32]{2,1,0:T(1,128)S(1)} %bitcast.30, s32[2]{0:T(128)S(1)} %pad_add_fusion.where_ref, s32[40]{0:T(128)S(1)} %get-tuple-element.37.chosen_ref, s32[2]{0:T(128)S(1)} %copy-done.4, ...), custom_call_target="tpu_custom_call" | custom-call | bytes 1130496 | tf_op jit(solution)/shard_map/pallas_call | solution.py:675
  14.6 0.1 collective-permute-start.4
  14.7 0.5 %collective-permute-start.3 = (f32[104,128]{1,0:T(8,128)S(1)}, f32[104,128]{1,0:T(8,128)S(1)}, u32[]{:S(2)}, u32[]{:S(2)}) collective-permute-start(f32[104,128]{1,0:T(8,128)S(1)} %get-tuple-element.45.own_ref), channel_id=1, source_target_pairs={{0,1},{1,2},{2,3},{3,0},{4,5},{5,6},{6,7},{7,4},{8,9},{9,10},{10,1... | collective-permute-start | bytes 159752 | tf_op jit(solution)/shard_map/ppermute | solution.py:686
  15.2 0.5 %shard_map.62 = (f32[19,128,128]{2,1,0:T(8,128)S(1)}, f32[160,128]{1,0:T(8,128)S(1)}, f32[160,128]{1,0:T(8,128)S(1)}) custom-call(f32[19,128,128]{2,1,0:T(8,128)S(1)} %bitcast.27, f32[3,128,128]{2,1,0:T(8,128)S(1)} %get-tuple-element.42.refs_1_), custom_call_target="tpu_custom_call" | custom-call | bytes 2818048 | tf_op jit(solution)/shard_map/pallas_call | solution.py:675
  15.7 0.8 %collective-permute-done.4.right_ref = f32[104,128]{1,0:T(8,128)S(1)} collective-permute-done((f32[104,128]{1,0:T(8,128)S(1)}, f32[104,128]{1,0:T(8,128)S(1)}, u32[]{:S(2)}, u32[]{:S(2)}) %collective-permute-start.4) | collective-permute-done | bytes 53280 | tf_op jit(solution)/shard_map/ppermute | solution.py:686
  16.5 1.9 %collective-permute-done.3.left_ref = f32[104,128]{1,0:T(8,128)S(1)} collective-permute-done((f32[104,128]{1,0:T(8,128)S(1)}, f32[104,128]{1,0:T(8,128)S(1)}, u32[]{:S(2)}, u32[]{:S(2)}) %collective-permute-start.3) | collective-permute-done | bytes 53280 | tf_op jit(solution)/shard_map/ppermute | solution.py:686
  18.4 0.1 shard_map.63
  18.5 1.6 %collective-permute-start.5 = (f32[176,128]{1,0:T(8,128)S(1)}, f32[176,128]{1,0:T(8,128)S(1)}, u32[]{:S(2)}, u32[]{:S(2)}) collective-permute-start(f32[176,128]{1,0:T(8,128)S(1)} %get-tuple-element.52), channel_id=1, source_target_pairs={{0,4},{4,8},{8,12},{12,16},{16,20},{20,24},{24,28},{28,0},{1,5},{5... | collective-permute-start | bytes 270344 | tf_op jit(solution)/shard_map/ppermute | solution.py:686
  20.1 3.2 %collective-permute-start.6 = (f32[176,128]{1,0:T(8,128)S(1)}, f32[176,128]{1,0:T(8,128)S(1)}, u32[]{:S(2)}, u32[]{:S(2)}) collective-permute-start(f32[176,128]{1,0:T(8,128)S(1)} %get-tuple-element.53), channel_id=1, source_target_pairs={{0,28},{4,0},{8,4},{12,8},{16,12},{20,16},{24,20},{28,24},{1,29},{... | collective-permute-start | bytes 270344 | tf_op jit(solution)/shard_map/ppermute | solution.py:686
  23.3 1.3 %shard_map.64 = (f32[19,128,128]{2,1,0:T(8,128)S(1)}, f32[19,8,128]{2,1,0:T(8,128)S(1)}) custom-call(f32[19,128,128]{2,1,0:T(8,128)S(1)} %get-tuple-element.43.post_ref, f32[19,8,128]{2,1,0:T(8,128)S(1)} %get-tuple-element.49.post_edge_ref), custom_call_target="tpu_custom_call" | custom-call | bytes 2646016 | tf_op jit(solution)/shard_map/pallas_call | solution.py:675
  24.6 1.2 %collective-permute-done.5.east_ref = f32[176,128]{1,0:T(8,128)S(1)} collective-permute-done((f32[176,128]{1,0:T(8,128)S(1)}, f32[176,128]{1,0:T(8,128)S(1)}, u32[]{:S(2)}, u32[]{:S(2)}) %collective-permute-start.5) | collective-permute-done | bytes 90144 | tf_op jit(solution)/shard_map/ppermute | solution.py:686
  25.8 0.7 %collective-permute-done.6.west_ref = f32[176,128]{1,0:T(8,128)S(1)} collective-permute-done((f32[176,128]{1,0:T(8,128)S(1)}, f32[176,128]{1,0:T(8,128)S(1)}, u32[]{:S(2)}, u32[]{:S(2)}) %collective-permute-start.6) | collective-permute-done | bytes 90144 | tf_op jit(solution)/shard_map/ppermute | solution.py:686
  26.5 5.0 %shard_map.65 = (f32[10,128,128]{2,1,0:T(8,128)S(1)}, f32[19,8,128]{2,1,0:T(8,128)S(1)}, f32[3,128,128]{2,1,0:T(8,128)S(1)}, f32[72,128]{1,0:T(8,128)S(1)}, f32[...) custom-call(s32[2]{0:T(128)S(1)} %pad_add_fusion.where_ref, s32[40]{0:T(128)S(1)} %get-tuple-element.37.chosen_ref, ...), custom_call_target="tpu_custom_call" | custom-call | bytes 2105344 | tf_op jit(solution)/shard_map/pallas_call | solution.py:675
  31.6 0.5 %collective-permute-start.7 = (f32[72,128]{1,0:T(8,128)S(1)}, f32[72,128]{1,0:T(8,128)S(1)}, u32[]{:S(2)}, u32[]{:S(2)}) collective-permute-start(f32[72,128]{1,0:T(8,128)S(1)} %get-tuple-element.59.own_ref), channel_id=1, source_target_pairs={{0,1},{1,2},{2,3},{3,0},{4,5},{5,6},{6,7},{7,4},{8,9},{9,10},{10,1... | collective-permute-start | bytes 110600 | tf_op jit(solution)/shard_map/ppermute | solution.py:686
  32.1 1.0 %collective-permute-start.11 = (f32[48,128]{1,0:T(8,128)S(1)}, f32[48,128]{1,0:T(8,128)S(1)}, u32[]{:S(2)}, u32[]{:S(2)}) collective-permute-start(f32[48,128]{1,0:T(8,128)S(1)} %get-tuple-element.68), channel_id=1, source_target_pairs={{0,2},{1,3},{2,0},{3,1},{4,6},{5,7},{6,4},{7,5},{8,10},{9,11},{10,... | collective-permute-start | bytes 73736 | tf_op jit(solution)/shard_map/ppermute | solution.py:686
  33.0 0.5 %shard_map.66 = (f32[19,128,128]{2,1,0:T(8,128)S(1)}, f32[160,128]{1,0:T(8,128)S(1)}, f32[160,128]{1,0:T(8,128)S(1)}) custom-call(f32[19,128,128]{2,1,0:T(8,128)S(1)} %get-tuple-element.50.streamed_ref.refs_0_, f32[10,128,128]{2,1,0:T(8,128)S(1)} %get-tuple-element.55.refs_1_, f32[3,128,128]{2,1,0:T(8,128)S(1)} %get-tuple-element.56.refs_2_), custom_call_target="tpu_custom_call" | custom-call | bytes 2818048 | tf_op jit(solution)/shard_map/pallas_call | solution.py:675
  33.6 1.4 %collective-permute-done.7.left_ref = f32[72,128]{1,0:T(8,128)S(1)} collective-permute-done((f32[72,128]{1,0:T(8,128)S(1)}, f32[72,128]{1,0:T(8,128)S(1)}, u32[]{:S(2)}, u32[]{:S(2)}) %collective-permute-start.7) | collective-permute-done | bytes 36896 | tf_op jit(solution)/shard_map/ppermute | solution.py:686
  35.1 0.5 %collective-permute-start.9 = (f32[176,128]{1,0:T(8,128)S(1)}, f32[176,128]{1,0:T(8,128)S(1)}, u32[]{:S(2)}, u32[]{:S(2)}) collective-permute-start(f32[176,128]{1,0:T(8,128)S(1)} %get-tuple-element.65), channel_id=1, source_target_pairs={{0,4},{4,8},{8,12},{12,16},{16,20},{20,24},{24,28},{28,0},{1,5},{5... | collective-permute-start | bytes 270344 | tf_op jit(solution)/shard_map/ppermute | solution.py:686
  35.6 4.2 %collective-permute-start.10 = (f32[176,128]{1,0:T(8,128)S(1)}, f32[176,128]{1,0:T(8,128)S(1)}, u32[]{:S(2)}, u32[]{:S(2)}) collective-permute-start(f32[176,128]{1,0:T(8,128)S(1)} %get-tuple-element.66), channel_id=1, source_target_pairs={{0,28},{4,0},{8,4},{12,8},{16,12},{20,16},{24,20},{28,24},{1,29},{... | collective-permute-start | bytes 270344 | tf_op jit(solution)/shard_map/ppermute | solution.py:686
  39.9 1.8 %shard_map.68 = (f32[19,128,128]{2,1,0:T(8,128)}, f32[10,128,128]{2,1,0:T(8,128)S(1)}) custom-call(f32[19,128,128]{2,1,0:T(8,128)S(1)} %get-tuple-element.57.post_ref, f32[19,8,128]{2,1,0:T(8,128)S(1)} %get-tuple-element.63.post_edge_ref), custom_call_target="tpu_custom_call" | custom-call | bytes 3801088 | tf_op jit(solution)/shard_map/pallas_call | solution.py:675
  41.6 0.7 %collective-permute-done.9.east_ref = f32[176,128]{1,0:T(8,128)S(1)} collective-permute-done((f32[176,128]{1,0:T(8,128)S(1)}, f32[176,128]{1,0:T(8,128)S(1)}, u32[]{:S(2)}, u32[]{:S(2)}) %collective-permute-start.9) | collective-permute-done | bytes 90144 | tf_op jit(solution)/shard_map/ppermute | solution.py:686
  42.4 1.1 %shard_map.69 = (f32[19,128,128]{2,1,0:T(8,128)}, f32[48,128]{1,0:T(8,128)}) custom-call(f32[19,128,128]{2,1,0:T(8,128)S(1)} %get-tuple-element.57.post_ref, f32[19,8,128]{2,1,0:T(8,128)S(1)} %get-tuple-element.63.post_edge_ref, f32[10,128,128]{2,1,0:T(8,128)S(1)} %get-tuple-element.64.before_ref, ...), custom_call_target="tpu_custom_call", output_to_operand_aliasing={{0}: (6, {})} | custom-call | bytes 2539520 | tf_op jit(solution)/shard_map/pallas_call | solution.py:675
  (15 shorter events, 0.1 us)
Async XLA Ops:
  0.6 5.6 %copy-start.3 = (s32[2,32,1]{1,2,0:T(1,128)S(1)}, s32[2,32,1]{1,2,0:T(1,128)}, u32[]{:S(2)}) copy-start(s32[2,32,1]{1,2,0:T(1,128)} %param.6) | copy-start | bytes 772
  0.6 1.3 %copy-start = (f32[19,16,4,256]{3,2,1,0:T(4,128)S(1)}, f32[19,16,4,256]{3,2,1,0:T(4,128)}, u32[]{:S(2)}) copy-start(f32[19,16,4,256]{3,2,1,0:T(4,128)} %param.4) | copy-start | bytes 3735556
  1.9 0.7 %copy-start.2 = (f32[2,3,1024]{2,0,1:T(2,128)S(1)}, f32[2,3,1024]{2,0,1:T(2,128)}, u32[]{:S(2)}) copy-start(f32[2,3,1024]{2,0,1:T(2,128)} %param.5) | copy-start | bytes 73732
  2.7 3.5 %copy-start.1 = (f32[19,16,4,256]{3,2,1,0:T(4,128)S(1)}, f32[19,16,4,256]{3,2,1,0:T(4,128)}, u32[]{:S(2)}) copy-start(f32[19,16,4,256]{3,2,1,0:T(4,128)} %param.4) | copy-start | bytes 3735556
  2.7 7.0 %copy-start.4 = (s32[2]{0:T(128)S(1)}, s32[2]{0:T(128)}, u32[]{:S(2)}) copy-start(s32[2]{0:T(128)} %stiff_ref.1) | copy-start | bytes 28
  2.9 4.8 %collective-permute-start.2 = (f32[72,128]{1,0:T(8,128)S(1)}, f32[72,128]{1,0:T(8,128)S(1)}, u32[]{:S(2)}, u32[]{:S(2)}) collective-permute-start(f32[72,128]{1,0:T(8,128)S(1)} %get-tuple-element.41.refs_0_), channel_id=1, source_target_pairs={{0,3},{1,0},{2,1},{3,2},{4,7},{5,4},{6,5},{7,6},{8,11},{9,8},{10,9... | collective-permute-start | bytes 110600 | tf_op jit(solution)/shard_map/ppermute | solution.py:686
  5.3 4.3 %collective-permute-start.1 = (f32[72,128]{1,0:T(8,128)S(1)}, f32[72,128]{1,0:T(8,128)S(1)}, u32[]{:S(2)}, u32[]{:S(2)}) collective-permute-start(f32[72,128]{1,0:T(8,128)S(1)} %get-tuple-element.41.refs_0_), channel_id=1, source_target_pairs={{0,2},{1,3},{2,0},{3,1},{4,6},{5,7},{6,4},{7,5},{8,10},{9,11},{10,... | collective-permute-start | bytes 110600 | tf_op jit(solution)/shard_map/ppermute | solution.py:686
  6.0 3.7 %collective-permute-start = (f32[72,128]{1,0:T(8,128)S(1)}, f32[72,128]{1,0:T(8,128)S(1)}, u32[]{:S(2)}, u32[]{:S(2)}) collective-permute-start(f32[72,128]{1,0:T(8,128)S(1)} %get-tuple-element.41.refs_0_), channel_id=1, source_target_pairs={{0,1},{1,2},{2,3},{3,0},{4,5},{5,6},{6,7},{7,4},{8,9},{9,10},{10,1... | collective-permute-start | bytes 110600 | tf_op jit(solution)/shard_map/ppermute | solution.py:686
  14.6 1.8 %collective-permute-start.4 = (f32[104,128]{1,0:T(8,128)S(1)}, f32[104,128]{1,0:T(8,128)S(1)}, u32[]{:S(2)}, u32[]{:S(2)}) collective-permute-start(f32[104,128]{1,0:T(8,128)S(1)} %get-tuple-element.46), channel_id=1, source_target_pairs={{0,3},{1,0},{2,1},{3,2},{4,7},{5,4},{6,5},{7,6},{8,11},{9,8},{10,9... | collective-permute-start | bytes 159752 | tf_op jit(solution)/shard_map/ppermute | solution.py:686
  14.7 3.7 %collective-permute-start.3 = (f32[104,128]{1,0:T(8,128)S(1)}, f32[104,128]{1,0:T(8,128)S(1)}, u32[]{:S(2)}, u32[]{:S(2)}) collective-permute-start(f32[104,128]{1,0:T(8,128)S(1)} %get-tuple-element.45.own_ref), channel_id=1, source_target_pairs={{0,1},{1,2},{2,3},{3,0},{4,5},{5,6},{6,7},{7,4},{8,9},{9,10},{10,1... | collective-permute-start | bytes 159752 | tf_op jit(solution)/shard_map/ppermute | solution.py:686
  18.5 7.3 %collective-permute-start.5 = (f32[176,128]{1,0:T(8,128)S(1)}, f32[176,128]{1,0:T(8,128)S(1)}, u32[]{:S(2)}, u32[]{:S(2)}) collective-permute-start(f32[176,128]{1,0:T(8,128)S(1)} %get-tuple-element.52), channel_id=1, source_target_pairs={{0,4},{4,8},{8,12},{12,16},{16,20},{20,24},{24,28},{28,0},{1,5},{5... | collective-permute-start | bytes 270344 | tf_op jit(solution)/shard_map/ppermute | solution.py:686
  20.1 6.5 %collective-permute-start.6 = (f32[176,128]{1,0:T(8,128)S(1)}, f32[176,128]{1,0:T(8,128)S(1)}, u32[]{:S(2)}, u32[]{:S(2)}) collective-permute-start(f32[176,128]{1,0:T(8,128)S(1)} %get-tuple-element.53), channel_id=1, source_target_pairs={{0,28},{4,0},{8,4},{12,8},{16,12},{20,16},{24,20},{28,24},{1,29},{... | collective-permute-start | bytes 270344 | tf_op jit(solution)/shard_map/ppermute | solution.py:686
  31.5 2.0 %collective-permute-start.8 = (f32[72,128]{1,0:T(8,128)S(1)}, f32[72,128]{1,0:T(8,128)S(1)}, u32[]{:S(2)}, u32[]{:S(2)}) collective-permute-start(f32[72,128]{1,0:T(8,128)S(1)} %get-tuple-element.60), channel_id=1, source_target_pairs={{0,3},{1,0},{2,1},{3,2},{4,7},{5,4},{6,5},{7,6},{8,11},{9,8},{10,9... | collective-permute-start | bytes 110600 | tf_op jit(solution)/shard_map/ppermute | solution.py:686
  31.6 3.4 %collective-permute-start.7 = (f32[72,128]{1,0:T(8,128)S(1)}, f32[72,128]{1,0:T(8,128)S(1)}, u32[]{:S(2)}, u32[]{:S(2)}) collective-permute-start(f32[72,128]{1,0:T(8,128)S(1)} %get-tuple-element.59.own_ref), channel_id=1, source_target_pairs={{0,1},{1,2},{2,3},{3,0},{4,5},{5,6},{6,7},{7,4},{8,9},{9,10},{10,1... | collective-permute-start | bytes 110600 | tf_op jit(solution)/shard_map/ppermute | solution.py:686
  32.1 7.8 %collective-permute-start.11 = (f32[48,128]{1,0:T(8,128)S(1)}, f32[48,128]{1,0:T(8,128)S(1)}, u32[]{:S(2)}, u32[]{:S(2)}) collective-permute-start(f32[48,128]{1,0:T(8,128)S(1)} %get-tuple-element.68), channel_id=1, source_target_pairs={{0,2},{1,3},{2,0},{3,1},{4,6},{5,7},{6,4},{7,5},{8,10},{9,11},{10,... | collective-permute-start | bytes 73736 | tf_op jit(solution)/shard_map/ppermute | solution.py:686
  35.1 7.3 %collective-permute-start.9 = (f32[176,128]{1,0:T(8,128)S(1)}, f32[176,128]{1,0:T(8,128)S(1)}, u32[]{:S(2)}, u32[]{:S(2)}) collective-permute-start(f32[176,128]{1,0:T(8,128)S(1)} %get-tuple-element.65), channel_id=1, source_target_pairs={{0,4},{4,8},{8,12},{12,16},{16,20},{20,24},{24,28},{28,0},{1,5},{5... | collective-permute-start | bytes 270344 | tf_op jit(solution)/shard_map/ppermute | solution.py:686
  35.6 6.7 %collective-permute-start.10 = (f32[176,128]{1,0:T(8,128)S(1)}, f32[176,128]{1,0:T(8,128)S(1)}, u32[]{:S(2)}, u32[]{:S(2)}) collective-permute-start(f32[176,128]{1,0:T(8,128)S(1)} %get-tuple-element.66), channel_id=1, source_target_pairs={{0,28},{4,0},{8,4},{12,8},{16,12},{20,16},{24,20},{28,24},{1,29},{... | collective-permute-start | bytes 270344 | tf_op jit(solution)/shard_map/ppermute | solution.py:686
